TPU v7x, 256 devices: a whole 4x4x8 slice. The times are simulated.
256 devices in a mesh: dp: 16 (over y, x_hi, core), mem: 16 (over x_lo, z).
Axes of the slice: x: 4 (x_hi: 2, x_lo: 2; x = x_hi * 2 + x_lo), y: 4, z: 8, core: 2. Of those that a mesh axis runs over, the one named last changes fastest.
Arguments:
- queries: bfloat16 [4096, 4096], P(('dp', 'mem')), may hold values from -8 to 8
- memory: bfloat16 [32768, 4096], P('mem'), may hold values from -7 to 7
- log_scale: float32 [1], replicated, may hold values from 1.0986 to 1.6094
- labels: int32 [4096], P('dp'), may hold values from 0 to 32767, as said below
- valid: int32 [32768], P('mem'), may hold values from 0 to 1
- cotangent: float32 [4096], P('dp'), may hold values from -20 to 20
Outputs:
- grad_queries: bfloat16 [4096, 4096], P(('dp', 'mem'))
- scale_grad: float32 [1], replicated
Inputs may be any that keep to these rules, and one draw needn't show every extreme that they name: `labels`: every label names a memory row whose valid entry is 1.
All inputs are finite; a program needn't handle non-finite values.
Results may differ from a plain program's by a relative error of at most 0.022.
Values may be sent and summed in bfloat16 or wider, within the bound.
No kernel may reach another device: no remote copies, remote signals or barrier semaphores. Data moves between devices by JAX's collectives and lax.ppermute only.
A program may use at most 64 MiB of HBM per device.

v0:
```python
import jax
import jax.numpy as jnp
from jax import lax
from jax.sharding import PartitionSpec as P


def shards(queries, memory, log_scale, labels, valid, cotangent):
    scale = jnp.exp(log_scale[0])
    mem_rows = memory.shape[0]
    q_rows = queries.shape[0]
    live = valid > 0
    start_row = lax.axis_index("mem") * mem_rows
    raw = lax.dot_general(
        lax.all_gather(queries, "mem", axis=0, tiled=True),
        memory,
        (((1,), (1,)), ((), ())),
        preferred_element_type=jnp.float32,
    )
    logits = jnp.where(live[None, :], scale * raw, jnp.float32(-1e30))
    local_top = jnp.max(logits, axis=1)
    top = lax.pmax(local_top, "mem")
    expo = jnp.exp(logits - top[:, None])
    total = lax.psum(jnp.sum(expo, axis=1), "mem")
    columns = jnp.arange(mem_rows, dtype=jnp.int32)
    hit = ((labels - start_row)[:, None] == columns[None, :]).astype(jnp.float32)
    weight = expo / total[:, None] - hit
    scale_part = jnp.sum(cotangent * jnp.sum(weight * raw, axis=1))
    weight_half = weight.astype(jnp.bfloat16)
    summed = lax.psum_scatter(
        jnp.dot(weight_half, memory, preferred_element_type=jnp.float32).astype(jnp.bfloat16),
        "mem",
        scatter_dimension=0,
        tiled=True,
    ).astype(jnp.float32)
    own_grad = lax.dynamic_slice_in_dim(cotangent, lax.axis_index("mem") * q_rows, q_rows)
    grad_queries = (scale * own_grad[:, None] * summed).astype(jnp.bfloat16)
    count = cotangent.shape[0] * lax.axis_size("dp")
    scale_grad = (scale * lax.psum(scale_part, ("dp", "mem")) / count).reshape(1)
    return (grad_queries, scale_grad)


def solution(mesh):
    placed = (P(("dp", "mem"), None), P("mem", None), P(), P("dp"), P("mem"), P("dp"))
    return jax.shard_map(
        shards, mesh=mesh, in_specs=placed, out_specs=(P(("dp", "mem"), None), P()), check_vma=False
    )
```

profile of v0, /device:TPU:32, one launch (start us, length us, event | category | flops | bytes accessed | tf_op | source)
XLA Modules:
  0.0 255.9 jit_solution(11012103242494897976)
XLA Ops:
  7.2 0.0 all-gather.2.cloned.1.call-start
  7.2 0.7 all-gather.2.cloned.1.call-update
  7.9 0.0 reduce-scatter.2.cloned.1.call-start
  8.6 0.7 broadcast_subtract_fusion
  9.3 0.7 broadcast_compare_fusion
  10.0 72.9 %all-gather.2.cloned.1.call-done = bf16[256,4096]{1,0:T(8,128)(2,1)} async-done(((bf16[16,4096]{1,0:T(8,128)(2,1)}), bf16[256,4096]{1,0:T(8,128)(2,1)}) %all-gather.2.cloned.1.call-update) | async-done | bytes 2097168 | tf_op jit(solution)/shard_map/all_gather | solution.py:14
  82.9 8.9 %fusion = (f32[256]{0:T(256)S(1)}, f32[256,2048]{1,0:T(8,128)S(1)}) fusion(f32[]{:T(128)} %bitcast, pred[2048]{0:T(1024)(128)(4,1)S(1)} %broadcast_compare_fusion, bf16[256,4096]{1,0:T(8,128)(2,1)} %all-gather.2.cloned.1.call-done, bf16[2048,4096]{1,0:T(8,128)(2,1)} %param.7), kind=kOutput, calls=%fused_computation.6 | convolution fusion | flops 4296540160 | bytes 20974596 | tf_op jit(solution)/shard_map/dot_general | solution.py:13
  91.8 32.2 %pmax.7 = f32[256]{0:T(256)S(1)} all-reduce(f32[256]{0:T(256)S(1)} %get-tuple-element.2), channel_id=1, replica_groups=mesh['dp'=16,'mem'=16] {'mem'}, use_global_device_ids=true, to_apply=%region_1.2 | all-reduce | flops 256 | bytes 2048 | tf_op jit(solution)/shard_map/pmax | solution.py:21
  124.0 0.5 fusion.1
  124.5 33.2 %psum.14 = f32[256]{0:T(256)S(1)} all-reduce(f32[256]{0:T(256)S(1)} %fusion.1), channel_id=1, replica_groups=mesh['dp'=16,'mem'=16] {'mem'}, use_global_device_ids=true, to_apply=%region_3.4 | all-reduce | flops 256 | bytes 2048 | tf_op jit(solution)/shard_map/psum | solution.py:23
  157.7 12.3 %convolution_convert_fusion = bf16[256,4096]{1,0:T(8,128)(2,1)} fusion(bf16[2048,4096]{1,0:T(8,128)(2,1)} %param.7, f32[256,2048]{1,0:T(8,128)S(1)} %get-tuple-element.3, s32[256]{0:T(256)S(1)} %broadcast_subtract_fusion, f32[256]{0:T(256)S(1)} %psum.14, f32[256]{0:T(256)S(1)} %pmax.7, f32[]{:T(128)} %bitcast, pred[2048]{0:T(1024)(128)(4,1)S(1)} %broadcast_compare_fusion), kind=kOutput, calls=%fused_computation | convolution fusion | flops 4300210176 | bytes 20976644 | tf_op jit(solution)/shard_map/dot_general | solution.py:30
  170.0 0.0 copy-start
  170.0 0.0 reduce-scatter.2.cloned.1.call-update
  170.0 1.0 multiply_reduce_fusion
  171.0 0.0 copy-done
  171.0 0.6 multiply_reduce_fusion.1
  171.6 0.1 dynamic-slice_multiply_fusion
  171.7 74.0 %psum.15 = f32[]{:T(128)} all-reduce(f32[]{:T(128)} %multiply_reduce_fusion.1), channel_id=1, replica_groups=mesh['dp'=16,'mem'=16] {'dp','mem'}, use_global_device_ids=true, to_apply=%region_7.8 | all-reduce | flops 1 | bytes 8 | tf_op jit(solution)/shard_map/psum | solution.py:38
  246.3 0.0 reduce-scatter.2.cloned.1.call-done
  246.3 1.6 multiply_convert_fusion
Async XLA Ops:
  7.2 75.7 %all-gather.2.cloned.1.call-start = ((), (), s32[]{:S(2)}) async-start(), calls=%async_computation.1 | async-start | bytes 2228224 | tf_op jit(solution)/shard_map/all_gather | solution.py:14
  7.9 238.4 %reduce-scatter.2.cloned.1.call-start = ((), (), s32[]{:S(2)}) async-start(), calls=%async_computation.2 | async-start | bytes 2228224 | tf_op jit(solution)/shard_map/reduce_scatter | solution.py:29
  170.0 1.0 copy-start
Sparse Core Ops, SparseCore 0:
  9.8 73.0 all-gather.1
  170.1 68.9 reduce-scatter.1
where the time goes:
time: 258 us; the launch traced here: 256 us
  blocking collectives  139 us (54%)
  waiting for transfers between devices  73.6 us (29%)
  matrix products  21.2 us (8%)
  between operations  16.5 us (6%)
  other arithmetic  5.24 us (2%)
    psum x1, blocking collectives, shards(): lax.psum(scale_part, ('dp', 'mem'))  74 us
    all_gather x1, waiting for transfers between devices, shards(): lax.all_gather(queries, 'mem', axis=0, tiled=True)  72.9 us
    psum x1, blocking collectives, shards(): total = lax.psum(jnp.sum(expo, axis=1), 'mem')  33.2 us
    pmax x1, blocking collectives, shards(): top = lax.pmax(local_top, 'mem')  32.2 us
    dot_general x1, matrix products, shards(): jnp.dot(weight_half, memory, preferred_element_type=jnp.float32)  12.3 us
    dot_general x1, matrix products, shards(): lax.dot_general(lax.all_gather(queries, 'mem', axis=0, tiled=True), memor...  8.88 us
  transfers between devices with their start and end apart: 2, of which 1 were waited for; matrix products, arithmetic and copies ran while one was open for 1% of the time, Pallas kernels for 0%

commit v1 on v0

v1 whole, which is shorter than its diff:
```python
import jax
import jax.numpy as jnp
from jax import lax
from jax.experimental import pallas as pl
from jax.experimental.pallas import tpu as pltpu
from jax.sharding import PartitionSpec as P

AXES = ("dp", "mem")
NEG = -1e30
VMEM = 48 * 1024 * 1024
BLK = 256
COLS = 512


def table(move):
    pairs = []
    for y in range(4):
        for x in range(4):
            for c in range(2):
                for z in range(8):
                    index = lambda y, x, c, z: (((y * 2 + x // 2) * 2 + c) * 2 + x % 2) * 8 + z
                    pairs.append((index(y, x, c, z), index(*move(y, x, c, z))))
    return pairs


def along_z(k):
    return table(lambda y, x, c, z: (y, x, c, (z + k) % 8))


def partner_of(x, c):
    if c == 0:
        return x ^ 1
    return (x + 1) % 4 if x % 2 else (x - 1) % 4


PARTNER = table(lambda y, x, c, z: (y, partner_of(x, c), c, z))
CORE = table(lambda y, x, c, z: (y, x, 1 - c, z))
X1 = table(lambda y, x, c, z: (y, x ^ 1, c, z))
X2 = table(lambda y, x, c, z: (y, x ^ 2, c, z))
Y1 = table(lambda y, x, c, z: (y ^ 1, x, c, z))
Y2 = table(lambda y, x, c, z: (y ^ 2, x, c, z))


def send(x, pairs):
    return lax.ppermute(x, AXES, pairs)


def logits_kernel(scale_ref, shift_ref, q_ref, mem_ref, lab_ref, valid_ref, e_ref, stat_ref, l_scr, m_scr, ll_scr):
    i = pl.program_id(0)

    @pl.when(i == 0)
    def _():
        m_scr[...] = jnp.full_like(m_scr, NEG)
        ll_scr[...] = jnp.zeros_like(ll_scr)

    raw = lax.dot_general(
        q_ref[...], mem_ref[...], (((1,), (1,)), ((), ())), preferred_element_type=jnp.float32
    )
    logit = raw * scale_ref[0]
    column = lax.broadcasted_iota(jnp.int32, logit.shape, 1) + i * BLK
    hit = lab_ref[...] == column
    kept = jnp.where(jnp.logical_and(valid_ref[...] > 0, jnp.logical_not(hit)), logit, NEG)
    l_scr[:, pl.ds(pl.multiple_of(i * BLK, BLK), BLK)] = kept
    m_scr[...] = jnp.maximum(m_scr[...], jnp.max(kept, axis=1, keepdims=True))
    ll_scr[...] += jnp.sum(jnp.where(hit, logit, 0.0), axis=1, keepdims=True)

    @pl.when(i == pl.num_programs(0) - 1)
    def _():
        rows = l_scr.shape[0]
        half = rows // 2
        step = 32
        lane = lax.broadcasted_iota(jnp.int32, (step, 128), 1)
        tiles = []
        for r in range(0, rows, step):
            top = m_scr[r:r + step, :]
            val = l_scr[r:r + step, :]
            e = jnp.exp(val - top)
            e_ref[r:r + step, :] = e.astype(jnp.bfloat16)
            s = jnp.sum(e, axis=1, keepdims=True)
            t = jnp.sum(e * val, axis=1, keepdims=True)
            tiles.append(
                jnp.where(lane == 0, top, jnp.where(lane == 1, s, jnp.where(lane == 2, t, ll_scr[r:r + step, :])))
            )
        full = jnp.concatenate(tiles, axis=0)
        own = pltpu.roll(full[:half].T, shift_ref[0], 1)
        other = pltpu.roll(full[half:].T, shift_ref[0], 1)
        stat_ref[0:4, :] = own[0:4, :]
        stat_ref[4:8, :] = other[0:4, :]


def logits_call(scale, shift, q, memory, lab, valid):
    rows, depth = q.shape
    n = memory.shape[0]
    return pl.pallas_call(
        logits_kernel,
        grid=(n // BLK,),
        in_specs=[
            pl.BlockSpec(memory_space=pltpu.SMEM),
            pl.BlockSpec(memory_space=pltpu.SMEM),
            pl.BlockSpec((rows, depth), lambda i: (0, 0)),
            pl.BlockSpec((BLK, depth), lambda i: (i, 0)),
            pl.BlockSpec((rows, 1), lambda i: (0, 0)),
            pl.BlockSpec((1, BLK), lambda i: (0, i)),
        ],
        out_specs=[pl.BlockSpec((rows, n), lambda i: (0, 0)), pl.BlockSpec((8, 128), lambda i: (0, 0))],
        out_shape=[
            jax.ShapeDtypeStruct((rows, n), jnp.bfloat16),
            jax.ShapeDtypeStruct((8, 128), jnp.float32),
        ],
        scratch_shapes=[
            pltpu.VMEM((rows, n), jnp.float32),
            pltpu.VMEM((rows, 1), jnp.float32),
            pltpu.VMEM((rows, 1), jnp.float32),
        ],
        compiler_params=pltpu.CompilerParams(vmem_limit_bytes=VMEM),
        cost_estimate=pl.CostEstimate(
            flops=2 * rows * n * depth, bytes_accessed=2 * n * depth, transcendentals=rows * n
        ),
        name="logits",
    )(scale, shift, q, memory, lab, valid)


def product_kernel(e_ref, mem_ref, a_ref, b5_ref, b3_ref):
    out = jnp.dot(e_ref[...], mem_ref[...], preferred_element_type=jnp.float32)
    a_ref[...] = out[0:128].astype(a_ref.dtype)
    b5_ref[...] = out[128:208].astype(b5_ref.dtype)
    b3_ref[...] = out[208:256].astype(b3_ref.dtype)


def product_call(e, memory, own_dtype, name):
    rows, n = e.shape
    depth = memory.shape[1]
    return pl.pallas_call(
        product_kernel,
        grid=(depth // COLS,),
        in_specs=[pl.BlockSpec((rows, n), lambda i: (0, 0)), pl.BlockSpec((n, COLS), lambda i: (0, i))],
        out_specs=[pl.BlockSpec((k, COLS), lambda i: (0, i)) for k in (128, 80, 48)],
        out_shape=[
            jax.ShapeDtypeStruct((128, depth), own_dtype),
            jax.ShapeDtypeStruct((80, depth), jnp.bfloat16),
            jax.ShapeDtypeStruct((48, depth), jnp.bfloat16),
        ],
        compiler_params=pltpu.CompilerParams(vmem_limit_bytes=VMEM),
        cost_estimate=pl.CostEstimate(
            flops=2 * rows * n * depth, bytes_accessed=2 * n * depth, transcendentals=0
        ),
        name=name,
    )(e, memory)


def merge_kernel(z_ref, cot_ref, sets_ref, coef_ref, part_ref):
    z = z_ref[0]
    sets = [sets_ref[lax.rem(a - z + 12, 8)] for a in range(8)]
    top = sets[0][0:1]
    logit = jnp.zeros_like(top)
    for s in sets:
        top = jnp.maximum(top, jnp.maximum(s[0:1], s[4:5]))
        logit = logit + s[3:4] + s[7:8]
    top = jnp.maximum(top, logit)
    rest = jnp.zeros_like(top)
    first = jnp.zeros_like(top)
    for s in sets:
        for k in (0, 4):
            f = jnp.exp(s[k:k + 1] - top)
            rest = rest + f * s[k + 1:k + 2]
            first = first + f * s[k + 2:k + 3]
    total = rest + jnp.exp(logit - top)
    mine = sets_ref[4]
    inverse = 1.0 / total
    label_weight = -rest * inverse
    own = jnp.exp(mine[0:1] - top) * inverse
    other = jnp.exp(mine[4:5] - top) * inverse
    part = cot_ref[...] * (first * inverse + label_weight * logit)
    part_ref[...] = jnp.broadcast_to(jnp.sum(part, axis=1, keepdims=True), part_ref.shape)
    row = lax.broadcasted_iota(jnp.int32, (8, 128), 0)
    stack = jnp.where(row == 0, own, jnp.where(row == 1, other, label_weight))
    back = lax.rem((10 - z) * 16, 128)
    coef_ref[...] = pltpu.roll(stack, back, 1).T


def merge_call(z, cot, sets):
    return pl.pallas_call(
        merge_kernel,
        in_specs=[
            pl.BlockSpec(memory_space=pltpu.SMEM),
            pl.BlockSpec(memory_space=pltpu.VMEM),
            pl.BlockSpec(memory_space=pltpu.VMEM),
        ],
        out_specs=[pl.BlockSpec(memory_space=pltpu.VMEM), pl.BlockSpec(memory_space=pltpu.VMEM)],
        out_shape=[jax.ShapeDtypeStruct((128, 8), jnp.float32), jax.ShapeDtypeStruct((8, 128), jnp.float32)],
        name="merge",
    )(z, cot, sets)


def shards(queries, memory, log_scale, labels, valid, cotangent):
    scale = jnp.exp(log_scale)
    where = lax.axis_index("mem")
    z = lax.rem(where, 8)
    x_lo = where // 8
    start_row = where * memory.shape[0]
    roll_by = lax.rem(z + 6, 8) * 16

    own_labels = lax.dynamic_slice_in_dim(labels, x_lo * 128, 128)
    own_cot = lax.dynamic_slice_in_dim(cotangent, x_lo * 128, 128)
    rolled = lax.dynamic_slice_in_dim(jnp.concatenate([own_labels, own_labels]), roll_by, 128)
    other = send(rolled.astype(jnp.float32), PARTNER).astype(jnp.int32)
    lab = (jnp.concatenate([rolled, other]) - start_row)[:, None]

    up1, down1, up2, down2 = (send(queries, along_z(k)) for k in (1, -1, 2, -2))
    near = jnp.concatenate([up2, up1, queries, down1, down2])
    up3, down3 = send(up2, along_z(1)), send(down2, along_z(-1))
    low4, high4 = send(up2[:8], along_z(2)), send(down2[8:], along_z(-2))
    far = jnp.concatenate([down3, low4, high4, up3])
    near_other = send(near, PARTNER)
    far_other = send(far, PARTNER)
    everything = jnp.concatenate([near, far, near_other, far_other])

    columns = jnp.arange(memory.shape[0], dtype=jnp.int32)
    hits = (lab == columns[None, :]).astype(jnp.bfloat16)
    g_own, g5, g3 = product_call(hits, memory, jnp.bfloat16, "label_rows")
    g5 = send(g5, PARTNER)
    g3 = send(g3, PARTNER)

    shift = roll_by.reshape(1)
    e, stat = logits_call(scale, shift, everything, memory, lab, valid[None, :])
    stat_other = send(stat, PARTNER)
    pair = jnp.concatenate([stat[0:4], stat_other[4:8]])
    o_own, o5, o3 = product_call(e, memory, jnp.float32, "weighted")
    r3 = send(o3, PARTNER)
    r5 = send(o5, PARTNER)
    s_up, s_down = send(pair, along_z(1)), send(pair, along_z(-1))
    three = jnp.stack([s_up, pair, s_down])
    t_up, t_down = send(three, along_z(3)), send(three[:2], along_z(-3))
    sets = jnp.concatenate([t_up, three, t_down])
    coef, part = merge_call(z.reshape(1), own_cot[None, :], sets)

    f32 = jnp.float32
    bf16 = jnp.bfloat16

    def combine(rows, o_other, g_other):
        c = coef[rows]
        g = g_own[rows].astype(f32) + g_other.astype(f32)
        return c[:, 0:1] * o_own[rows] + c[:, 1:2] * o_other.astype(f32) + c[:, 2:3] * g

    p_far = combine(slice(80, 128), r3, g3).astype(bf16)
    p_near = combine(slice(0, 80), r5, g5)
    a3 = send(p_far[0:16], along_z(1))
    a5 = send(p_far[32:48], along_z(-1))
    a4l = send(p_far[16:24], along_z(2))
    a4h = send(p_far[24:32], along_z(-2))
    a1 = send(p_near[48:64].astype(bf16), along_z(1))
    a7 = send(p_near[16:32].astype(bf16), along_z(-1))
    zero = jnp.zeros((8, memory.shape[1]), f32)
    p2 = p_near[64:80] + a3.astype(f32) + jnp.concatenate([a4l.astype(f32), zero])
    p6 = p_near[0:16] + a5.astype(f32) + jnp.concatenate([zero, a4h.astype(f32)])
    a2 = send(p2.astype(bf16), along_z(2))
    a6 = send(p6.astype(bf16), along_z(-2))
    summed = p_near[32:48] + (a1.astype(f32) + a7.astype(f32)) + (a2.astype(f32) + a6.astype(f32))
    q_rows = queries.shape[0]
    my_cot = lax.dynamic_slice_in_dim(cotangent, where * q_rows, q_rows)
    grad_queries = (scale * my_cot[:, None] * summed).astype(bf16)

    for pairs in (CORE, X1, X2, Y1, Y2):
        part = part + send(part, pairs)
    count = cotangent.shape[0] * lax.axis_size("dp")
    scale_grad = part[0, 0:1] / count
    return (grad_queries, scale_grad)


def solution(mesh):
    placed = (P(("dp", "mem"), None), P("mem", None), P(), P("dp"), P("mem"), P("dp"))
    return jax.shard_map(
        shards, mesh=mesh, in_specs=placed, out_specs=(P(("dp", "mem"), None), P()), check_vma=False
    )
```

time: 258 us -> 143 us (0.55)
  blocking collectives: 139 us -> 0 us
  starting transfers between devices: 0.08 us -> 57.8 us
  waiting for transfers between devices: 73.6 us -> 29.4 us
  Pallas kernels: 0 us -> 36.1 us
  matrix products: 21.2 us -> 0 us
  between operations: 16.5 us -> 3.41 us
  local copies, waits for them, and re-layouts: 0.01 us -> 7.55 us
    psum x2 -> x0, blocking collectives: 107 us -> none  [the longest x1 74 us: shards(): lax.psum(scale_part, ('dp', 'mem'))]
    all_gather x1 -> x0, waiting for transfers between devices: 72.9 us -> none  [shards(): lax.all_gather(queries, 'mem', axis=0, tiled=True)]
    ppermute x0 -> x33, starting transfers between devices: none -> 57.8 us  [send(): return lax.ppermute(x, AXES, pairs)]
    pallas_call x0 -> x4, Pallas kernels: none -> 36.1 us  [the longest x2 22.4 us: product_call(): pl.pallas_call(product_kernel, grid=(depth // COLS,), in_specs=[pl.BlockS...]
    pmax x1 -> x0, blocking collectives: 32.2 us -> none  [shards(): top = lax.pmax(local_top, 'mem')]
    ppermute x0 -> x33, waiting for transfers between devices: none -> 29.4 us  [send(): return lax.ppermute(x, AXES, pairs)]
    dot_general x2 -> x0, matrix products: 21.2 us -> none  [the longest x1 12.3 us: shards(): jnp.dot(weight_half, memory, preferred_element_type=jnp.float32)]
    slice x0 -> x10, local copies, waits for them, and re-layouts: none -> 2.78 us  [the longest x2 2.2 us: combine(): c[:, 0:1] * o_own[rows] + c[:, 1:2] * o_other.astype(f32) + c[:, 2:3] * g]
  transfers between devices with their start and end apart: 2 -> 33, of which waited for: 1 -> 16; matrix products, arithmetic and copies ran while one was open for 1% -> 8% of each run, Pallas kernels for 0% -> 17%
where the time goes in v1:
time: 143 us; the launch traced here: 140 us
  starting transfers between devices  57.8 us (40%)
  Pallas kernels  36.1 us (25%)
  waiting for transfers between devices  29.4 us (21%)
  local copies, waits for them, and re-layouts  7.55 us (5%)
  other arithmetic  5.99 us (4%)
  between operations  3.41 us (2%)
    ppermute x33, starting transfers between devices, send(): return lax.ppermute(x, AXES, pairs)  57.8 us
    ppermute x33, waiting for transfers between devices, send(): return lax.ppermute(x, AXES, pairs)  29.4 us
    pallas_call x2, Pallas kernels, product_call(): pl.pallas_call(product_kernel, grid=(depth // COLS,), in_specs=[pl.BlockS...  22.4 us
    pallas_call x1, Pallas kernels, logits_call(): pl.pallas_call(logits_kernel, grid=(n // BLK,), in_specs=[pl.BlockSpec(me...  12 us
  transfers between devices with their start and end apart: 33, of which 16 were waited for; matrix products, arithmetic and copies ran while one was open for 8% of the time, Pallas kernels for 17%

profile of v1, /device:TPU:32, one launch (start us, length us, event | category | flops | bytes accessed | tf_op | source)
XLA Modules:
  0.0 140.2 jit_solution(10043374176752699044)
XLA Ops:
  0.6 3.3 %collective-permute-start = (bf16[16,4096]{1,0:T(8,128)(2,1)}, bf16[16,4096]{1,0:T(8,128)(2,1)S(1)}, u32[]{:S(2)}, u32[]{:S(2)}) collective-permute-start(bf16[16,4096]{1,0:T(8,128)(2,1)} %param.6), channel_id=1, source_target_pairs={{0,2},{1,3},{2,4},{3,5},{4,6},{5,7},{6,0},{7,1},{16,18},{17,19},{1... | collective-permute-start | bytes 393224 | tf_op jit(solution)/shard_map/ppermute | solution.py:45
  4.0 3.1 %collective-permute-start.1 = (bf16[16,4096]{1,0:T(8,128)(2,1)}, bf16[16,4096]{1,0:T(8,128)(2,1)S(1)}, u32[]{:S(2)}, u32[]{:S(2)}) collective-permute-start(bf16[16,4096]{1,0:T(8,128)(2,1)} %param.6), channel_id=1, source_target_pairs={{0,1},{1,2},{2,3},{3,4},{4,5},{5,6},{6,7},{7,0},{16,17},{17,18},{1... | collective-permute-start | bytes 393224 | tf_op jit(solution)/shard_map/ppermute | solution.py:45
  7.1 1.1 collective-permute-start.3
  8.2 0.8 dynamic_slice.14
  9.1 1.5 %collective-permute-start.10 = (f32[128]{0:T(128)S(1)}, f32[128]{0:T(128)S(1)}, u32[]{:S(2)}, u32[]{:S(2)}) collective-permute-start(f32[128]{0:T(128)S(1)} %get-tuple-element.30), channel_id=1, source_target_pairs={{0,8},{1,9},{2,10},{3,11},{4,12},{5,13},{6,14},{7,15},{16,56},{17,... | collective-permute-start | bytes 1544 | tf_op jit(solution)/shard_map/ppermute | solution.py:45
  10.6 1.3 dynamic-slice_bitcast_fusion.cot_ref
  12.6 0.1 copy.13
  12.8 0.2 fusion.e_ref
  13.1 1.9 %collective-permute-start.5 = (bf16[8,4096]{1,0:T(8,128)(2,1)S(1)}, bf16[8,4096]{1,0:T(8,128)(2,1)S(1)}, u32[]{:S(2)}, u32[]{:S(2)}) collective-permute-start(bf16[8,4096]{1,0:T(8,128)(2,1)S(1)} %slice.108), channel_id=1, source_target_pairs={{0,2},{1,3},{2,4},{3,5},{4,6},{5,7},{6,0},{7,1},{16,18},{17,19},{1... | collective-permute-start | bytes 196616 | tf_op jit(solution)/shard_map/ppermute | solution.py:45
  15.0 1.6 %collective-permute-done.3 = bf16[16,4096]{1,0:T(8,128)(2,1)S(1)} collective-permute-done((bf16[16,4096]{1,0:T(8,128)(2,1)}, bf16[16,4096]{1,0:T(8,128)(2,1)S(1)}, u32[]{:S(2)}, u32[]{:S(2)}) %collective-permute-start.3) | collective-permute-done | bytes 131104 | tf_op jit(solution)/shard_map/ppermute | solution.py:45
  16.6 2.1 %collective-permute-start.6 = (bf16[8,4096]{1,0:T(8,128)(2,1)S(1)}, bf16[8,4096]{1,0:T(8,128)(2,1)S(1)}, u32[]{:S(2)}, u32[]{:S(2)}) collective-permute-start(bf16[8,4096]{1,0:T(8,128)(2,1)S(1)} %slice.109), channel_id=1, source_target_pairs={{0,6},{1,7},{2,0},{3,1},{4,2},{5,3},{6,4},{7,5},{16,22},{17,23},{1... | collective-permute-start | bytes 196616 | tf_op jit(solution)/shard_map/ppermute | solution.py:45
  18.8 1.6 %collective-permute-start.4 = (bf16[16,4096]{1,0:T(8,128)(2,1)S(1)}, bf16[16,4096]{1,0:T(8,128)(2,1)S(1)}, u32[]{:S(2)}, u32[]{:S(2)}) collective-permute-start(bf16[16,4096]{1,0:T(8,128)(2,1)S(1)} %collective-permute-done.3), channel_id=1, source_target_pairs={{0,7},{1,0},{2,1},{3,2},{4,3},{5,4},{6,5},{7,6},{16,23},{17,16},{1... | collective-permute-start | bytes 393224 | tf_op jit(solution)/shard_map/ppermute | solution.py:45
  20.4 0.5 collective-permute-start.7
  20.9 1.6 %collective-permute-start.8 = (bf16[80,4096]{1,0:T(8,128)(2,1)S(1)}, bf16[80,4096]{1,0:T(8,128)(2,1)S(1)}, u32[]{:S(2)}, u32[]{:S(2)}) collective-permute-start(bf16[80,4096]{1,0:T(8,128)(2,1)S(1)} %get-tuple-element.40), channel_id=1, source_target_pairs={{0,8},{1,9},{2,10},{3,11},{4,12},{5,13},{6,14},{7,15},{16,56},{17,... | collective-permute-start | bytes 1966088 | tf_op jit(solution)/shard_map/ppermute | solution.py:45
  22.5 0.8 collective-permute-done.6
  23.4 1.3 collective-permute-done.4
  24.7 0.7 collective-permute-done.7
  25.4 1.6 %collective-permute-start.9 = (bf16[48,4096]{1,0:T(8,128)(2,1)S(1)}, bf16[48,4096]{1,0:T(8,128)(2,1)S(1)}, u32[]{:S(2)}, u32[]{:S(2)}) collective-permute-start(bf16[48,4096]{1,0:T(8,128)(2,1)S(1)} %pad_maximum_fusion), channel_id=1, source_target_pairs={{0,8},{1,9},{2,10},{3,11},{4,12},{5,13},{6,14},{7,15},{16,56},{17,... | collective-permute-start | bytes 1179656 | tf_op jit(solution)/shard_map/ppermute | solution.py:45
  27.1 4.6 %collective-permute-done.8 = bf16[80,4096]{1,0:T(8,128)(2,1)S(1)} collective-permute-done((bf16[80,4096]{1,0:T(8,128)(2,1)S(1)}, bf16[80,4096]{1,0:T(8,128)(2,1)S(1)}, u32[]{:S(2)}, u32[]{:S(2)}) %collective-permute-start.8) | collective-permute-done | bytes 655392 | tf_op jit(solution)/shard_map/ppermute | solution.py:45
  31.7 4.2 %collective-permute-done.9 = bf16[48,4096]{1,0:T(8,128)(2,1)S(1)} collective-permute-done((bf16[48,4096]{1,0:T(8,128)(2,1)S(1)}, bf16[48,4096]{1,0:T(8,128)(2,1)S(1)}, u32[]{:S(2)}, u32[]{:S(2)}) %collective-permute-start.9) | collective-permute-done | bytes 393248 | tf_op jit(solution)/shard_map/ppermute | solution.py:45
  35.9 12.0 %logits.1 = (bf16[256,2048]{1,0:T(8,128)(2,1)S(1)}, f32[8,128]{1,0:T(8,128)S(1)}) custom-call(f32[1]{0:T(128)} %exp.3.scale_ref, s32[1]{0:T(128)} %bitcast.3.shift_ref, bf16[256,4096]{1,0:T(8,128)(2,1)S(1)} %constant_dynamic-update-slice_fusion.5.q_ref, bf16[2048,4096]{1,0:T(8,128)(2,1)} %mem_ref.5, s32[256,1]{1,0:T(8,128)S(1)} %broadcast_subtract_fusion.lab_ref, ...), custom_call_target="tpu_custom_call" | custom-call | flops 4294967296 | bytes 16777216 | tf_op jit(solution)/shard_map/logits/pallas_call | solution.py:94
  47.9 1.5 %collective-permute-start.11 = (f32[8,128]{1,0:T(8,128)S(1)}, f32[8,128]{1,0:T(8,128)S(1)}, u32[]{:S(2)}, u32[]{:S(2)}) collective-permute-start(f32[8,128]{1,0:T(8,128)S(1)} %get-tuple-element.12), channel_id=1, source_target_pairs={{0,8},{1,9},{2,10},{3,11},{4,12},{5,13},{6,14},{7,15},{16,56},{17,... | collective-permute-start | bytes 12296 | tf_op jit(solution)/shard_map/ppermute | solution.py:45
  49.4 11.2 %label_rows.1 = (bf16[128,4096]{1,0:T(8,128)(2,1)S(1)}, bf16[80,4096]{1,0:T(8,128)(2,1)}, bf16[48,4096]{1,0:T(8,128)(2,1)S(1)}) custom-call(bf16[256,2048]{1,0:T(8,128)(2,1)S(1)} %fusion.e_ref, bf16[2048,4096]{1,0:T(8,128)(2,1)} %mem_ref.5), custom_call_target="tpu_custom_call" | custom-call | flops 4294967296 | bytes 16777216 | tf_op jit(solution)/shard_map/label_rows/pallas_call | solution.py:133
  60.6 0.5 collective-permute-start.21
  61.1 1.5 %collective-permute-start.17 = (bf16[80,4096]{1,0:T(8,128)(2,1)}, bf16[80,4096]{1,0:T(8,128)(2,1)}, u32[]{:S(2)}, u32[]{:S(2)}) collective-permute-start(bf16[80,4096]{1,0:T(8,128)(2,1)} %get-tuple-element.18), channel_id=1, source_target_pairs={{0,8},{1,9},{2,10},{3,11},{4,12},{5,13},{6,14},{7,15},{16,56},{17,... | collective-permute-start | bytes 1966088 | tf_op jit(solution)/shard_map/ppermute | solution.py:45
  62.6 2.1 %collective-permute-start.12 = (f32[8,128]{1,0:T(8,128)S(1)}, f32[8,128]{1,0:T(8,128)S(1)}, u32[]{:S(2)}, u32[]{:S(2)}) collective-permute-start(f32[8,128]{1,0:T(8,128)S(1)} %get-tuple-element.51), channel_id=1, source_target_pairs={{0,1},{1,2},{2,3},{3,4},{4,5},{5,6},{6,7},{7,0},{16,17},{17,18},{1... | collective-permute-start | bytes 12296 | tf_op jit(solution)/shard_map/ppermute | solution.py:45
  64.7 0.1 collective-permute-start.13
  64.9 11.3 %weighted.1 = (f32[128,4096]{1,0:T(8,128)S(1)}, bf16[80,4096]{1,0:T(8,128)(2,1)}, bf16[48,4096]{1,0:T(8,128)(2,1)}) custom-call(bf16[256,2048]{1,0:T(8,128)(2,1)S(1)} %get-tuple-element.14.e_ref, bf16[2048,4096]{1,0:T(8,128)(2,1)} %mem_ref.5), custom_call_target="tpu_custom_call" | custom-call | flops 4294967296 | bytes 16777216 | tf_op jit(solution)/shard_map/weighted/pallas_call | solution.py:133
  76.2 0.5 collective-permute-start.20
  76.7 1.5 %collective-permute-start.16 = (bf16[80,4096]{1,0:T(8,128)(2,1)}, bf16[80,4096]{1,0:T(8,128)(2,1)}, u32[]{:S(2)}, u32[]{:S(2)}) collective-permute-start(bf16[80,4096]{1,0:T(8,128)(2,1)} %get-tuple-element.16), channel_id=1, source_target_pairs={{0,8},{1,9},{2,10},{3,11},{4,12},{5,13},{6,14},{7,15},{16,56},{17,... | collective-permute-start | bytes 1966088 | tf_op jit(solution)/shard_map/ppermute | solution.py:45
  78.2 6.5 %collective-permute-start.14 = (f32[3,8,128]{2,1,0:T(8,128)S(1)}, f32[3,8,128]{2,1,0:T(8,128)S(1)}, u32[]{:S(2)}, u32[]{:S(2)}) collective-permute-start(f32[3,8,128]{2,1,0:T(8,128)S(1)} %pad_maximum_fusion.1), channel_id=1, source_target_pairs={{0,3},{1,4},{2,5},{3,6},{4,7},{5,0},{6,1},{7,2},{16,19},{17,20},{1... | collective-permute-start | bytes 36872 | tf_op jit(solution)/shard_map/ppermute | solution.py:45
  84.7 1.4 %collective-permute-done.14 = f32[3,8,128]{2,1,0:T(8,128)S(1)} collective-permute-done((f32[3,8,128]{2,1,0:T(8,128)S(1)}, f32[3,8,128]{2,1,0:T(8,128)S(1)}, u32[]{:S(2)}, u32[]{:S(2)}) %collective-permute-start.14) | collective-permute-done | bytes 12320 | tf_op jit(solution)/shard_map/ppermute | solution.py:45
  86.1 2.2 %collective-permute-start.15 = (f32[2,8,128]{2,1,0:T(8,128)S(1)}, f32[2,8,128]{2,1,0:T(8,128)S(1)}, u32[]{:S(2)}, u32[]{:S(2)}) collective-permute-start(f32[2,8,128]{2,1,0:T(8,128)S(1)} %pad_maximum_fusion.2), channel_id=1, source_target_pairs={{0,5},{1,6},{2,7},{3,0},{4,1},{5,2},{6,3},{7,4},{16,21},{17,22},{1... | collective-permute-start | bytes 24584 | tf_op jit(solution)/shard_map/ppermute | solution.py:45
  88.3 0.6 constant_dynamic-update-slice_fusion.20
  88.9 0.6 constant_dynamic-update-slice_fusion.19
  89.5 0.6 constant_dynamic-update-slice_fusion.18
  90.1 0.6 constant_dynamic-update-slice_fusion.17
  90.7 2.3 %collective-permute-done.15 = f32[2,8,128]{2,1,0:T(8,128)S(1)} collective-permute-done((f32[2,8,128]{2,1,0:T(8,128)S(1)}, f32[2,8,128]{2,1,0:T(8,128)S(1)}, u32[]{:S(2)}, u32[]{:S(2)}) %collective-permute-start.15) | collective-permute-done | bytes 8224 | tf_op jit(solution)/shard_map/ppermute | solution.py:45
  93.0 0.6 constant_dynamic-update-slice_fusion.16.sets_ref
  93.6 1.6 %merge.1 = (f32[128,8]{1,0:T(8,128)}, f32[8,128]{1,0:T(8,128)}) custom-call(s32[1]{0:T(128)} %bitcast.1.z_ref, f32[1,128]{1,0:T(1,128)} %dynamic-slice_bitcast_fusion.cot_ref, f32[8,8,128]{2,1,0:T(8,128)} %constant_dynamic-update-slice_fusion.16.sets_ref), custom_call_target="tpu_custom_call" | custom-call | tf_op jit(solution)/shard_map/merge/pallas_call | solution.py:182
  95.2 1.1 slice_reduce_fusion.5
  96.3 1.1 slice_reduce_fusion.2
  97.4 1.4 add_convert_fusion
  98.8 1.1 collective-permute-start.22
  99.9 1.0 collective-permute-start.25
  101.0 2.4 %collective-permute-start.23 = (bf16[8,4096]{1,0:T(8,128)(2,1)S(1)}, bf16[8,4096]{1,0:T(8,128)(2,1)S(1)}, u32[]{:S(2)}, u32[]{:S(2)}) collective-permute-start(bf16[8,4096]{1,0:T(8,128)(2,1)S(1)} %get-tuple-element.36), channel_id=1, source_target_pairs={{0,2},{1,3},{2,4},{3,5},{4,6},{5,7},{6,0},{7,1},{16,18},{17,19},{1... | collective-permute-start | bytes 196616 | tf_op jit(solution)/shard_map/ppermute | solution.py:45
  103.4 1.8 %collective-permute-start.26 = (bf16[8,4096]{1,0:T(8,128)(2,1)S(1)}, bf16[8,4096]{1,0:T(8,128)(2,1)S(1)}, u32[]{:S(2)}, u32[]{:S(2)}) collective-permute-start(bf16[8,4096]{1,0:T(8,128)(2,1)S(1)} %get-tuple-element.37), channel_id=1, source_target_pairs={{0,6},{1,7},{2,0},{3,1},{4,2},{5,3},{6,4},{7,5},{16,22},{17,23},{1... | collective-permute-start | bytes 196616 | tf_op jit(solution)/shard_map/ppermute | solution.py:45
  105.2 1.7 %fusion.9 = (bf16[80,4096]{1,0:T(8,128)(2,1)S(1)}, f32[80,4096]{1,0:T(8,128)S(1)}) fusion(bf16[80,4096]{1,0:T(8,128)(2,1)} %collective-permute-done.17, bf16[128,4096]{1,0:T(8,128)(2,1)S(1)} %get-tuple-element.17, f32[80]{0:T(128)S(1)} %get-tuple-element.26, bf16[80,4096]{1,0:T(8,128)(2,1)} %collective-permute-done.16, f32[80]{0:T(128)S(1)} %get-tuple-element.27, ...), kind=kLoop, calls=%fused_computation.53 | loop fusion | flops 3276800 | bytes 5243840 | tf_op jit(solution)/shard_map/convert.5
  106.9 0.5 collective-permute-done.23
  107.4 1.2 collective-permute-done.26
  108.7 3.5 %collective-permute-start.24 = (bf16[16,4096]{1,0:T(8,128)(2,1)S(1)}, bf16[16,4096]{1,0:T(8,128)(2,1)S(1)}, u32[]{:S(2)}, u32[]{:S(2)}) collective-permute-start(bf16[16,4096]{1,0:T(8,128)(2,1)S(1)} %get-tuple-element.32), channel_id=1, source_target_pairs={{0,2},{1,3},{2,4},{3,5},{4,6},{5,7},{6,0},{7,1},{16,18},{17,19},{1... | collective-permute-start | bytes 393224 | tf_op jit(solution)/shard_map/ppermute | solution.py:45
  112.2 0.7 collective-permute-start.27
  112.9 4.6 %collective-permute-start.18 = (bf16[16,4096]{1,0:T(8,128)(2,1)S(1)}, bf16[16,4096]{1,0:T(8,128)(2,1)S(1)}, u32[]{:S(2)}, u32[]{:S(2)}) collective-permute-start(bf16[16,4096]{1,0:T(8,128)(2,1)S(1)} %get-tuple-element.34), channel_id=1, source_target_pairs={{0,1},{1,2},{2,3},{3,4},{4,5},{5,6},{6,7},{7,0},{16,17},{17,18},{1... | collective-permute-start | bytes 393224 | tf_op jit(solution)/shard_map/ppermute | solution.py:45
  117.6 1.2 collective-permute-done.28
  118.7 0.6 collective-permute-start.29
  119.3 3.0 %collective-permute-done.29 = f32[8,128]{1,0:T(8,128)S(1)} collective-permute-done((f32[8,128]{1,0:T(8,128)S(1)}, f32[8,128]{1,0:T(8,128)S(1)}, u32[]{:S(2)}, u32[]{:S(2)}) %collective-permute-start.29) | collective-permute-done | bytes 4128 | tf_op jit(solution)/shard_map/ppermute | solution.py:45
  122.3 2.5 %collective-permute-start.30 = (f32[8,128]{1,0:T(8,128)S(1)}, f32[8,128]{1,0:T(8,128)S(1)}, u32[]{:S(2)}, u32[]{:S(2)}) collective-permute-start(f32[8,128]{1,0:T(8,128)S(1)} %add.94), channel_id=1, source_target_pairs={{0,32},{1,33},{2,34},{3,35},{4,36},{5,37},{6,38},{7,39},{16,48},{1... | collective-permute-start | bytes 12296 | tf_op jit(solution)/shard_map/ppermute | solution.py:45
  124.8 2.6 %collective-permute-done.30 = f32[8,128]{1,0:T(8,128)S(1)} collective-permute-done((f32[8,128]{1,0:T(8,128)S(1)}, f32[8,128]{1,0:T(8,128)S(1)}, u32[]{:S(2)}, u32[]{:S(2)}) %collective-permute-start.30) | collective-permute-done | bytes 4128 | tf_op jit(solution)/shard_map/ppermute | solution.py:45
  127.5 1.6 %collective-permute-start.31 = (f32[8,128]{1,0:T(8,128)S(1)}, f32[8,128]{1,0:T(8,128)S(1)}, u32[]{:S(2)}, u32[]{:S(2)}) collective-permute-start(f32[8,128]{1,0:T(8,128)S(1)} %add.95), channel_id=1, source_target_pairs={{0,64},{1,65},{2,66},{3,67},{4,68},{5,69},{6,70},{7,71},{16,80},{1... | collective-permute-start | bytes 12296 | tf_op jit(solution)/shard_map/ppermute | solution.py:45
  129.0 2.0 %collective-permute-done.31 = f32[8,128]{1,0:T(8,128)S(1)} collective-permute-done((f32[8,128]{1,0:T(8,128)S(1)}, f32[8,128]{1,0:T(8,128)S(1)}, u32[]{:S(2)}, u32[]{:S(2)}) %collective-permute-start.31) | collective-permute-done | bytes 4128 | tf_op jit(solution)/shard_map/ppermute | solution.py:45
  131.1 3.2 %collective-permute-start.32 = (f32[8,128]{1,0:T(8,128)S(1)}, f32[8,128]{1,0:T(8,128)S(1)}, u32[]{:S(2)}, u32[]{:S(2)}) collective-permute-start(f32[8,128]{1,0:T(8,128)S(1)} %add.96), channel_id=1, source_target_pairs={{0,128},{1,129},{2,130},{3,131},{4,132},{5,133},{6,134},{7,135},{1... | collective-permute-start | bytes 12296 | tf_op jit(solution)/shard_map/ppermute | solution.py:45
  134.3 1.9 %collective-permute-done.32 = f32[8,128]{1,0:T(8,128)S(1)} collective-permute-done((f32[8,128]{1,0:T(8,128)S(1)}, f32[8,128]{1,0:T(8,128)S(1)}, u32[]{:S(2)}, u32[]{:S(2)}) %collective-permute-start.32) | collective-permute-done | bytes 4128 | tf_op jit(solution)/shard_map/ppermute | solution.py:45
  136.2 0.5 slice.107
  137.4 1.7 %fusion.7 = bf16[16,4096]{1,0:T(8,128)(2,1)} fusion(f32[80,4096]{1,0:T(8,128)} %copy-done.1, bf16[16,4096]{1,0:T(8,128)(2,1)S(1)} %collective-permute-done.27, bf16[16,4096]{1,0:T(8,128)(2,1)S(1)} %collective-permute-done.24, bf16[16,4096]{1,0:T(8,128)(2,1)S(1)} %collective-permute-done.19, bf16[16,4096]{1,0:T(8,128)(2,1)S(1)} %collective-permute-done.18, ...), kind=kLoop, calls=%fused_computation.14 | loop fusion | flops 655360 | bytes 917568 | tf_op jit(solution)/shard_map/convert_element_type | solution.py:261
  (66 shorter events, 0.7 us)
Async XLA Ops:
  0.6 18.1 %copy-start.2 = (bf16[16,4096]{1,0:T(8,128)(2,1)S(1)}, bf16[16,4096]{1,0:T(8,128)(2,1)}, u32[]{:S(2)}) copy-start(bf16[16,4096]{1,0:T(8,128)(2,1)} %param.6) | copy-start | bytes 393220
  0.6 12.4 %collective-permute-start = (bf16[16,4096]{1,0:T(8,128)(2,1)}, bf16[16,4096]{1,0:T(8,128)(2,1)S(1)}, u32[]{:S(2)}, u32[]{:S(2)}) collective-permute-start(bf16[16,4096]{1,0:T(8,128)(2,1)} %param.6), channel_id=1, source_target_pairs={{0,2},{1,3},{2,4},{3,5},{4,6},{5,7},{6,0},{7,1},{16,18},{17,19},{1... | collective-permute-start | bytes 393224 | tf_op jit(solution)/shard_map/ppermute | solution.py:45
  4.0 14.7 %collective-permute-start.1 = (bf16[16,4096]{1,0:T(8,128)(2,1)}, bf16[16,4096]{1,0:T(8,128)(2,1)S(1)}, u32[]{:S(2)}, u32[]{:S(2)}) collective-permute-start(bf16[16,4096]{1,0:T(8,128)(2,1)} %param.6), channel_id=1, source_target_pairs={{0,1},{1,2},{2,3},{3,4},{4,5},{5,6},{6,7},{7,0},{16,17},{17,18},{1... | collective-permute-start | bytes 393224 | tf_op jit(solution)/shard_map/ppermute | solution.py:45
  7.1 13.8 %collective-permute-start.2 = (bf16[16,4096]{1,0:T(8,128)(2,1)}, bf16[16,4096]{1,0:T(8,128)(2,1)S(1)}, u32[]{:S(2)}, u32[]{:S(2)}) collective-permute-start(bf16[16,4096]{1,0:T(8,128)(2,1)} %param.6), channel_id=1, source_target_pairs={{0,7},{1,0},{2,1},{3,2},{4,3},{5,4},{6,5},{7,6},{16,23},{17,16},{1... | collective-permute-start | bytes 393224 | tf_op jit(solution)/shard_map/ppermute | solution.py:45
  7.1 9.5 %collective-permute-start.3 = (bf16[16,4096]{1,0:T(8,128)(2,1)}, bf16[16,4096]{1,0:T(8,128)(2,1)S(1)}, u32[]{:S(2)}, u32[]{:S(2)}) collective-permute-start(bf16[16,4096]{1,0:T(8,128)(2,1)} %param.6), channel_id=1, source_target_pairs={{0,6},{1,7},{2,0},{3,1},{4,2},{5,3},{6,4},{7,5},{16,22},{17,23},{1... | collective-permute-start | bytes 393224 | tf_op jit(solution)/shard_map/ppermute | solution.py:45
  9.1 3.6 %collective-permute-start.10 = (f32[128]{0:T(128)S(1)}, f32[128]{0:T(128)S(1)}, u32[]{:S(2)}, u32[]{:S(2)}) collective-permute-start(f32[128]{0:T(128)S(1)} %get-tuple-element.30), channel_id=1, source_target_pairs={{0,8},{1,9},{2,10},{3,11},{4,12},{5,13},{6,14},{7,15},{16,56},{17,... | collective-permute-start | bytes 1544 | tf_op jit(solution)/shard_map/ppermute | solution.py:45
  13.1 9.4 %collective-permute-start.5 = (bf16[8,4096]{1,0:T(8,128)(2,1)S(1)}, bf16[8,4096]{1,0:T(8,128)(2,1)S(1)}, u32[]{:S(2)}, u32[]{:S(2)}) collective-permute-start(bf16[8,4096]{1,0:T(8,128)(2,1)S(1)} %slice.108), channel_id=1, source_target_pairs={{0,2},{1,3},{2,4},{3,5},{4,6},{5,7},{6,0},{7,1},{16,18},{17,19},{1... | collective-permute-start | bytes 196616 | tf_op jit(solution)/shard_map/ppermute | solution.py:45
  16.6 6.8 %collective-permute-start.6 = (bf16[8,4096]{1,0:T(8,128)(2,1)S(1)}, bf16[8,4096]{1,0:T(8,128)(2,1)S(1)}, u32[]{:S(2)}, u32[]{:S(2)}) collective-permute-start(bf16[8,4096]{1,0:T(8,128)(2,1)S(1)} %slice.109), channel_id=1, source_target_pairs={{0,6},{1,7},{2,0},{3,1},{4,2},{5,3},{6,4},{7,5},{16,22},{17,23},{1... | collective-permute-start | bytes 196616 | tf_op jit(solution)/shard_map/ppermute | solution.py:45
  18.8 5.9 %collective-permute-start.4 = (bf16[16,4096]{1,0:T(8,128)(2,1)S(1)}, bf16[16,4096]{1,0:T(8,128)(2,1)S(1)}, u32[]{:S(2)}, u32[]{:S(2)}) collective-permute-start(bf16[16,4096]{1,0:T(8,128)(2,1)S(1)} %collective-permute-done.3), channel_id=1, source_target_pairs={{0,7},{1,0},{2,1},{3,2},{4,3},{5,4},{6,5},{7,6},{16,23},{17,16},{1... | collective-permute-start | bytes 393224 | tf_op jit(solution)/shard_map/ppermute | solution.py:45
  20.4 5.0 %collective-permute-start.7 = (bf16[16,4096]{1,0:T(8,128)(2,1)S(1)}, bf16[16,4096]{1,0:T(8,128)(2,1)S(1)}, u32[]{:S(2)}, u32[]{:S(2)}) collective-permute-start(bf16[16,4096]{1,0:T(8,128)(2,1)S(1)} %collective-permute-done), channel_id=1, source_target_pairs={{0,1},{1,2},{2,3},{3,4},{4,5},{5,6},{6,7},{7,0},{16,17},{17,18},{1... | collective-permute-start | bytes 393224 | tf_op jit(solution)/shard_map/ppermute | solution.py:45
  20.9 15.0 %copy-start = (s32[2048]{0:T(1024)S(1)}, s32[2048]{0:T(1024)}, u32[]{:S(2)}) copy-start(s32[2048]{0:T(1024)} %param.10) | copy-start | bytes 24580
  20.9 10.7 %collective-permute-start.8 = (bf16[80,4096]{1,0:T(8,128)(2,1)S(1)}, bf16[80,4096]{1,0:T(8,128)(2,1)S(1)}, u32[]{:S(2)}, u32[]{:S(2)}) collective-permute-start(bf16[80,4096]{1,0:T(8,128)(2,1)S(1)} %get-tuple-element.40), channel_id=1, source_target_pairs={{0,8},{1,9},{2,10},{3,11},{4,12},{5,13},{6,14},{7,15},{16,56},{17,... | collective-permute-start | bytes 1966088 | tf_op jit(solution)/shard_map/ppermute | solution.py:45
  25.4 10.4 %collective-permute-start.9 = (bf16[48,4096]{1,0:T(8,128)(2,1)S(1)}, bf16[48,4096]{1,0:T(8,128)(2,1)S(1)}, u32[]{:S(2)}, u32[]{:S(2)}) collective-permute-start(bf16[48,4096]{1,0:T(8,128)(2,1)S(1)} %pad_maximum_fusion), channel_id=1, source_target_pairs={{0,8},{1,9},{2,10},{3,11},{4,12},{5,13},{6,14},{7,15},{16,56},{17,... | collective-permute-start | bytes 1179656 | tf_op jit(solution)/shard_map/ppermute | solution.py:45
  47.9 14.7 %collective-permute-start.11 = (f32[8,128]{1,0:T(8,128)S(1)}, f32[8,128]{1,0:T(8,128)S(1)}, u32[]{:S(2)}, u32[]{:S(2)}) collective-permute-start(f32[8,128]{1,0:T(8,128)S(1)} %get-tuple-element.12), channel_id=1, source_target_pairs={{0,8},{1,9},{2,10},{3,11},{4,12},{5,13},{6,14},{7,15},{16,56},{17,... | collective-permute-start | bytes 12296 | tf_op jit(solution)/shard_map/ppermute | solution.py:45
  60.6 36.8 %collective-permute-start.21 = (bf16[48,4096]{1,0:T(8,128)(2,1)S(1)}, bf16[48,4096]{1,0:T(8,128)(2,1)}, u32[]{:S(2)}, u32[]{:S(2)}) collective-permute-start(bf16[48,4096]{1,0:T(8,128)(2,1)S(1)} %get-tuple-element.20), channel_id=1, source_target_pairs={{0,8},{1,9},{2,10},{3,11},{4,12},{5,13},{6,14},{7,15},{16,56},{17,... | collective-permute-start | bytes 1179656 | tf_op jit(solution)/shard_map/ppermute | solution.py:45
  61.1 42.3 %collective-permute-start.17 = (bf16[80,4096]{1,0:T(8,128)(2,1)}, bf16[80,4096]{1,0:T(8,128)(2,1)}, u32[]{:S(2)}, u32[]{:S(2)}) collective-permute-start(bf16[80,4096]{1,0:T(8,128)(2,1)} %get-tuple-element.18), channel_id=1, source_target_pairs={{0,8},{1,9},{2,10},{3,11},{4,12},{5,13},{6,14},{7,15},{16,56},{17,... | collective-permute-start | bytes 1966088 | tf_op jit(solution)/shard_map/ppermute | solution.py:45
  62.6 14.1 %collective-permute-start.12 = (f32[8,128]{1,0:T(8,128)S(1)}, f32[8,128]{1,0:T(8,128)S(1)}, u32[]{:S(2)}, u32[]{:S(2)}) collective-permute-start(f32[8,128]{1,0:T(8,128)S(1)} %get-tuple-element.51), channel_id=1, source_target_pairs={{0,1},{1,2},{2,3},{3,4},{4,5},{5,6},{6,7},{7,0},{16,17},{17,18},{1... | collective-permute-start | bytes 12296 | tf_op jit(solution)/shard_map/ppermute | solution.py:45
  64.7 13.5 %collective-permute-start.13 = (f32[8,128]{1,0:T(8,128)S(1)}, f32[8,128]{1,0:T(8,128)S(1)}, u32[]{:S(2)}, u32[]{:S(2)}) collective-permute-start(f32[8,128]{1,0:T(8,128)S(1)} %get-tuple-element.51), channel_id=1, source_target_pairs={{0,7},{1,0},{2,1},{3,2},{4,3},{5,4},{6,5},{7,6},{16,23},{17,16},{1... | collective-permute-start | bytes 12296 | tf_op jit(solution)/shard_map/ppermute | solution.py:45
  76.2 21.2 %collective-permute-start.20 = (bf16[48,4096]{1,0:T(8,128)(2,1)}, bf16[48,4096]{1,0:T(8,128)(2,1)}, u32[]{:S(2)}, u32[]{:S(2)}) collective-permute-start(bf16[48,4096]{1,0:T(8,128)(2,1)} %get-tuple-element.19), channel_id=1, source_target_pairs={{0,8},{1,9},{2,10},{3,11},{4,12},{5,13},{6,14},{7,15},{16,56},{17,... | collective-permute-start | bytes 1179656 | tf_op jit(solution)/shard_map/ppermute | solution.py:45
  76.7 28.5 %collective-permute-start.16 = (bf16[80,4096]{1,0:T(8,128)(2,1)}, bf16[80,4096]{1,0:T(8,128)(2,1)}, u32[]{:S(2)}, u32[]{:S(2)}) collective-permute-start(bf16[80,4096]{1,0:T(8,128)(2,1)} %get-tuple-element.16), channel_id=1, source_target_pairs={{0,8},{1,9},{2,10},{3,11},{4,12},{5,13},{6,14},{7,15},{16,56},{17,... | collective-permute-start | bytes 1966088 | tf_op jit(solution)/shard_map/ppermute | solution.py:45
  78.2 7.9 %collective-permute-start.14 = (f32[3,8,128]{2,1,0:T(8,128)S(1)}, f32[3,8,128]{2,1,0:T(8,128)S(1)}, u32[]{:S(2)}, u32[]{:S(2)}) collective-permute-start(f32[3,8,128]{2,1,0:T(8,128)S(1)} %pad_maximum_fusion.1), channel_id=1, source_target_pairs={{0,3},{1,4},{2,5},{3,6},{4,7},{5,0},{6,1},{7,2},{16,19},{17,20},{1... | collective-permute-start | bytes 36872 | tf_op jit(solution)/shard_map/ppermute | solution.py:45
  86.1 6.9 %collective-permute-start.15 = (f32[2,8,128]{2,1,0:T(8,128)S(1)}, f32[2,8,128]{2,1,0:T(8,128)S(1)}, u32[]{:S(2)}, u32[]{:S(2)}) collective-permute-start(f32[2,8,128]{2,1,0:T(8,128)S(1)} %pad_maximum_fusion.2), channel_id=1, source_target_pairs={{0,5},{1,6},{2,7},{3,0},{4,1},{5,2},{6,3},{7,4},{16,21},{17,22},{1... | collective-permute-start | bytes 24584 | tf_op jit(solution)/shard_map/ppermute | solution.py:45
  98.8 9.8 %collective-permute-start.22 = (bf16[16,4096]{1,0:T(8,128)(2,1)S(1)}, bf16[16,4096]{1,0:T(8,128)(2,1)S(1)}, u32[]{:S(2)}, u32[]{:S(2)}) collective-permute-start(bf16[16,4096]{1,0:T(8,128)(2,1)S(1)} %get-tuple-element.38), channel_id=1, source_target_pairs={{0,1},{1,2},{2,3},{3,4},{4,5},{5,6},{6,7},{7,0},{16,17},{17,18},{1... | collective-permute-start | bytes 393224 | tf_op jit(solution)/shard_map/ppermute | solution.py:45
  99.9 8.7 %collective-permute-start.25 = (bf16[16,4096]{1,0:T(8,128)(2,1)S(1)}, bf16[16,4096]{1,0:T(8,128)(2,1)S(1)}, u32[]{:S(2)}, u32[]{:S(2)}) collective-permute-start(bf16[16,4096]{1,0:T(8,128)(2,1)S(1)} %get-tuple-element.39), channel_id=1, source_target_pairs={{0,7},{1,0},{2,1},{3,2},{4,3},{5,4},{6,5},{7,6},{16,23},{17,16},{1... | collective-permute-start | bytes 393224 | tf_op jit(solution)/shard_map/ppermute | solution.py:45
  101.0 6.5 %collective-permute-start.23 = (bf16[8,4096]{1,0:T(8,128)(2,1)S(1)}, bf16[8,4096]{1,0:T(8,128)(2,1)S(1)}, u32[]{:S(2)}, u32[]{:S(2)}) collective-permute-start(bf16[8,4096]{1,0:T(8,128)(2,1)S(1)} %get-tuple-element.36), channel_id=1, source_target_pairs={{0,2},{1,3},{2,4},{3,5},{4,6},{5,7},{6,0},{7,1},{16,18},{17,19},{1... | collective-permute-start | bytes 196616 | tf_op jit(solution)/shard_map/ppermute | solution.py:45
  103.4 5.2 %collective-permute-start.26 = (bf16[8,4096]{1,0:T(8,128)(2,1)S(1)}, bf16[8,4096]{1,0:T(8,128)(2,1)S(1)}, u32[]{:S(2)}, u32[]{:S(2)}) collective-permute-start(bf16[8,4096]{1,0:T(8,128)(2,1)S(1)} %get-tuple-element.37), channel_id=1, source_target_pairs={{0,6},{1,7},{2,0},{3,1},{4,2},{5,3},{6,4},{7,5},{16,22},{17,23},{1... | collective-permute-start | bytes 196616 | tf_op jit(solution)/shard_map/ppermute | solution.py:45
  105.2 12.4 %copy-start.3 = (f32[8,128]{1,0:T(8,128)S(1)}, f32[8,128]{1,0:T(8,128)}, u32[]{:S(2)}) copy-start(f32[8,128]{1,0:T(8,128)} %get-tuple-element.21) | copy-start | bytes 12292
  105.2 29.1 %copy-start.4 = (f32[256]{0:T(256)S(1)}, f32[256]{0:T(256)}, u32[]{:S(2)}) copy-start(f32[256]{0:T(256)} %param.11) | copy-start | bytes 3076
  106.9 1.7 %copy-start.1 = (f32[80,4096]{1,0:T(8,128)}, f32[80,4096]{1,0:T(8,128)S(1)}, u32[]{:S(2)}) copy-start(f32[80,4096]{1,0:T(8,128)S(1)} %get-tuple-element.29) | copy-start | bytes 3932164
  108.7 28.7 %collective-permute-start.24 = (bf16[16,4096]{1,0:T(8,128)(2,1)S(1)}, bf16[16,4096]{1,0:T(8,128)(2,1)S(1)}, u32[]{:S(2)}, u32[]{:S(2)}) collective-permute-start(bf16[16,4096]{1,0:T(8,128)(2,1)S(1)} %get-tuple-element.32), channel_id=1, source_target_pairs={{0,2},{1,3},{2,4},{3,5},{4,6},{5,7},{6,0},{7,1},{16,18},{17,19},{1... | collective-permute-start | bytes 393224 | tf_op jit(solution)/shard_map/ppermute | solution.py:45
  112.2 25.1 %collective-permute-start.27 = (bf16[16,4096]{1,0:T(8,128)(2,1)S(1)}, bf16[16,4096]{1,0:T(8,128)(2,1)S(1)}, u32[]{:S(2)}, u32[]{:S(2)}) collective-permute-start(bf16[16,4096]{1,0:T(8,128)(2,1)S(1)} %get-tuple-element.33), channel_id=1, source_target_pairs={{0,6},{1,7},{2,0},{3,1},{4,2},{5,3},{6,4},{7,5},{16,22},{17,23},{1... | collective-permute-start | bytes 393224 | tf_op jit(solution)/shard_map/ppermute | solution.py:45
  112.9 24.4 %collective-permute-start.18 = (bf16[16,4096]{1,0:T(8,128)(2,1)S(1)}, bf16[16,4096]{1,0:T(8,128)(2,1)S(1)}, u32[]{:S(2)}, u32[]{:S(2)}) collective-permute-start(bf16[16,4096]{1,0:T(8,128)(2,1)S(1)} %get-tuple-element.34), channel_id=1, source_target_pairs={{0,1},{1,2},{2,3},{3,4},{4,5},{5,6},{6,7},{7,0},{16,17},{17,18},{1... | collective-permute-start | bytes 393224 | tf_op jit(solution)/shard_map/ppermute | solution.py:45
  117.6 19.8 %collective-permute-start.19 = (bf16[16,4096]{1,0:T(8,128)(2,1)S(1)}, bf16[16,4096]{1,0:T(8,128)(2,1)S(1)}, u32[]{:S(2)}, u32[]{:S(2)}) collective-permute-start(bf16[16,4096]{1,0:T(8,128)(2,1)S(1)} %get-tuple-element.35), channel_id=1, source_target_pairs={{0,7},{1,0},{2,1},{3,2},{4,3},{5,4},{6,5},{7,6},{16,23},{17,16},{1... | collective-permute-start | bytes 393224 | tf_op jit(solution)/shard_map/ppermute | solution.py:45
  117.6 1.2 collective-permute-start.28
  118.7 3.6 %collective-permute-start.29 = (f32[8,128]{1,0:T(8,128)S(1)}, f32[8,128]{1,0:T(8,128)S(1)}, u32[]{:S(2)}, u32[]{:S(2)}) collective-permute-start(f32[8,128]{1,0:T(8,128)S(1)} %add.93), channel_id=1, source_target_pairs={{0,8},{1,9},{2,10},{3,11},{4,12},{5,13},{6,14},{7,15},{16,24},{17,... | collective-permute-start | bytes 12296 | tf_op jit(solution)/shard_map/ppermute | solution.py:45
  122.3 5.1 %collective-permute-start.30 = (f32[8,128]{1,0:T(8,128)S(1)}, f32[8,128]{1,0:T(8,128)S(1)}, u32[]{:S(2)}, u32[]{:S(2)}) collective-permute-start(f32[8,128]{1,0:T(8,128)S(1)} %add.94), channel_id=1, source_target_pairs={{0,32},{1,33},{2,34},{3,35},{4,36},{5,37},{6,38},{7,39},{16,48},{1... | collective-permute-start | bytes 12296 | tf_op jit(solution)/shard_map/ppermute | solution.py:45
  127.5 3.6 %collective-permute-start.31 = (f32[8,128]{1,0:T(8,128)S(1)}, f32[8,128]{1,0:T(8,128)S(1)}, u32[]{:S(2)}, u32[]{:S(2)}) collective-permute-start(f32[8,128]{1,0:T(8,128)S(1)} %add.95), channel_id=1, source_target_pairs={{0,64},{1,65},{2,66},{3,67},{4,68},{5,69},{6,70},{7,71},{16,80},{1... | collective-permute-start | bytes 12296 | tf_op jit(solution)/shard_map/ppermute | solution.py:45
  131.1 5.1 %collective-permute-start.32 = (f32[8,128]{1,0:T(8,128)S(1)}, f32[8,128]{1,0:T(8,128)S(1)}, u32[]{:S(2)}, u32[]{:S(2)}) collective-permute-start(f32[8,128]{1,0:T(8,128)S(1)} %add.96), channel_id=1, source_target_pairs={{0,128},{1,129},{2,130},{3,131},{4,132},{5,133},{6,134},{7,135},{1... | collective-permute-start | bytes 12296 | tf_op jit(solution)/shard_map/ppermute | solution.py:45

commit v2 on v0

v2 whole, which is shorter than its diff:
```python
import functools

import jax
import jax.numpy as jnp
from jax import lax
from jax.experimental import pallas as pl
from jax.experimental.pallas import tpu as pltpu
from jax.sharding import PartitionSpec as P

AXES = ("dp", "mem")
NEG = -1e30
BLK = 512
COLS = 1024


def table(move):
    pairs = []
    for y in range(4):
        for x in range(4):
            for c in range(2):
                for z in range(8):
                    index = lambda y, x, c, z: (((y * 2 + x // 2) * 2 + c) * 2 + x % 2) * 8 + z
                    pairs.append((index(y, x, c, z), index(*move(y, x, c, z))))
    return pairs


def along_z(k):
    return table(lambda y, x, c, z: (y, x, c, (z + k) % 8))


def partner_of(x, c):
    if c == 0:
        return x ^ 1
    return (x + 1) % 4 if x % 2 else (x - 1) % 4


PARTNER = table(lambda y, x, c, z: (y, partner_of(x, c), c, z))
CORE = table(lambda y, x, c, z: (y, x, 1 - c, z))
CROSS = table(lambda y, x, c, z: (y, partner_of(x, 1 - c), c, z))
Y1 = table(lambda y, x, c, z: (y ^ 1, x, c, z))
Y2 = table(lambda y, x, c, z: (y ^ 2, x, c, z))


def send(x, pairs):
    return lax.ppermute(x, AXES, pairs)


def logits_kernel(scale_ref, shift_ref, q_ref, mem_ref, lab_ref, valid_ref, e_ref, stat_ref, l_scr):
    rows, n = l_scr.shape
    scale = scale_ref[0]
    top = jnp.full((rows, 1), NEG, jnp.float32)
    picked = jnp.zeros((rows, 1), jnp.float32)
    for i in range(0, n, BLK):
        raw = lax.dot_general(
            q_ref[...], mem_ref[i:i + BLK, :], (((1,), (1,)), ((), ())), preferred_element_type=jnp.float32
        )
        logit = raw * scale
        column = lax.broadcasted_iota(jnp.int32, logit.shape, 1) + i
        hit = lab_ref[...] == column
        kept = jnp.where(jnp.logical_and(valid_ref[:, i:i + BLK] > 0, jnp.logical_not(hit)), logit, NEG)
        l_scr[:, i:i + BLK] = kept
        top = jnp.maximum(top, jnp.max(kept, axis=1, keepdims=True))
        picked = picked + jnp.sum(jnp.where(hit, logit, 0.0), axis=1, keepdims=True)
    half = rows // 2
    step = 32
    lane = lax.broadcasted_iota(jnp.int32, (step, 128), 1)
    tiles = []
    for r in range(0, rows, step):
        m = top[r:r + step]
        val = l_scr[r:r + step, :]
        e = jnp.exp(val - m)
        e_ref[r:r + step, :] = e.astype(jnp.bfloat16)
        s = jnp.sum(e, axis=1, keepdims=True)
        t = jnp.sum(e * val, axis=1, keepdims=True)
        tiles.append(jnp.where(lane == 0, m, jnp.where(lane == 1, s, jnp.where(lane == 2, t, picked[r:r + step]))))
    full = jnp.concatenate(tiles, axis=0)
    own = pltpu.roll(full[:half].T, shift_ref[0], 1)
    other = pltpu.roll(full[half:].T, shift_ref[0], 1)
    for k in range(4):
        stat_ref[2 * k:2 * k + 1, :] = own[k:k + 1, :]
        stat_ref[2 * k + 1:2 * k + 2, :] = other[k:k + 1, :]


def vmem():
    return pl.BlockSpec(memory_space=pltpu.VMEM)


def smem():
    return pl.BlockSpec(memory_space=pltpu.SMEM)


def params(mib):
    return pltpu.CompilerParams(vmem_limit_bytes=mib * 1024 * 1024)


def logits_call(scale, shift, q, memory, lab, valid):
    rows, depth = q.shape
    n = memory.shape[0]
    return pl.pallas_call(
        logits_kernel,
        in_specs=[smem(), smem(), vmem(), vmem(), vmem(), vmem()],
        out_specs=[vmem(), vmem()],
        out_shape=[
            jax.ShapeDtypeStruct((rows, n), jnp.bfloat16),
            jax.ShapeDtypeStruct((8, 128), jnp.float32),
        ],
        scratch_shapes=[pltpu.VMEM((rows, n), jnp.float32)],
        compiler_params=params(16),
        cost_estimate=pl.CostEstimate(
            flops=2 * rows * n * depth, bytes_accessed=2 * n * depth, transcendentals=rows * n
        ),
        name="logits",
    )(scale, shift, q, memory, lab, valid)


def weighted_kernel(first, e_ref, mem_ref, own_ref, other_ref):
    for c in range(0, own_ref.shape[1], COLS):
        at = slice(c, c + COLS)
        out = jnp.dot(e_ref[...], mem_ref[:, first + c:first + c + COLS], preferred_element_type=jnp.float32)
        own_ref[:, at] = out[:128]
        other_ref[:, at] = out[128:].astype(other_ref.dtype)


def weighted_call(e, memory, first, width):
    rows, n = e.shape
    return pl.pallas_call(
        functools.partial(weighted_kernel, first),
        in_specs=[vmem(), vmem()],
        out_specs=[vmem(), vmem()],
        out_shape=[
            jax.ShapeDtypeStruct((128, width), jnp.float32),
            jax.ShapeDtypeStruct((128, width), jnp.bfloat16),
        ],
        compiler_params=params(16),
        cost_estimate=pl.CostEstimate(flops=2 * rows * n * width, bytes_accessed=2 * n * width, transcendentals=0),
        name="weighted",
    )(e, memory)


def labels_kernel(lab_ref, mem_ref, copy_ref, own_ref, other_ref, hit_scr, sems):
    rows, n = hit_scr.shape
    depth = mem_ref.shape[1]
    pieces = depth // COLS

    def piece(k):
        at = pl.ds(k * COLS, COLS)
        return pltpu.make_async_copy(mem_ref.at[:, at], copy_ref.at[:, at], sems.at[k])

    for k in range(pieces):
        piece(k).start()
    for i in range(0, n, BLK):
        column = lax.broadcasted_iota(jnp.int32, (rows, BLK), 1) + i
        hit_scr[:, i:i + BLK] = jnp.where(lab_ref[...] == column, 1.0, 0.0).astype(jnp.bfloat16)
    for k in range(pieces):
        piece(k).wait()
        c = k * COLS
        out = jnp.dot(hit_scr[...], copy_ref[:, c:c + COLS], preferred_element_type=jnp.float32)
        own_ref[:, c:c + COLS] = out[:128].astype(own_ref.dtype)
        other_ref[:, c:c + COLS] = out[128:].astype(other_ref.dtype)


def labels_call(lab, memory):
    rows = lab.shape[0]
    n, depth = memory.shape
    return pl.pallas_call(
        labels_kernel,
        in_specs=[vmem(), pl.BlockSpec(memory_space=pltpu.HBM)],
        out_specs=[vmem()] * 3,
        out_shape=[
            pltpu.VMEM((n, depth), jnp.bfloat16),
            jax.ShapeDtypeStruct((128, depth), jnp.bfloat16),
            jax.ShapeDtypeStruct((128, depth), jnp.bfloat16),
        ],
        scratch_shapes=[pltpu.VMEM((rows, n), jnp.bfloat16), pltpu.SemaphoreType.DMA((depth // COLS,))],
        compiler_params=params(16),
        cost_estimate=pl.CostEstimate(
            flops=2 * rows * n * depth, bytes_accessed=2 * n * depth, transcendentals=0
        ),
        name="label_rows",
    )(lab, memory)


def mix_kernel(place_ref, cot_ref, up_ref, mid_ref, down_ref, oa_ref, ob_ref, ra_ref, rb_ref, g_ref, gr_ref,
               pu_ref, pd_ref, p4a_ref, p4b_ref, p0_ref, p2_ref, p6_ref, part_ref, sets):
    f32, bf16 = jnp.float32, jnp.bfloat16
    z, x_lo = place_ref[0], place_ref[1]
    sets[0:3] = up_ref[...]
    sets[3:6] = mid_ref[...]
    sets[6:8] = down_ref[...]
    mine, theirs = sets[4, 0], sets[4, 1]
    flat = []
    for a in range(8):
        at = lax.rem(a - z + 12, 8)
        own, other = sets[at, 0], sets[at, 1]
        row = lax.broadcasted_iota(jnp.int32, other.shape, 0)
        swapped = jnp.where(row % 2 == 0, pltpu.roll(other, 7, 0), pltpu.roll(other, 1, 0))
        is_low = x_lo == 0
        flat += [jnp.where(is_low, own, swapped), jnp.where(is_low, swapped, own)]
    top = flat[0][0:2]
    logit = jnp.zeros_like(top)
    for s in flat:
        top = jnp.maximum(top, s[0:2])
        logit = logit + s[6:8]
    top = jnp.maximum(top, logit)
    rest = jnp.zeros_like(top)
    first = jnp.zeros_like(top)
    for s in flat:
        f = jnp.exp(s[0:2] - top)
        rest = rest + f * s[2:4]
        first = first + f * s[4:6]
    inverse = 1.0 / (rest + jnp.exp(logit - top))
    label_weight = -rest * inverse
    part = jnp.sum(cot_ref[...] * (first * inverse + label_weight * logit), axis=1, keepdims=True)
    part_ref[...] = jnp.broadcast_to(part[0:1] + part[1:2], part_ref.shape)
    c_own = jnp.exp(mine[0:1] - top[0:1]) * inverse[0:1]
    c_other = jnp.exp(theirs[1:2] - top[0:1]) * inverse[0:1]
    row = lax.broadcasted_iota(jnp.int32, (8, 128), 0)
    stack = jnp.where(row == 0, c_own, jnp.where(row == 1, c_other, label_weight[0:1]))
    coef = pltpu.roll(stack, lax.rem((10 - z) * 16, 128), 1).T
    half = oa_ref.shape[1]

    def mixed(k):
        at = slice(16 * k, 16 * k + 16)
        c = coef[at]
        sides = []
        for o_ref, r_ref, first in ((oa_ref, ra_ref, 0), (ob_ref, rb_ref, half)):
            cols = slice(first, first + half)
            g = g_ref[at, cols].astype(f32) + gr_ref[at, cols].astype(f32)
            sides.append(c[:, 0:1] * o_ref[at, :] + c[:, 1:2] * r_ref[at, :].astype(f32) + c[:, 2:3] * g)
        return jnp.concatenate(sides, axis=1)

    p6_ref[...] = mixed(0)
    pd_ref[0:16, :] = mixed(1).astype(bf16)
    p0_ref[...] = mixed(2)
    pu_ref[0:16, :] = mixed(3).astype(bf16)
    p2_ref[...] = mixed(4)
    pu_ref[16:32, :] = mixed(5).astype(bf16)
    p4 = mixed(6).astype(bf16)
    p4a_ref[...] = p4[:, :half]
    p4b_ref[...] = p4[:, half:]
    pd_ref[16:32, :] = mixed(7).astype(bf16)


def mix_call(place, cot, up, mid, down, oa, ob, ra, rb, g, gr):
    depth = g.shape[1]
    bf16, f32 = jnp.bfloat16, jnp.float32
    return pl.pallas_call(
        mix_kernel,
        in_specs=[smem()] + [vmem()] * 10,
        out_specs=[vmem()] * 8,
        out_shape=[
            jax.ShapeDtypeStruct((32, depth), bf16),
            jax.ShapeDtypeStruct((32, depth), bf16),
            jax.ShapeDtypeStruct((16, depth // 2), bf16),
            jax.ShapeDtypeStruct((16, depth // 2), bf16),
            jax.ShapeDtypeStruct((16, depth), f32),
            jax.ShapeDtypeStruct((16, depth), f32),
            jax.ShapeDtypeStruct((16, depth), f32),
            jax.ShapeDtypeStruct((8, 128), f32),
        ],
        scratch_shapes=[pltpu.VMEM((8, 2, 8, 128), f32)],
        compiler_params=params(16),
        name="mix",
    )(place, cot, up, mid, down, oa, ob, ra, rb, g, gr)


def shards(queries, memory, log_scale, labels, valid, cotangent):
    f32, bf16 = jnp.float32, jnp.bfloat16
    together = lambda *arrays: lax.optimization_barrier(arrays)
    scale = jnp.exp(log_scale)
    where = lax.axis_index("mem")
    z = lax.rem(where, 8)
    x_lo = where // 8
    half = memory.shape[1] // 2
    start_row = where * memory.shape[0]
    roll_by = lax.rem(z + 6, 8) * 16

    own_labels = lax.dynamic_slice_in_dim(labels, x_lo * 128, 128)
    own_cot = lax.dynamic_slice_in_dim(cotangent, x_lo * 128, 128)
    rolled = lax.dynamic_slice_in_dim(jnp.concatenate([own_labels, own_labels]), roll_by, 128)
    other = send(jnp.stack([rolled.astype(f32), own_cot]), PARTNER)
    lab = (jnp.concatenate([rolled, other[0].astype(jnp.int32)]) - start_row)[:, None]
    cots = jnp.stack([own_cot, other[1]])

    up1, down1, up2, down2 = (send(queries, along_z(k)) for k in (1, -1, 2, -2))
    near = jnp.concatenate([up2, up1, queries, down1, down2])
    up3, down3 = send(up2, along_z(1)), send(down2, along_z(-1))
    low4, high4 = send(up2[:, :half], along_z(2)), send(down2[:, half:], along_z(-2))
    far = jnp.concatenate([down3, jnp.concatenate([low4, high4], axis=1), up3])
    near_other = send(near, PARTNER)
    far_other = send(far, PARTNER)

    late_lab, _ = together(lab, far)
    resident, g, g_other = labels_call(late_lab, pltpu.with_memory_space_constraint(memory, pltpu.HBM))
    resident = pltpu.with_memory_space_constraint(resident, pltpu.VMEM)
    everything = jnp.concatenate([near, far, near_other, far_other])
    g_other = send(g_other, PARTNER)

    e, stat = logits_call(scale, roll_by.reshape(1), everything, resident, lab, valid[None, :])
    stat_other = send(stat, PARTNER)
    e, g_other = together(e, g_other)
    oa, o_other = weighted_call(e, resident, 0, half)
    stat_other, o_other, e = together(stat_other, o_other, e)
    ra = send(o_other, PARTNER)
    pair = jnp.stack([stat, stat_other])
    ob, o_other = weighted_call(e, resident, half, half)
    rb = send(o_other, PARTNER)
    s_up, s_down = send(pair, along_z(1)), send(pair, along_z(-1))
    three = jnp.stack([s_up, pair, s_down])
    t_up, t_down = send(three, along_z(3)), send(three[:2], along_z(-3))
    pu, pd, p4a, p4b, p0, p2, p6, part = mix_call(
        jnp.stack([z, x_lo]), cots, t_up, three, t_down, oa, ob, ra, rb, g, g_other
    )
    au, ad = send(pu, along_z(1)), send(pd, along_z(-1))
    a4a, a4b = send(p4a, along_z(2)), send(p4b, along_z(-2))
    part = part + send(part, CROSS)
    au, ad, a4a, a4b, part = together(au, ad, a4a, a4b, part)
    zero = jnp.zeros((16, half), f32)
    p2 = p2 + au[16:].astype(f32) + jnp.concatenate([a4a.astype(f32), zero], axis=1)
    p6 = p6 + ad[16:].astype(f32) + jnp.concatenate([zero, a4b.astype(f32)], axis=1)
    a2 = send(p2.astype(bf16), along_z(2))
    a6 = send(p6.astype(bf16), along_z(-2))
    for pairs in (CORE, Y1, Y2):
        part = part + send(part, pairs)
    summed = p0 + (au[:16].astype(f32) + ad[:16].astype(f32)) + (a2.astype(f32) + a6.astype(f32))
    q_rows = queries.shape[0]
    my_cot = lax.dynamic_slice_in_dim(cotangent, where * q_rows, q_rows)
    grad_queries = (scale * my_cot[:, None] * summed).astype(bf16)

    count = cotangent.shape[0] * lax.axis_size("dp")
    scale_grad = part[0, 0:1] / count
    return (grad_queries, scale_grad)


def solution(mesh):
    placed = (P(("dp", "mem"), None), P("mem", None), P(), P("dp"), P("mem"), P("dp"))
    return jax.shard_map(
        shards, mesh=mesh, in_specs=placed, out_specs=(P(("dp", "mem"), None), P()), check_vma=False
    )
```

time: 258 us -> 108 us (0.42)
  the two profiles are of different devices: /device:TPU:32 before, /device:TPU:26 now
where the time goes in v2:
time: 108 us
  starting transfers between devices  47.2 us (44%)
  waiting for transfers between devices  34 us (31%)
  Pallas kernels  19.2 us (18%)
  between operations  3.42 us (3%)
  local copies, waits for them, and re-layouts  3.28 us (3%)
  other arithmetic  1.15 us (1%)
    ppermute x29, starting transfers between devices, send(): return lax.ppermute(x, AXES, pairs)  47.2 us
    ppermute x29, waiting for transfers between devices, send(): return lax.ppermute(x, AXES, pairs)  34 us
    pallas_call x1, Pallas kernels, labels_call(): pl.pallas_call(labels_kernel, in_specs=[vmem(), pl.BlockSpec(memory_space...  7.48 us
    pallas_call x1, Pallas kernels, logits_call(): pl.pallas_call(logits_kernel, in_specs=[smem(), smem(), vmem(), vmem(), v...  5.48 us
    pallas_call x2, Pallas kernels, weighted_call(): pl.pallas_call(functools.partial(weighted_kernel, first), in_specs=[vmem(...  4.78 us
  transfers between devices with their start and end apart: 29, of which 14 were waited for; matrix products, arithmetic and copies ran while one was open for 2% of the time, Pallas kernels for 14%

profile of v2, /device:TPU:26, one launch (start us, length us, event | category | flops | bytes accessed | tf_op | source)
XLA Modules:
  0.0 108.3 jit_solution(4272170409454171796)
XLA Ops:
  0.7 0.8 dynamic-slice_bitcast_fusion
  1.4 0.8 dynamic_slice.14
  2.2 0.1 dynamic-slice_bitcast_fusion.1
  2.3 0.6 collective-permute-start
  2.9 5.9 %collective-permute-start.3 = (bf16[16,4096]{1,0:T(8,128)(2,1)}, bf16[16,4096]{1,0:T(8,128)(2,1)S(1)}, u32[]{:S(2)}, u32[]{:S(2)}) collective-permute-start(bf16[16,4096]{1,0:T(8,128)(2,1)} %param.6), channel_id=1, source_target_pairs={{0,7},{1,0},{2,1},{3,2},{4,3},{5,4},{6,5},{7,6},{16,23},{17,16},{1... | collective-permute-start | bytes 393224 | tf_op jit(solution)/shard_map/ppermute | solution.py:45
  8.7 0.0 collective-permute-start.2
  8.7 4.1 %collective-permute-start.4 = (bf16[16,4096]{1,0:T(8,128)(2,1)}, bf16[16,4096]{1,0:T(8,128)(2,1)S(1)}, u32[]{:S(2)}, u32[]{:S(2)}) collective-permute-start(bf16[16,4096]{1,0:T(8,128)(2,1)} %param.6), channel_id=1, source_target_pairs={{0,6},{1,7},{2,0},{3,1},{4,2},{5,3},{6,4},{7,5},{16,22},{17,23},{1... | collective-permute-start | bytes 393224 | tf_op jit(solution)/shard_map/ppermute | solution.py:45
  13.6 0.1 copy.10
  13.7 6.0 %collective-permute-done.1 = bf16[16,4096]{1,0:T(8,128)(2,1)S(1)} collective-permute-done((bf16[16,4096]{1,0:T(8,128)(2,1)}, bf16[16,4096]{1,0:T(8,128)(2,1)S(1)}, u32[]{:S(2)}, u32[]{:S(2)}) %collective-permute-start.1) | collective-permute-done | bytes 131104 | tf_op jit(solution)/shard_map/ppermute | solution.py:45
  19.7 0.0 collective-permute-start.6
  19.8 4.2 %collective-permute-start.7 = (bf16[16,2048]{1,0:T(8,128)(2,1)S(1)}, bf16[16,2048]{1,0:T(8,128)(2,1)S(1)}, u32[]{:S(2)}, u32[]{:S(2)}) collective-permute-start(bf16[16,2048]{1,0:T(8,128)(2,1)S(1)} %slice.39), channel_id=1, source_target_pairs={{0,6},{1,7},{2,0},{3,1},{4,2},{5,3},{6,4},{7,5},{16,22},{17,23},{1... | collective-permute-start | bytes 196616 | tf_op jit(solution)/shard_map/ppermute | solution.py:45
  24.0 0.9 constant_dynamic-update-slice_fusion.2
  25.0 3.3 %collective-permute-start.8 = (bf16[16,4096]{1,0:T(8,128)(2,1)S(1)}, bf16[16,4096]{1,0:T(8,128)(2,1)S(1)}, u32[]{:S(2)}, u32[]{:S(2)}) collective-permute-start(bf16[16,4096]{1,0:T(8,128)(2,1)S(1)} %collective-permute-done.1), channel_id=1, source_target_pairs={{0,1},{1,2},{2,3},{3,4},{4,5},{5,6},{6,7},{7,0},{16,17},{17,18},{1... | collective-permute-start | bytes 393224 | tf_op jit(solution)/shard_map/ppermute | solution.py:45
  28.2 0.0 collective-permute-start.5
  28.3 0.0 collective-permute-done.3
  28.3 2.0 %collective-permute-start.9 = (bf16[80,4096]{1,0:T(8,128)(2,1)S(1)}, bf16[80,4096]{1,0:T(8,128)(2,1)S(1)}, u32[]{:S(2)}, u32[]{:S(2)}) collective-permute-start(bf16[80,4096]{1,0:T(8,128)(2,1)S(1)} %get-tuple-element.58), channel_id=1, source_target_pairs={{0,8},{1,9},{2,10},{3,11},{4,12},{5,13},{6,14},{7,15},{16,56},{17,... | collective-permute-start | bytes 1966088 | tf_op jit(solution)/shard_map/ppermute | solution.py:45
  30.3 0.0 collective-permute-done.6
  30.3 0.0 collective-permute-done.7
  30.3 0.9 collective-permute-done.8
  31.2 2.0 %collective-permute-done.5 = bf16[16,4096]{1,0:T(8,128)(2,1)S(1)} collective-permute-done((bf16[16,4096]{1,0:T(8,128)(2,1)S(1)}, bf16[16,4096]{1,0:T(8,128)(2,1)S(1)}, u32[]{:S(2)}, u32[]{:S(2)}) %collective-permute-start.5) | collective-permute-done | bytes 131104 | tf_op jit(solution)/shard_map/ppermute | solution.py:45
  33.2 1.8 %collective-permute-start.10 = (bf16[48,4096]{1,0:T(8,128)(2,1)S(1)}, bf16[48,4096]{1,0:T(8,128)(2,1)S(1)}, u32[]{:S(2)}, u32[]{:S(2)}) collective-permute-start(bf16[48,4096]{1,0:T(8,128)(2,1)S(1)} %pad_maximum_fusion), channel_id=1, source_target_pairs={{0,8},{1,9},{2,10},{3,11},{4,12},{5,13},{6,14},{7,15},{16,56},{17,... | collective-permute-start | bytes 1179656 | tf_op jit(solution)/shard_map/ppermute | solution.py:45
  35.1 7.5 %label_rows.1 = (bf16[2048,4096]{1,0:T(8,128)(2,1)S(1)}, bf16[128,4096]{1,0:T(8,128)(2,1)S(1)}, bf16[128,4096]{1,0:T(8,128)(2,1)S(1)}) custom-call(s32[256,1]{1,0:T(8,128)S(1)} %broadcast_subtract_fusion.lab_ref, bf16[2048,4096]{1,0:T(8,128)(2,1)} %mem_ref.1), custom_call_target="tpu_custom_call" | custom-call | flops 4294967296 | bytes 16777216 | tf_op jit(solution)/shard_map/label_rows/pallas_call | solution.py:165
  42.6 0.0 copy-start
  42.6 0.5 collective-permute-start.12
  43.3 5.5 %logits.1 = (bf16[256,2048]{1,0:T(8,128)(2,1)S(1)}, f32[8,128]{1,0:T(8,128)S(1)}) custom-call(f32[1]{0:T(128)} %exp.3.scale_ref, s32[1]{0:T(128)} %bitcast.5.shift_ref, bf16[256,4096]{1,0:T(8,128)(2,1)S(1)} %constant_dynamic-update-slice_fusion.5.q_ref, bf16[2048,4096]{1,0:T(8,128)(2,1)S(1)} %get-tuple-element.31.mem_ref, ...), custom_call_target="tpu_custom_call" | custom-call | flops 4294967296 | bytes 16777216 | tf_op jit(solution)/shard_map/logits/pallas_call | solution.py:99
  48.8 1.9 %collective-permute-start.11 = (f32[8,128]{1,0:T(8,128)S(1)}, f32[8,128]{1,0:T(8,128)S(1)}, u32[]{:S(2)}, u32[]{:S(2)}) collective-permute-start(f32[8,128]{1,0:T(8,128)S(1)} %get-tuple-element.32), channel_id=1, source_target_pairs={{0,8},{1,9},{2,10},{3,11},{4,12},{5,13},{6,14},{7,15},{16,56},{17,... | collective-permute-start | bytes 12296 | tf_op jit(solution)/shard_map/ppermute | solution.py:45
  50.7 7.0 %collective-permute-done.12.gr_ref = bf16[128,4096]{1,0:T(8,128)(2,1)S(1)} collective-permute-done((bf16[128,4096]{1,0:T(8,128)(2,1)S(1)}, bf16[128,4096]{1,0:T(8,128)(2,1)S(1)}, u32[]{:S(2)}, u32[]{:S(2)}) %collective-permute-start.12) | collective-permute-done | bytes 1048608 | tf_op jit(solution)/shard_map/ppermute | solution.py:45
  57.6 2.4 %weighted.2 = (f32[128,2048]{1,0:T(8,128)S(1)}, bf16[128,2048]{1,0:T(8,128)(2,1)S(1)}) custom-call(bf16[256,2048]{1,0:T(8,128)(2,1)S(1)} %get-tuple-element.39.e_ref, bf16[2048,4096]{1,0:T(8,128)(2,1)S(1)} %get-tuple-element.31.mem_ref), custom_call_target="tpu_custom_call" | custom-call | flops 2147483648 | bytes 8388608 | tf_op jit(solution)/shard_map/weighted/pallas_call | solution.py:126
  60.0 2.4 %weighted.3 = (f32[128,2048]{1,0:T(8,128)S(1)}, bf16[128,2048]{1,0:T(8,128)(2,1)S(1)}) custom-call(bf16[256,2048]{1,0:T(8,128)(2,1)S(1)} %get-tuple-element.39.e_ref, bf16[2048,4096]{1,0:T(8,128)(2,1)S(1)} %get-tuple-element.31.mem_ref), custom_call_target="tpu_custom_call" | custom-call | flops 2147483648 | bytes 8388608 | tf_op jit(solution)/shard_map/weighted/pallas_call | solution.py:126
  62.4 0.4 collective-permute-start.18
  62.8 1.8 %collective-permute-start.17 = (bf16[128,2048]{1,0:T(8,128)(2,1)S(1)}, bf16[128,2048]{1,0:T(8,128)(2,1)S(1)}, u32[]{:S(2)}, u32[]{:S(2)}) collective-permute-start(bf16[128,2048]{1,0:T(8,128)(2,1)S(1)} %get-tuple-element.41), channel_id=1, source_target_pairs={{0,8},{1,9},{2,10},{3,11},{4,12},{5,13},{6,14},{7,15},{16,56},{17,... | collective-permute-start | bytes 1572872 | tf_op jit(solution)/shard_map/ppermute | solution.py:45
  64.6 0.1 collective-permute-start.13
  64.7 0.1 pad_add_fusion.2.place_ref
  64.7 3.1 %collective-permute-start.14 = (f32[2,8,128]{2,1,0:T(8,128)S(1)}, f32[2,8,128]{2,1,0:T(8,128)S(1)}, u32[]{:S(2)}, u32[]{:S(2)}) collective-permute-start(f32[2,8,128]{2,1,0:T(8,128)S(1)} %get-tuple-element.69), channel_id=1, source_target_pairs={{0,7},{1,0},{2,1},{3,2},{4,3},{5,4},{6,5},{7,6},{16,23},{17,16},{1... | collective-permute-start | bytes 24584 | tf_op jit(solution)/shard_map/ppermute | solution.py:45
  67.9 1.6 %collective-permute-done.13 = f32[2,8,128]{2,1,0:T(8,128)S(1)} collective-permute-done((f32[2,8,128]{2,1,0:T(8,128)S(1)}, f32[2,8,128]{2,1,0:T(8,128)S(1)}, u32[]{:S(2)}, u32[]{:S(2)}) %collective-permute-start.13) | collective-permute-done | bytes 8224 | tf_op jit(solution)/shard_map/ppermute | solution.py:45
  69.5 0.0 collective-permute-start.16
  69.5 0.0 collective-permute-done.14
  69.5 3.8 %collective-permute-start.15 = (f32[3,2,8,128]{3,2,1,0:T(8,128)S(1)}, f32[3,2,8,128]{3,2,1,0:T(8,128)S(1)}, u32[]{:S(2)}, u32[]{:S(2)}) collective-permute-start(f32[3,2,8,128]{3,2,1,0:T(8,128)S(1)} %pad_maximum_fusion.1.mid_ref), channel_id=1, source_target_pairs={{0,3},{1,4},{2,5},{3,6},{4,7},{5,0},{6,1},{7,2},{16,19},{17,20},{1... | collective-permute-start | bytes 73736 | tf_op jit(solution)/shard_map/ppermute | solution.py:45
  73.3 1.7 %collective-permute-done.16.down_ref = f32[2,2,8,128]{3,2,1,0:T(8,128)S(1)} collective-permute-done((f32[2,2,8,128]{3,2,1,0:T(8,128)S(1)}, f32[2,2,8,128]{3,2,1,0:T(8,128)S(1)}, u32[]{:S(2)}, u32[]{:S(2)}) %collective-permute-start.16) | collective-permute-done | bytes 16416 | tf_op jit(solution)/shard_map/ppermute | solution.py:45
  75.0 1.9 %collective-permute-done.15.up_ref = f32[3,2,8,128]{3,2,1,0:T(8,128)S(1)} collective-permute-done((f32[3,2,8,128]{3,2,1,0:T(8,128)S(1)}, f32[3,2,8,128]{3,2,1,0:T(8,128)S(1)}, u32[]{:S(2)}, u32[]{:S(2)}) %collective-permute-start.15) | collective-permute-done | bytes 24608 | tf_op jit(solution)/shard_map/ppermute | solution.py:45
  76.9 0.0 collective-permute-done.18.rb_ref
  76.9 0.4 collective-permute-done.17.ra_ref
  77.3 1.5 %mix.1 = (bf16[32,4096]{1,0:T(8,128)(2,1)S(1)}, bf16[32,4096]{1,0:T(8,128)(2,1)S(1)}, bf16[16,2048]{1,0:T(8,128)(2,1)S(1)}, bf16[16,2048]{1,0:T(8,128)(2,1)S(1)}...) custom-call(s32[2]{0:T(128)S(1)} %pad_add_fusion.2.place_ref, ...), custom_call_target="tpu_custom_call" | custom-call | tf_op jit(solution)/shard_map/mix/pallas_call | solution.py:247
  78.8 0.2 collective-permute-start.19
  79.0 3.1 %collective-permute-start.20 = (bf16[32,4096]{1,0:T(8,128)(2,1)S(1)}, bf16[32,4096]{1,0:T(8,128)(2,1)S(1)}, u32[]{:S(2)}, u32[]{:S(2)}) collective-permute-start(bf16[32,4096]{1,0:T(8,128)(2,1)S(1)} %get-tuple-element.47), channel_id=1, source_target_pairs={{0,7},{1,0},{2,1},{3,2},{4,3},{5,4},{6,5},{7,6},{16,23},{17,16},{1... | collective-permute-start | bytes 786440 | tf_op jit(solution)/shard_map/ppermute | solution.py:45
  82.1 0.9 collective-permute-start.21
  83.0 3.3 %collective-permute-start.22 = (bf16[16,2048]{1,0:T(8,128)(2,1)S(1)}, bf16[16,2048]{1,0:T(8,128)(2,1)S(1)}, u32[]{:S(2)}, u32[]{:S(2)}) collective-permute-start(bf16[16,2048]{1,0:T(8,128)(2,1)S(1)} %get-tuple-element.49), channel_id=1, source_target_pairs={{0,6},{1,7},{2,0},{3,1},{4,2},{5,3},{6,4},{7,5},{16,22},{17,23},{1... | collective-permute-start | bytes 196616 | tf_op jit(solution)/shard_map/ppermute | solution.py:45
  86.3 0.0 collective-permute-start.23
  86.3 3.6 %collective-permute-done.23 = f32[8,128]{1,0:T(8,128)S(1)} collective-permute-done((f32[8,128]{1,0:T(8,128)S(1)}, f32[8,128]{1,0:T(8,128)S(1)}, u32[]{:S(2)}, u32[]{:S(2)}) %collective-permute-start.23) | collective-permute-done | bytes 4128 | tf_op jit(solution)/shard_map/ppermute | solution.py:45
  89.9 0.7 collective-permute-done.21
  90.6 0.3 collective-permute-done.22
  90.9 0.0 collective-permute-done.20
  91.0 2.5 %collective-permute-start.24 = (bf16[16,4096]{1,0:T(8,128)(2,1)S(1)}, bf16[16,4096]{1,0:T(8,128)(2,1)S(1)}, u32[]{:S(2)}, u32[]{:S(2)}) collective-permute-start(bf16[16,4096]{1,0:T(8,128)(2,1)S(1)} %add_convert_fusion.1), channel_id=1, source_target_pairs={{0,2},{1,3},{2,4},{3,5},{4,6},{5,7},{6,0},{7,1},{16,18},{17,19},{1... | collective-permute-start | bytes 393224 | tf_op jit(solution)/shard_map/ppermute | solution.py:45
  93.5 1.8 %collective-permute-start.25 = (bf16[16,4096]{1,0:T(8,128)(2,1)S(1)}, bf16[16,4096]{1,0:T(8,128)(2,1)S(1)}, u32[]{:S(2)}, u32[]{:S(2)}) collective-permute-start(bf16[16,4096]{1,0:T(8,128)(2,1)S(1)} %add_convert_fusion), channel_id=1, source_target_pairs={{0,6},{1,7},{2,0},{3,1},{4,2},{5,3},{6,4},{7,5},{16,22},{17,23},{1... | collective-permute-start | bytes 393224 | tf_op jit(solution)/shard_map/ppermute | solution.py:45
  95.3 0.0 collective-permute-start.26
  95.3 1.2 %collective-permute-done.26 = f32[8,128]{1,0:T(8,128)S(1)} collective-permute-done((f32[8,128]{1,0:T(8,128)S(1)}, f32[8,128]{1,0:T(8,128)S(1)}, u32[]{:S(2)}, u32[]{:S(2)}) %collective-permute-start.26) | collective-permute-done | bytes 4128 | tf_op jit(solution)/shard_map/ppermute | solution.py:45
  96.5 0.7 collective-permute-start.27
  97.2 2.9 %collective-permute-done.27 = f32[8,128]{1,0:T(8,128)S(1)} collective-permute-done((f32[8,128]{1,0:T(8,128)S(1)}, f32[8,128]{1,0:T(8,128)S(1)}, u32[]{:S(2)}, u32[]{:S(2)}) %collective-permute-start.27) | collective-permute-done | bytes 4128 | tf_op jit(solution)/shard_map/ppermute | solution.py:45
  100.1 1.2 %collective-permute-start.28 = (f32[8,128]{1,0:T(8,128)S(1)}, f32[8,128]{1,0:T(8,128)S(1)}, u32[]{:S(2)}, u32[]{:S(2)}) collective-permute-start(f32[8,128]{1,0:T(8,128)S(1)} %add.68), channel_id=1, source_target_pairs={{0,128},{1,129},{2,130},{3,131},{4,132},{5,133},{6,134},{7,135},{1... | collective-permute-start | bytes 12296 | tf_op jit(solution)/shard_map/ppermute | solution.py:45
  101.3 0.1 dynamic-slice_multiply_fusion
  101.4 3.8 %collective-permute-done.28 = f32[8,128]{1,0:T(8,128)S(1)} collective-permute-done((f32[8,128]{1,0:T(8,128)S(1)}, f32[8,128]{1,0:T(8,128)S(1)}, u32[]{:S(2)}, u32[]{:S(2)}) %collective-permute-start.28) | collective-permute-done | bytes 4128 | tf_op jit(solution)/shard_map/ppermute | solution.py:45
  105.2 0.5 slice.37
  106.4 0.0 collective-permute-done.24
  106.4 0.7 multiply_convert_fusion
  (40 shorter events, 0.4 us)
Async XLA Ops:
  2.3 11.3 %collective-permute-start = (f32[2,128]{1,0:T(2,128)S(1)}, f32[2,128]{1,0:T(2,128)S(1)}, u32[]{:S(2)}, u32[]{:S(2)}) collective-permute-start(f32[2,128]{1,0:T(2,128)S(1)} %pad_maximum_fusion.4), channel_id=1, source_target_pairs={{0,8},{1,9},{2,10},{3,11},{4,12},{5,13},{6,14},{7,15},{16,56},{17,... | collective-permute-start | bytes 3080 | tf_op jit(solution)/shard_map/ppermute | solution.py:45
  2.9 25.4 %collective-permute-start.3 = (bf16[16,4096]{1,0:T(8,128)(2,1)}, bf16[16,4096]{1,0:T(8,128)(2,1)S(1)}, u32[]{:S(2)}, u32[]{:S(2)}) collective-permute-start(bf16[16,4096]{1,0:T(8,128)(2,1)} %param.6), channel_id=1, source_target_pairs={{0,7},{1,0},{2,1},{3,2},{4,3},{5,4},{6,5},{7,6},{16,23},{17,16},{1... | collective-permute-start | bytes 393224 | tf_op jit(solution)/shard_map/ppermute | solution.py:45
  8.7 15.3 %collective-permute-start.2 = (bf16[16,4096]{1,0:T(8,128)(2,1)}, bf16[16,4096]{1,0:T(8,128)(2,1)S(1)}, u32[]{:S(2)}, u32[]{:S(2)}) collective-permute-start(bf16[16,4096]{1,0:T(8,128)(2,1)} %param.6), channel_id=1, source_target_pairs={{0,1},{1,2},{2,3},{3,4},{4,5},{5,6},{6,7},{7,0},{16,17},{17,18},{1... | collective-permute-start | bytes 393224 | tf_op jit(solution)/shard_map/ppermute | solution.py:45
  8.7 11.0 %collective-permute-start.1 = (bf16[16,4096]{1,0:T(8,128)(2,1)}, bf16[16,4096]{1,0:T(8,128)(2,1)S(1)}, u32[]{:S(2)}, u32[]{:S(2)}) collective-permute-start(bf16[16,4096]{1,0:T(8,128)(2,1)} %param.6), channel_id=1, source_target_pairs={{0,2},{1,3},{2,4},{3,5},{4,6},{5,7},{6,0},{7,1},{16,18},{17,19},{1... | collective-permute-start | bytes 393224 | tf_op jit(solution)/shard_map/ppermute | solution.py:45
  8.7 11.0 %collective-permute-start.4 = (bf16[16,4096]{1,0:T(8,128)(2,1)}, bf16[16,4096]{1,0:T(8,128)(2,1)S(1)}, u32[]{:S(2)}, u32[]{:S(2)}) collective-permute-start(bf16[16,4096]{1,0:T(8,128)(2,1)} %param.6), channel_id=1, source_target_pairs={{0,6},{1,7},{2,0},{3,1},{4,2},{5,3},{6,4},{7,5},{16,22},{17,23},{1... | collective-permute-start | bytes 393224 | tf_op jit(solution)/shard_map/ppermute | solution.py:45
  19.7 10.6 %collective-permute-start.6 = (bf16[16,2048]{1,0:T(8,128)(2,1)S(1)}, bf16[16,2048]{1,0:T(8,128)(2,1)S(1)}, u32[]{:S(2)}, u32[]{:S(2)}) collective-permute-start(bf16[16,2048]{1,0:T(8,128)(2,1)S(1)} %slice.38), channel_id=1, source_target_pairs={{0,2},{1,3},{2,4},{3,5},{4,6},{5,7},{6,0},{7,1},{16,18},{17,19},{1... | collective-permute-start | bytes 196616 | tf_op jit(solution)/shard_map/ppermute | solution.py:45
  19.8 10.5 %collective-permute-start.7 = (bf16[16,2048]{1,0:T(8,128)(2,1)S(1)}, bf16[16,2048]{1,0:T(8,128)(2,1)S(1)}, u32[]{:S(2)}, u32[]{:S(2)}) collective-permute-start(bf16[16,2048]{1,0:T(8,128)(2,1)S(1)} %slice.39), channel_id=1, source_target_pairs={{0,6},{1,7},{2,0},{3,1},{4,2},{5,3},{6,4},{7,5},{16,22},{17,23},{1... | collective-permute-start | bytes 196616 | tf_op jit(solution)/shard_map/ppermute | solution.py:45
  25.0 6.3 %collective-permute-start.8 = (bf16[16,4096]{1,0:T(8,128)(2,1)S(1)}, bf16[16,4096]{1,0:T(8,128)(2,1)S(1)}, u32[]{:S(2)}, u32[]{:S(2)}) collective-permute-start(bf16[16,4096]{1,0:T(8,128)(2,1)S(1)} %collective-permute-done.1), channel_id=1, source_target_pairs={{0,1},{1,2},{2,3},{3,4},{4,5},{5,6},{6,7},{7,0},{16,17},{17,18},{1... | collective-permute-start | bytes 393224 | tf_op jit(solution)/shard_map/ppermute | solution.py:45
  28.2 5.0 %collective-permute-start.5 = (bf16[16,4096]{1,0:T(8,128)(2,1)S(1)}, bf16[16,4096]{1,0:T(8,128)(2,1)S(1)}, u32[]{:S(2)}, u32[]{:S(2)}) collective-permute-start(bf16[16,4096]{1,0:T(8,128)(2,1)S(1)} %collective-permute-done.4), channel_id=1, source_target_pairs={{0,7},{1,0},{2,1},{3,2},{4,3},{5,4},{6,5},{7,6},{16,23},{17,16},{1... | collective-permute-start | bytes 393224 | tf_op jit(solution)/shard_map/ppermute | solution.py:45
  28.3 14.8 %collective-permute-start.9 = (bf16[80,4096]{1,0:T(8,128)(2,1)S(1)}, bf16[80,4096]{1,0:T(8,128)(2,1)S(1)}, u32[]{:S(2)}, u32[]{:S(2)}) collective-permute-start(bf16[80,4096]{1,0:T(8,128)(2,1)S(1)} %get-tuple-element.58), channel_id=1, source_target_pairs={{0,8},{1,9},{2,10},{3,11},{4,12},{5,13},{6,14},{7,15},{16,56},{17,... | collective-permute-start | bytes 1966088 | tf_op jit(solution)/shard_map/ppermute | solution.py:45
  33.2 10.0 %collective-permute-start.10 = (bf16[48,4096]{1,0:T(8,128)(2,1)S(1)}, bf16[48,4096]{1,0:T(8,128)(2,1)S(1)}, u32[]{:S(2)}, u32[]{:S(2)}) collective-permute-start(bf16[48,4096]{1,0:T(8,128)(2,1)S(1)} %pad_maximum_fusion), channel_id=1, source_target_pairs={{0,8},{1,9},{2,10},{3,11},{4,12},{5,13},{6,14},{7,15},{16,56},{17,... | collective-permute-start | bytes 1179656 | tf_op jit(solution)/shard_map/ppermute | solution.py:45
  42.6 0.7 copy-start
  42.6 15.1 %collective-permute-start.12 = (bf16[128,4096]{1,0:T(8,128)(2,1)S(1)}, bf16[128,4096]{1,0:T(8,128)(2,1)S(1)}, u32[]{:S(2)}, u32[]{:S(2)}) collective-permute-start(bf16[128,4096]{1,0:T(8,128)(2,1)S(1)} %get-tuple-element.34), channel_id=1, source_target_pairs={{0,8},{1,9},{2,10},{3,11},{4,12},{5,13},{6,14},{7,15},{16,56},{17,... | collective-permute-start | bytes 3145736 | tf_op jit(solution)/shard_map/ppermute | solution.py:45
  48.8 11.3 %collective-permute-start.11 = (f32[8,128]{1,0:T(8,128)S(1)}, f32[8,128]{1,0:T(8,128)S(1)}, u32[]{:S(2)}, u32[]{:S(2)}) collective-permute-start(f32[8,128]{1,0:T(8,128)S(1)} %get-tuple-element.32), channel_id=1, source_target_pairs={{0,8},{1,9},{2,10},{3,11},{4,12},{5,13},{6,14},{7,15},{16,56},{17,... | collective-permute-start | bytes 12296 | tf_op jit(solution)/shard_map/ppermute | solution.py:45
  62.4 14.5 %collective-permute-start.18 = (bf16[128,2048]{1,0:T(8,128)(2,1)S(1)}, bf16[128,2048]{1,0:T(8,128)(2,1)S(1)}, u32[]{:S(2)}, u32[]{:S(2)}) collective-permute-start(bf16[128,2048]{1,0:T(8,128)(2,1)S(1)} %get-tuple-element.42), channel_id=1, source_target_pairs={{0,8},{1,9},{2,10},{3,11},{4,12},{5,13},{6,14},{7,15},{16,56},{17,... | collective-permute-start | bytes 1572872 | tf_op jit(solution)/shard_map/ppermute | solution.py:45
  62.8 14.5 %collective-permute-start.17 = (bf16[128,2048]{1,0:T(8,128)(2,1)S(1)}, bf16[128,2048]{1,0:T(8,128)(2,1)S(1)}, u32[]{:S(2)}, u32[]{:S(2)}) collective-permute-start(bf16[128,2048]{1,0:T(8,128)(2,1)S(1)} %get-tuple-element.41), channel_id=1, source_target_pairs={{0,8},{1,9},{2,10},{3,11},{4,12},{5,13},{6,14},{7,15},{16,56},{17,... | collective-permute-start | bytes 1572872 | tf_op jit(solution)/shard_map/ppermute | solution.py:45
  64.6 4.9 %collective-permute-start.13 = (f32[2,8,128]{2,1,0:T(8,128)S(1)}, f32[2,8,128]{2,1,0:T(8,128)S(1)}, u32[]{:S(2)}, u32[]{:S(2)}) collective-permute-start(f32[2,8,128]{2,1,0:T(8,128)S(1)} %get-tuple-element.69), channel_id=1, source_target_pairs={{0,1},{1,2},{2,3},{3,4},{4,5},{5,6},{6,7},{7,0},{16,17},{17,18},{1... | collective-permute-start | bytes 24584 | tf_op jit(solution)/shard_map/ppermute | solution.py:45
  64.7 4.7 %collective-permute-start.14 = (f32[2,8,128]{2,1,0:T(8,128)S(1)}, f32[2,8,128]{2,1,0:T(8,128)S(1)}, u32[]{:S(2)}, u32[]{:S(2)}) collective-permute-start(f32[2,8,128]{2,1,0:T(8,128)S(1)} %get-tuple-element.69), channel_id=1, source_target_pairs={{0,7},{1,0},{2,1},{3,2},{4,3},{5,4},{6,5},{7,6},{16,23},{17,16},{1... | collective-permute-start | bytes 24584 | tf_op jit(solution)/shard_map/ppermute | solution.py:45
  69.5 5.5 %collective-permute-start.16 = (f32[2,2,8,128]{3,2,1,0:T(8,128)S(1)}, f32[2,2,8,128]{3,2,1,0:T(8,128)S(1)}, u32[]{:S(2)}, u32[]{:S(2)}) collective-permute-start(f32[2,2,8,128]{3,2,1,0:T(8,128)S(1)} %pad_maximum_fusion.2), channel_id=1, source_target_pairs={{0,5},{1,6},{2,7},{3,0},{4,1},{5,2},{6,3},{7,4},{16,21},{17,22},{1... | collective-permute-start | bytes 49160 | tf_op jit(solution)/shard_map/ppermute | solution.py:45
  69.5 7.4 %collective-permute-start.15 = (f32[3,2,8,128]{3,2,1,0:T(8,128)S(1)}, f32[3,2,8,128]{3,2,1,0:T(8,128)S(1)}, u32[]{:S(2)}, u32[]{:S(2)}) collective-permute-start(f32[3,2,8,128]{3,2,1,0:T(8,128)S(1)} %pad_maximum_fusion.1.mid_ref), channel_id=1, source_target_pairs={{0,3},{1,4},{2,5},{3,6},{4,7},{5,0},{6,1},{7,2},{16,19},{17,20},{1... | collective-permute-start | bytes 73736 | tf_op jit(solution)/shard_map/ppermute | solution.py:45
  77.3 24.0 %copy-start.1 = (f32[256]{0:T(256)S(1)}, f32[256]{0:T(256)}, u32[]{:S(2)}) copy-start(f32[256]{0:T(256)} %param.11) | copy-start | bytes 3076
  78.8 12.1 %collective-permute-start.19 = (bf16[32,4096]{1,0:T(8,128)(2,1)S(1)}, bf16[32,4096]{1,0:T(8,128)(2,1)S(1)}, u32[]{:S(2)}, u32[]{:S(2)}) collective-permute-start(bf16[32,4096]{1,0:T(8,128)(2,1)S(1)} %get-tuple-element.46), channel_id=1, source_target_pairs={{0,1},{1,2},{2,3},{3,4},{4,5},{5,6},{6,7},{7,0},{16,17},{17,18},{1... | collective-permute-start | bytes 786440 | tf_op jit(solution)/shard_map/ppermute | solution.py:45
  79.0 11.9 %collective-permute-start.20 = (bf16[32,4096]{1,0:T(8,128)(2,1)S(1)}, bf16[32,4096]{1,0:T(8,128)(2,1)S(1)}, u32[]{:S(2)}, u32[]{:S(2)}) collective-permute-start(bf16[32,4096]{1,0:T(8,128)(2,1)S(1)} %get-tuple-element.47), channel_id=1, source_target_pairs={{0,7},{1,0},{2,1},{3,2},{4,3},{5,4},{6,5},{7,6},{16,23},{17,16},{1... | collective-permute-start | bytes 786440 | tf_op jit(solution)/shard_map/ppermute | solution.py:45
  82.1 8.5 %collective-permute-start.21 = (bf16[16,2048]{1,0:T(8,128)(2,1)S(1)}, bf16[16,2048]{1,0:T(8,128)(2,1)S(1)}, u32[]{:S(2)}, u32[]{:S(2)}) collective-permute-start(bf16[16,2048]{1,0:T(8,128)(2,1)S(1)} %get-tuple-element.48), channel_id=1, source_target_pairs={{0,2},{1,3},{2,4},{3,5},{4,6},{5,7},{6,0},{7,1},{16,18},{17,19},{1... | collective-permute-start | bytes 196616 | tf_op jit(solution)/shard_map/ppermute | solution.py:45
  83.0 7.9 %collective-permute-start.22 = (bf16[16,2048]{1,0:T(8,128)(2,1)S(1)}, bf16[16,2048]{1,0:T(8,128)(2,1)S(1)}, u32[]{:S(2)}, u32[]{:S(2)}) collective-permute-start(bf16[16,2048]{1,0:T(8,128)(2,1)S(1)} %get-tuple-element.49), channel_id=1, source_target_pairs={{0,6},{1,7},{2,0},{3,1},{4,2},{5,3},{6,4},{7,5},{16,22},{17,23},{1... | collective-permute-start | bytes 196616 | tf_op jit(solution)/shard_map/ppermute | solution.py:45
  86.3 3.6 %collective-permute-start.23 = (f32[8,128]{1,0:T(8,128)S(1)}, f32[8,128]{1,0:T(8,128)S(1)}, u32[]{:S(2)}, u32[]{:S(2)}) collective-permute-start(f32[8,128]{1,0:T(8,128)S(1)} %get-tuple-element.50), channel_id=1, source_target_pairs={{0,40},{1,41},{2,42},{3,43},{4,44},{5,45},{6,46},{7,47},{16,24},{1... | collective-permute-start | bytes 12296 | tf_op jit(solution)/shard_map/ppermute | solution.py:45
  91.0 15.4 %collective-permute-start.24 = (bf16[16,4096]{1,0:T(8,128)(2,1)S(1)}, bf16[16,4096]{1,0:T(8,128)(2,1)S(1)}, u32[]{:S(2)}, u32[]{:S(2)}) collective-permute-start(bf16[16,4096]{1,0:T(8,128)(2,1)S(1)} %add_convert_fusion.1), channel_id=1, source_target_pairs={{0,2},{1,3},{2,4},{3,5},{4,6},{5,7},{6,0},{7,1},{16,18},{17,19},{1... | collective-permute-start | bytes 393224 | tf_op jit(solution)/shard_map/ppermute | solution.py:45
  93.5 12.9 %collective-permute-start.25 = (bf16[16,4096]{1,0:T(8,128)(2,1)S(1)}, bf16[16,4096]{1,0:T(8,128)(2,1)S(1)}, u32[]{:S(2)}, u32[]{:S(2)}) collective-permute-start(bf16[16,4096]{1,0:T(8,128)(2,1)S(1)} %add_convert_fusion), channel_id=1, source_target_pairs={{0,6},{1,7},{2,0},{3,1},{4,2},{5,3},{6,4},{7,5},{16,22},{17,23},{1... | collective-permute-start | bytes 393224 | tf_op jit(solution)/shard_map/ppermute | solution.py:45
  95.3 1.2 %collective-permute-start.26 = (f32[8,128]{1,0:T(8,128)S(1)}, f32[8,128]{1,0:T(8,128)S(1)}, u32[]{:S(2)}, u32[]{:S(2)}) collective-permute-start(f32[8,128]{1,0:T(8,128)S(1)} %add.58), channel_id=1, source_target_pairs={{0,16},{1,17},{2,18},{3,19},{4,20},{5,21},{6,22},{7,23},{16,0},{17... | collective-permute-start | bytes 12296 | tf_op jit(solution)/shard_map/ppermute | solution.py:45
  96.5 3.6 %collective-permute-start.27 = (f32[8,128]{1,0:T(8,128)S(1)}, f32[8,128]{1,0:T(8,128)S(1)}, u32[]{:S(2)}, u32[]{:S(2)}) collective-permute-start(f32[8,128]{1,0:T(8,128)S(1)} %add.67), channel_id=1, source_target_pairs={{0,64},{1,65},{2,66},{3,67},{4,68},{5,69},{6,70},{7,71},{16,80},{1... | collective-permute-start | bytes 12296 | tf_op jit(solution)/shard_map/ppermute | solution.py:45
  100.1 5.1 %collective-permute-start.28 = (f32[8,128]{1,0:T(8,128)S(1)}, f32[8,128]{1,0:T(8,128)S(1)}, u32[]{:S(2)}, u32[]{:S(2)}) collective-permute-start(f32[8,128]{1,0:T(8,128)S(1)} %add.68), channel_id=1, source_target_pairs={{0,128},{1,129},{2,130},{3,131},{4,132},{5,133},{6,134},{7,135},{1... | collective-permute-start | bytes 12296 | tf_op jit(solution)/shard_map/ppermute | solution.py:45

commit v3 on v2

v3 whole, which is shorter than its diff:
```python
import jax
import jax.numpy as jnp
from jax import lax
from jax.experimental import pallas as pl
from jax.experimental.pallas import tpu as pltpu
from jax.sharding import PartitionSpec as P

AXES = ("dp", "mem")
NEG = -1e30
BLK = 512
COLS = 1024


def table(move):
    pairs = []
    for y in range(4):
        for x in range(4):
            for c in range(2):
                for z in range(8):
                    index = lambda y, x, c, z: (((y * 2 + x // 2) * 2 + c) * 2 + x % 2) * 8 + z
                    pairs.append((index(y, x, c, z), index(*move(y, x, c, z))))
    return pairs


def along_z(k):
    return table(lambda y, x, c, z: (y, x, c, (z + k) % 8))


def partner_of(x, c):
    if c == 0:
        return x ^ 1
    return (x + 1) % 4 if x % 2 else (x - 1) % 4


PARTNER = table(lambda y, x, c, z: (y, partner_of(x, c), c, z))
CORE = table(lambda y, x, c, z: (y, x, 1 - c, z))
CROSS = table(lambda y, x, c, z: (y, partner_of(x, 1 - c), c, z))
Y1 = table(lambda y, x, c, z: (y ^ 1, x, c, z))
Y2 = table(lambda y, x, c, z: (y ^ 2, x, c, z))


def send(x, pairs):
    return lax.ppermute(x, AXES, pairs)


def both(up, down, k):
    down = send(down, along_z(-k))
    return send(up, along_z(k)), down


def fill(q_scr, first, own, two, up, down):
    depth = q_scr.shape[1]
    half = depth // 2
    near, next_, last = slice(0, depth), slice(depth, 2 * depth), slice(2 * depth, 2 * depth + half)
    places = (down, next_), (up, near), (own, near), (down, near), (up, next_), (two, next_), None, (two, near)
    for k, place in enumerate(places):
        if place is not None:
            q_scr[first + 16 * k:first + 16 * k + 16, :] = place[0][:, place[1]]
    q_scr[first + 96:first + 112, :half] = up[:, last]
    q_scr[first + 96:first + 112, half:] = down[:, last]


def pack_kernel(own_ref, up3_ref, down3_ref, lab_ref, cot_ref, up_ref, down_ref, two_ref, sems):
    f32, bf16 = jnp.float32, jnp.bfloat16
    depth = up3_ref.shape[1]
    half = depth // 2
    copies = [
        pltpu.make_async_copy(own_ref, ref.at[:, pl.ds(0, depth)], sems.at[k]) for k, ref in enumerate((up_ref, down_ref))
    ]
    for copy in copies:
        copy.start()
    up_ref[:, depth:2 * depth] = down3_ref[...]
    up_ref[:, 2 * depth:] = up3_ref[:, :half]
    down_ref[:, depth:2 * depth] = up3_ref[...]
    down_ref[:, 2 * depth:] = down3_ref[:, half:]
    two_ref[:, :depth] = up3_ref[...]
    two_ref[:, depth:2 * depth] = down3_ref[...]
    label = lab_ref[...]
    high = lax.shift_right_logical(label, 8)
    rest = cot_ref[...]
    terms = [high.astype(f32), (label - high * 256).astype(f32)]
    for _ in range(3):
        term = rest.astype(bf16).astype(f32)
        terms.append(term)
        rest = rest - term
    row = lax.broadcasted_iota(jnp.int32, (16, 128), 0)
    note = jnp.zeros((16, 128), f32)
    for k, term in enumerate(terms):
        note = jnp.where(row == k, term, note)
    two_ref[:, 2 * depth:] = note.astype(bf16)
    for copy in copies:
        copy.wait()


def pack_call(own, up3, down3, lab, cot):
    rows, depth = own.shape
    wide = 2 * depth + depth // 2
    return pl.pallas_call(
        pack_kernel,
        in_specs=[hbm()] + [vmem()] * 4,
        out_specs=[vmem()] * 3,
        out_shape=[jax.ShapeDtypeStruct((rows, k), jnp.bfloat16) for k in (wide, wide, 2 * depth + 128)],
        scratch_shapes=[pltpu.SemaphoreType.DMA((2,))],
        compiler_params=params(4),
        name="pack",
    )(pltpu.with_memory_space_constraint(own, pltpu.HBM), up3, down3, lab, cot)


def logits_kernel(scale_ref, shift_ref, own, two, up, down, own_x, two_x, up_x, down_x,
                  mem_ref, lab_ref, valid_ref, e_ref, stat_ref, q_scr, l_scr):
    fill(q_scr, 0, own, two, up, down)
    fill(q_scr, 128, own_x, two_x, up_x, down_x)
    rows, n = l_scr.shape
    scale = scale_ref[0]
    top = jnp.full((rows, 1), NEG, jnp.float32)
    picked = jnp.zeros((rows, 1), jnp.float32)
    for i in range(0, n, BLK):
        raw = lax.dot_general(
            q_scr[...], mem_ref[i:i + BLK, :], (((1,), (1,)), ((), ())), preferred_element_type=jnp.float32
        )
        logit = raw * scale
        column = lax.broadcasted_iota(jnp.int32, logit.shape, 1) + i
        hit = lab_ref[...] == column
        kept = jnp.where(jnp.logical_and(valid_ref[:, i:i + BLK] > 0, jnp.logical_not(hit)), logit, NEG)
        l_scr[:, i:i + BLK] = kept
        top = jnp.maximum(top, jnp.max(kept, axis=1, keepdims=True))
        picked = picked + jnp.sum(jnp.where(hit, logit, 0.0), axis=1, keepdims=True)
    half = rows // 2
    step = 32
    lane = lax.broadcasted_iota(jnp.int32, (step, 128), 1)
    tiles = []
    for r in range(0, rows, step):
        m = top[r:r + step]
        val = l_scr[r:r + step, :]
        e = jnp.exp(val - m)
        e_ref[r:r + step, :] = e.astype(jnp.bfloat16)
        s = jnp.sum(e, axis=1, keepdims=True)
        t = jnp.sum(e * val, axis=1, keepdims=True)
        tiles.append(jnp.where(lane == 0, m, jnp.where(lane == 1, s, jnp.where(lane == 2, t, picked[r:r + step]))))
    full = jnp.concatenate(tiles, axis=0)
    own = pltpu.roll(full[:half].T, shift_ref[0], 1)
    other = pltpu.roll(full[half:].T, shift_ref[0], 1)
    for k in range(4):
        stat_ref[2 * k:2 * k + 1, :] = own[k:k + 1, :]
        stat_ref[2 * k + 1:2 * k + 2, :] = other[k:k + 1, :]


def vmem():
    return pl.BlockSpec(memory_space=pltpu.VMEM)


def smem():
    return pl.BlockSpec(memory_space=pltpu.SMEM)


def params(mib):
    return pltpu.CompilerParams(vmem_limit_bytes=mib * 1024 * 1024)


def logits_call(scale, shift, blocks, memory, lab, valid):
    n, depth = memory.shape
    rows = lab.shape[0]
    return pl.pallas_call(
        logits_kernel,
        in_specs=[smem(), smem()] + [vmem()] * (len(blocks) + 3),
        out_specs=[vmem(), vmem()],
        out_shape=[
            jax.ShapeDtypeStruct((rows, n), jnp.bfloat16),
            jax.ShapeDtypeStruct((8, 128), jnp.float32),
        ],
        scratch_shapes=[
            pltpu.VMEM((rows, depth), jnp.bfloat16),
            pltpu.VMEM((rows, n), jnp.float32),
        ],
        compiler_params=params(8),
        cost_estimate=pl.CostEstimate(
            flops=2 * rows * n * depth, bytes_accessed=2 * n * depth, transcendentals=rows * n
        ),
        name="logits",
    )(scale, shift, *blocks, memory, lab, valid)


FIRST = (3, 0, 6, 1, 4)
SECOND = (2, 5, 7)


def weighted_kernel(e_ref, mem_ref, g_ref, own_ref, first_ref, second_ref):
    second_ref[16 * len(SECOND):, :] = g_ref[...]
    for c in range(0, mem_ref.shape[1], COLS):
        at = slice(c, c + COLS)
        out = jnp.dot(e_ref[...], mem_ref[:, at], preferred_element_type=jnp.float32)
        spread(out, at, own_ref, first_ref, second_ref)


def spread(out, at, own_ref, first_ref, second_ref):
    own_ref[:, at] = out[:128].astype(own_ref.dtype)
    for ref, order in ((first_ref, FIRST), (second_ref, SECOND)):
        for i, k in enumerate(order):
            ref[16 * i:16 * i + 16, at] = out[128 + 16 * k:144 + 16 * k].astype(ref.dtype)


def weighted_call(e, memory, g):
    rows, n = e.shape
    depth = memory.shape[1]
    return pl.pallas_call(
        weighted_kernel,
        in_specs=[vmem()] * 3,
        out_specs=[vmem()] * 3,
        out_shape=[
            jax.ShapeDtypeStruct((128, depth), jnp.float32),
            jax.ShapeDtypeStruct((16 * len(FIRST), depth), jnp.bfloat16),
            jax.ShapeDtypeStruct((32 * len(SECOND), depth), jnp.bfloat16),
        ],
        compiler_params=params(8),
        cost_estimate=pl.CostEstimate(flops=2 * rows * n * depth, bytes_accessed=2 * n * depth, transcendentals=0),
        name="weighted",
    )(e, memory, g)


def labels_kernel(lab_ref, mem_ref, copy_ref, own_ref, first_ref, second_ref, hit_scr, sems):
    rows, n = hit_scr.shape
    pieces = mem_ref.shape[1] // COLS

    def piece(k):
        at = pl.ds(k * COLS, COLS)
        return pltpu.make_async_copy(mem_ref.at[:, at], copy_ref.at[:, at], sems.at[k])

    for k in range(pieces):
        piece(k).start()
    for i in range(0, n, BLK):
        column = lax.broadcasted_iota(jnp.int32, (rows, BLK), 1) + i
        hit_scr[:, i:i + BLK] = jnp.where(lab_ref[...] == column, 1.0, 0.0).astype(jnp.bfloat16)
    for k in range(pieces):
        piece(k).wait()
        at = slice(k * COLS, k * COLS + COLS)
        out = jnp.dot(hit_scr[...], copy_ref[:, at], preferred_element_type=jnp.float32)
        spread(out, at, own_ref, first_ref, second_ref)


def hbm():
    return pl.BlockSpec(memory_space=pltpu.HBM)


def labels_call(lab, memory):
    rows = lab.shape[0]
    n, depth = memory.shape
    return pl.pallas_call(
        labels_kernel,
        in_specs=[vmem(), hbm()],
        out_specs=[vmem()] * 4,
        out_shape=[
            pltpu.VMEM((n, depth), jnp.bfloat16),
            jax.ShapeDtypeStruct((128, depth), jnp.bfloat16),
            jax.ShapeDtypeStruct((16 * len(FIRST), depth), jnp.bfloat16),
            jax.ShapeDtypeStruct((16 * len(SECOND), depth), jnp.bfloat16),
        ],
        scratch_shapes=[pltpu.VMEM((rows, n), jnp.bfloat16), pltpu.SemaphoreType.DMA((depth // COLS,))],
        compiler_params=params(8),
        cost_estimate=pl.CostEstimate(
            flops=2 * rows * n * depth, bytes_accessed=2 * n * depth, transcendentals=0
        ),
        name="label_rows",
    )(lab, pltpu.with_memory_space_constraint(memory, pltpu.HBM))


def merge_kernel(place_ref, cot_ref, up_ref, mid_ref, down_ref, coef_ref, part_ref, sets):
    z, x_lo = place_ref[0], place_ref[1]
    sets[0:3] = up_ref[...]
    sets[3:6] = mid_ref[...]
    sets[6:8] = down_ref[...]
    mine, theirs = sets[4, 0], sets[4, 1]
    flat = []
    for a in range(8):
        at = lax.rem(a - z + 12, 8)
        own, other = sets[at, 0], sets[at, 1]
        row = lax.broadcasted_iota(jnp.int32, other.shape, 0)
        swapped = jnp.where(row % 2 == 0, pltpu.roll(other, 7, 0), pltpu.roll(other, 1, 0))
        is_low = x_lo == 0
        flat += [jnp.where(is_low, own, swapped), jnp.where(is_low, swapped, own)]
    top = flat[0][0:2]
    logit = jnp.zeros_like(top)
    for s in flat:
        top = jnp.maximum(top, s[0:2])
        logit = logit + s[6:8]
    top = jnp.maximum(top, logit)
    rest = jnp.zeros_like(top)
    first = jnp.zeros_like(top)
    for s in flat:
        f = jnp.exp(s[0:2] - top)
        rest = rest + f * s[2:4]
        first = first + f * s[4:6]
    inverse = 1.0 / (rest + jnp.exp(logit - top))
    label_weight = -rest * inverse
    part = jnp.sum(cot_ref[...] * (first * inverse + label_weight * logit), axis=1, keepdims=True)
    part_ref[...] = jnp.broadcast_to(part[0:1] + part[1:2], part_ref.shape)
    c_own = jnp.exp(mine[0:1] - top[0:1]) * inverse[0:1]
    c_other = jnp.exp(theirs[1:2] - top[0:1]) * inverse[0:1]
    row = lax.broadcasted_iota(jnp.int32, (8, 128), 0)
    stack = jnp.where(row == 0, c_own, jnp.where(row == 1, c_other, label_weight[0:1]))
    coef_ref[...] = pltpu.roll(stack, lax.rem((10 - z) * 16, 128), 1).T


def merge_call(place, cot, up, mid, down):
    return pl.pallas_call(
        merge_kernel,
        in_specs=[smem()] + [vmem()] * 4,
        out_specs=[vmem()] * 2,
        out_shape=[jax.ShapeDtypeStruct((128, 8), jnp.float32), jax.ShapeDtypeStruct((8, 128), jnp.float32)],
        scratch_shapes=[pltpu.VMEM((8, 2, 8, 128), jnp.float32)],
        compiler_params=params(4),
        name="merge",
    )(place, cot, up, mid, down)


def mix_kernel(coef_ref, o_ref, r_ref, g_ref, gr_ref, pu_ref, pd_ref):
    bf16 = jnp.bfloat16
    half = o_ref.shape[1] // 2
    depth = 2 * half
    for i, (ref, first) in enumerate(((pu_ref, 0), (pu_ref, depth), (None, 0), (pd_ref, 0), (pd_ref, depth))):
        p = mixed(coef_ref, o_ref, r_ref, g_ref, gr_ref, FIRST[i], i, i).astype(bf16)
        if i == 2:
            pu_ref[:, 2 * depth:] = p[:, :half]
            pd_ref[:, 2 * depth:] = p[:, half:]
        else:
            ref[:, first:first + depth] = p


def mixed(coef_ref, o_ref, r_ref, g_ref, gr_ref, k, i, j):
    f32 = jnp.float32
    at, there = slice(16 * k, 16 * k + 16), slice(16 * i, 16 * i + 16)
    label = slice(16 * j, 16 * j + 16)
    c = coef_ref[at, :]
    g = g_ref[at, :].astype(f32) + gr_ref[label, :].astype(f32)
    return c[:, 0:1] * o_ref[at, :] + c[:, 1:2] * r_ref[there, :].astype(f32) + c[:, 2:3] * g


def mix_call(coef, o, r, g, gr):
    depth = g.shape[1]
    bf16 = jnp.bfloat16
    return pl.pallas_call(
        mix_kernel,
        in_specs=[vmem()] * 5,
        out_specs=[vmem()] * 2,
        out_shape=[jax.ShapeDtypeStruct((16, 2 * depth + depth // 2), bf16)] * 2,
        compiler_params=params(8),
        name="mix",
    )(coef, o, r, g, gr)


def rest_kernel(coef_ref, o_ref, r_ref, g_ref, *outs):
    for i, out in enumerate(outs):
        out[...] = mixed(coef_ref, o_ref, r_ref, g_ref, r_ref, SECOND[i], i, i + len(SECOND))


def rest_call(coef, o, r, g):
    depth = g.shape[1]
    return pl.pallas_call(
        rest_kernel,
        in_specs=[vmem()] * 4,
        out_specs=[vmem()] * 3,
        out_shape=[jax.ShapeDtypeStruct((16, depth), jnp.float32)] * 3,
        compiler_params=params(8),
        name="rest",
    )(coef, o, r, g)


def shards(queries, memory, log_scale, labels, valid, cotangent):
    f32, bf16 = jnp.float32, jnp.bfloat16
    together = lambda *arrays: lax.optimization_barrier(arrays)
    scale = jnp.exp(log_scale)
    where = lax.axis_index("mem")
    z = lax.rem(where, 8)
    x_lo = where // 8
    depth = memory.shape[1]
    half = depth // 2
    start_row = where * memory.shape[0]
    roll_by = lax.rem(z + 6, 8) * 16

    up3, down3 = both(queries, queries, 3)
    own_labels = lax.dynamic_slice_in_dim(labels, x_lo * 128, 128)
    own_cot = lax.dynamic_slice_in_dim(cotangent, x_lo * 128, 128)
    rolled = lax.dynamic_slice_in_dim(jnp.concatenate([own_labels, own_labels]), roll_by, 128)
    up3, late_queries = together(up3, queries)
    to_up, to_down, to_x = pack_call(late_queries, up3, down3, rolled[None, :], own_cot[None, :])
    up, down = both(to_up, to_down, 1)
    own_x = send(queries, PARTNER)
    two_x = send(to_x, PARTNER)
    note = two_x[:, 2 * depth:].astype(f32)
    lab = (jnp.concatenate([rolled, (note[0] * 256.0 + note[1]).astype(jnp.int32)]) - start_row)[:, None]
    cots = jnp.stack([own_cot, (note[2] + note[3]) + note[4]])
    up, down, lab = together(up, down, lab)
    up_x, down_x = send(up, PARTNER), send(down, PARTNER)
    resident, g, g_first, g_second = labels_call(lab, memory)
    resident = pltpu.with_memory_space_constraint(resident, pltpu.VMEM)
    g_first_x = send(g_first, PARTNER)
    blocks = (to_up, to_x, up, down, own_x, two_x, up_x, down_x)

    e, stat = logits_call(scale, roll_by.reshape(1), blocks, resident, lab, valid[None, :])
    stat_other = send(stat, PARTNER)
    o, o_first, o_second = weighted_call(e, resident, g_second)
    stat_other, o_first, o_second, g_first_x = together(stat_other, o_first, o_second, g_first_x)
    r_first = send(o_first, PARTNER)
    pair = jnp.stack([stat, stat_other])
    s_up, s_down = both(pair, pair, 1)
    s_up, s_down, o_second = together(s_up, s_down, o_second)
    r_second = send(o_second, PARTNER)
    three = jnp.stack([s_up, pair, s_down])
    t_up, t_down = both(three, three[:2], 3)
    t_up, late_z, late_x = together(t_up, z, x_lo)
    coef, part = merge_call(jnp.stack([late_z, late_x]), cots, t_up, three, t_down)
    pu, pd = mix_call(coef, o, r_first, g, g_first_x)
    au, ad = both(pu, pd, 1)
    p0, p3, p5 = rest_call(coef, o, r_second, g)
    for pairs in (CROSS, CORE):
        part = part + send(part, pairs)
    au, ad, part, p0, p3, p5 = together(au, ad, part, p0, p3, p5)
    zero = jnp.zeros((16, half), f32)
    near, next_, last = slice(0, depth), slice(depth, 2 * depth), slice(2 * depth, 2 * depth + half)
    p3 = p3 + ad[:, next_].astype(f32) + jnp.concatenate([au[:, last].astype(f32), zero], axis=1)
    p5 = p5 + au[:, next_].astype(f32) + jnp.concatenate([zero, ad[:, last].astype(f32)], axis=1)
    p3, p5, part = together(p3.astype(bf16), p5.astype(bf16), part)
    a3, a5 = both(p3, p5, 3)
    for pairs in (Y1, Y2):
        part = part + send(part, pairs)
    summed = p0 + (au[:, near].astype(f32) + ad[:, near].astype(f32)) + (a3.astype(f32) + a5.astype(f32))
    q_rows = queries.shape[0]
    a3, last_cot = together(a3, cotangent)
    my_cot = lax.dynamic_slice_in_dim(last_cot, where * q_rows, q_rows)
    grad_queries = (scale * my_cot[:, None] * summed).astype(bf16)

    count = cotangent.shape[0] * lax.axis_size("dp")
    scale_grad = part[0, 0:1] / count
    return (grad_queries, scale_grad)


def solution(mesh):
    placed = (P(("dp", "mem"), None), P("mem", None), P(), P("dp"), P("mem"), P("dp"))
    return jax.shard_map(
        shards, mesh=mesh, in_specs=placed, out_specs=(P(("dp", "mem"), None), P()), check_vma=False
    )
```

time: 108 us -> 103 us (0.954)
  the two profiles are of different devices: /device:TPU:26 before, /device:TPU:32 now
where the time goes in v3:
time: 103 us; the launch traced here: 101 us
  starting transfers between devices  39.2 us (38%)
  waiting for transfers between devices  35.6 us (35%)
  Pallas kernels  20 us (19%)
  between operations  3.28 us (3%)
  local copies, waits for them, and re-layouts  2.24 us (2%)
  other arithmetic  1.05 us (1%)
    ppermute x24, starting transfers between devices, send(): return lax.ppermute(x, AXES, pairs)  39.2 us
    ppermute x24, waiting for transfers between devices, send(): return lax.ppermute(x, AXES, pairs)  35.6 us
    pallas_call x1, Pallas kernels, labels_call(): pl.pallas_call(labels_kernel, in_specs=[vmem(), hbm()], out_specs=[vmem()...  7.41 us
    pallas_call x1, Pallas kernels, logits_call(): pl.pallas_call(logits_kernel, in_specs=[smem(), smem()] + [vmem()] * (len...  5.48 us
    pallas_call x1, Pallas kernels, weighted_call(): pl.pallas_call(weighted_kernel, in_specs=[vmem()] * 3, out_specs=[vmem()]...  4.52 us
  transfers between devices with their start and end apart: 24, of which 15 were waited for; matrix products, arithmetic and copies ran while one was open for 2% of the time, Pallas kernels for 19%

profile of v3, /device:TPU:32, one launch (start us, length us, event | category | flops | bytes accessed | tf_op | source)
XLA Modules:
  0.0 101.3 jit_solution(16574039676301841573)
XLA Ops:
  0.6 5.9 %collective-permute-start = (bf16[16,4096]{1,0:T(8,128)(2,1)}, bf16[16,4096]{1,0:T(8,128)(2,1)S(1)}, u32[]{:S(2)}, u32[]{:S(2)}) collective-permute-start(bf16[16,4096]{1,0:T(8,128)(2,1)} %own_ref), channel_id=1, source_target_pairs={{0,3},{1,4},{2,5},{3,6},{4,7},{5,0},{6,1},{7,2},{16,19},{17,20},{1... | collective-permute-start | bytes 393224 | tf_op jit(solution)/shard_map/ppermute | solution.py:43
  6.6 0.1 collective-permute-start.1
  6.7 0.8 dynamic_slice.12
  7.4 0.8 dynamic-slice_bitcast_fusion.cot_ref
  8.2 0.1 dynamic-slice_bitcast_fusion.1
  8.2 7.2 %collective-permute-done.up3_ref = bf16[16,4096]{1,0:T(8,128)(2,1)S(1)} collective-permute-done((bf16[16,4096]{1,0:T(8,128)(2,1)}, bf16[16,4096]{1,0:T(8,128)(2,1)S(1)}, u32[]{:S(2)}, u32[]{:S(2)}) %collective-permute-start) | collective-permute-done | bytes 131104 | tf_op jit(solution)/shard_map/ppermute | solution.py:43
  15.4 3.2 %collective-permute-done.1.down3_ref = bf16[16,4096]{1,0:T(8,128)(2,1)S(1)} collective-permute-done((bf16[16,4096]{1,0:T(8,128)(2,1)}, bf16[16,4096]{1,0:T(8,128)(2,1)S(1)}, u32[]{:S(2)}, u32[]{:S(2)}) %collective-permute-start.1) | collective-permute-done | bytes 131104 | tf_op jit(solution)/shard_map/ppermute | solution.py:43
  18.6 1.0 pack.1
  19.6 1.6 %collective-permute-start.4 = (bf16[16,8320]{1,0:T(8,128)(2,1)S(1)}, bf16[16,8320]{1,0:T(8,128)(2,1)S(1)}, u32[]{:S(2)}, u32[]{:S(2)}) collective-permute-start(bf16[16,8320]{1,0:T(8,128)(2,1)S(1)} %get-tuple-element.49.two), channel_id=1, source_target_pairs={{0,8},{1,9},{2,10},{3,11},{4,12},{5,13},{6,14},{7,15},{16,56},{17,... | collective-permute-start | bytes 798728 | tf_op jit(solution)/shard_map/ppermute | solution.py:43
  21.2 0.5 collective-permute-start.5
  22.4 0.1 collective-permute-start.3
  22.5 2.0 %collective-permute-start.2 = (bf16[16,10240]{1,0:T(8,128)(2,1)S(1)}, bf16[16,10240]{1,0:T(8,128)(2,1)S(1)}, u32[]{:S(2)}, u32[]{:S(2)}) collective-permute-start(bf16[16,10240]{1,0:T(8,128)(2,1)S(1)} %get-tuple-element.48.own), channel_id=1, source_target_pairs={{0,1},{1,2},{2,3},{3,4},{4,5},{5,6},{6,7},{7,0},{16,17},{17,18},{1... | collective-permute-start | bytes 983048 | tf_op jit(solution)/shard_map/ppermute | solution.py:43
  24.6 1.6 %collective-permute-done.4.two_x = bf16[16,8320]{1,0:T(8,128)(2,1)S(1)} collective-permute-done((bf16[16,8320]{1,0:T(8,128)(2,1)S(1)}, bf16[16,8320]{1,0:T(8,128)(2,1)S(1)}, u32[]{:S(2)}, u32[]{:S(2)}) %collective-permute-start.4) | collective-permute-done | bytes 266272 | tf_op jit(solution)/shard_map/ppermute | solution.py:43
  26.2 0.1 copy.10
  26.3 6.0 %collective-permute-done.3.down = bf16[16,10240]{1,0:T(8,128)(2,1)S(1)} collective-permute-done((bf16[16,10240]{1,0:T(8,128)(2,1)S(1)}, bf16[16,10240]{1,0:T(8,128)(2,1)S(1)}, u32[]{:S(2)}, u32[]{:S(2)}) %collective-permute-start.3) | collective-permute-done | bytes 327712 | tf_op jit(solution)/shard_map/ppermute | solution.py:43
  32.3 0.1 collective-permute-done.2.up
  32.4 0.3 collective-permute-start.6
  32.7 1.7 %collective-permute-start.7 = (bf16[16,10240]{1,0:T(8,128)(2,1)S(1)}, bf16[16,10240]{1,0:T(8,128)(2,1)S(1)}, u32[]{:S(2)}, u32[]{:S(2)}) collective-permute-start(bf16[16,10240]{1,0:T(8,128)(2,1)S(1)} %collective-permute-done.3.down), channel_id=1, source_target_pairs={{0,8},{1,9},{2,10},{3,11},{4,12},{5,13},{6,14},{7,15},{16,56},{17,... | collective-permute-start | bytes 983048 | tf_op jit(solution)/shard_map/ppermute | solution.py:43
  34.4 7.4 %label_rows.1 = (bf16[2048,4096]{1,0:T(8,128)(2,1)S(1)}, bf16[128,4096]{1,0:T(8,128)(2,1)S(1)}, bf16[80,4096]{1,0:T(8,128)(2,1)S(1)}, bf16[48,4096]{1,0:T(8,128)(2,1)S(1)}) custom-call(s32[256,1]{1,0:T(8,128)S(1)} %broadcast_subtract_fusion.lab_ref, bf16[2048,4096]{1,0:T(8,128)(2,1)} %mem_ref.1), custom_call_target="tpu_custom_call" | custom-call | flops 4294967296 | bytes 16777216 | tf_op jit(solution)/shard_map/label_rows/pallas_call | solution.py:247
  41.8 0.5 collective-permute-start.9
  42.4 0.0 collective-permute-done.5.own_x
  42.4 0.0 collective-permute-done.6.up_x
  42.4 0.6 collective-permute-done.7.down_x
  43.0 5.5 %logits.1 = (bf16[256,2048]{1,0:T(8,128)(2,1)S(1)}, f32[8,128]{1,0:T(8,128)S(1)}) custom-call(f32[1]{0:T(128)} %exp.3.scale_ref, s32[1]{0:T(128)} %bitcast.1.shift_ref, bf16[16,10240]{1,0:T(8,128)(2,1)S(1)} %get-tuple-element.48.own, bf16[16,8320]{1,0:T(8,128)(2,1)S(1)} %get-tuple-element.49.two, bf16[16,10240]{1,0:T(8,128)(2,1)S(1)} %collective-permute-done.2.up, ...), custom_call_target="tpu_custom_call" | custom-call | flops 4294967296 | bytes 16777216 | tf_op jit(solution)/shard_map/logits/pallas_call | solution.py:163
  48.5 1.2 %collective-permute-start.8 = (f32[8,128]{1,0:T(8,128)S(1)}, f32[8,128]{1,0:T(8,128)S(1)}, u32[]{:S(2)}, u32[]{:S(2)}) collective-permute-start(f32[8,128]{1,0:T(8,128)S(1)} %get-tuple-element.55), channel_id=1, source_target_pairs={{0,8},{1,9},{2,10},{3,11},{4,12},{5,13},{6,14},{7,15},{16,56},{17,... | collective-permute-start | bytes 12296 | tf_op jit(solution)/shard_map/ppermute | solution.py:43
  49.6 4.5 %weighted.1 = (f32[128,4096]{1,0:T(8,128)S(1)}, bf16[80,4096]{1,0:T(8,128)(2,1)S(1)}, bf16[96,4096]{1,0:T(8,128)(2,1)S(1)}) custom-call(bf16[256,2048]{1,0:T(8,128)(2,1)S(1)} %get-tuple-element.56.e_ref, bf16[2048,4096]{1,0:T(8,128)(2,1)S(1)} %get-tuple-element.54.mem_ref, bf16[48,4096]{1,0:T(8,128)(2,1)S(1)} %get-tuple-element.57.g_ref), custom_call_target="tpu_custom_call" | custom-call | flops 4294967296 | bytes 16777216 | tf_op jit(solution)/shard_map/weighted/pallas_call | solution.py:205
  54.2 0.0 collective-permute-done.8
  54.2 0.0 collective-permute-done.9.gr_ref
  54.2 0.9 collective-permute-start.14
  55.1 1.3 %collective-permute-start.11 = (f32[2,8,128]{2,1,0:T(8,128)S(1)}, f32[2,8,128]{2,1,0:T(8,128)S(1)}, u32[]{:S(2)}, u32[]{:S(2)}) collective-permute-start(f32[2,8,128]{2,1,0:T(8,128)S(1)} %get-tuple-element.93), channel_id=1, source_target_pairs={{0,7},{1,0},{2,1},{3,2},{4,3},{5,4},{6,5},{7,6},{16,23},{17,16},{1... | collective-permute-start | bytes 24584 | tf_op jit(solution)/shard_map/ppermute | solution.py:43
  56.4 0.7 collective-permute-start.10
  57.2 1.6 %collective-permute-done.11 = f32[2,8,128]{2,1,0:T(8,128)S(1)} collective-permute-done((f32[2,8,128]{2,1,0:T(8,128)S(1)}, f32[2,8,128]{2,1,0:T(8,128)S(1)}, u32[]{:S(2)}, u32[]{:S(2)}) %collective-permute-start.11) | collective-permute-done | bytes 8224 | tf_op jit(solution)/shard_map/ppermute | solution.py:43
  58.8 1.3 %collective-permute-done.10 = f32[2,8,128]{2,1,0:T(8,128)S(1)} collective-permute-done((f32[2,8,128]{2,1,0:T(8,128)S(1)}, f32[2,8,128]{2,1,0:T(8,128)S(1)}, u32[]{:S(2)}, u32[]{:S(2)}) %collective-permute-start.10) | collective-permute-done | bytes 8224 | tf_op jit(solution)/shard_map/ppermute | solution.py:43
  60.1 1.2 %collective-permute-start.19 = (bf16[96,4096]{1,0:T(8,128)(2,1)S(1)}, bf16[96,4096]{1,0:T(8,128)(2,1)S(1)}, u32[]{:S(2)}, u32[]{:S(2)}) collective-permute-start(bf16[96,4096]{1,0:T(8,128)(2,1)S(1)} %get-tuple-element.76), channel_id=1, source_target_pairs={{0,8},{1,9},{2,10},{3,11},{4,12},{5,13},{6,14},{7,15},{16,56},{17,... | collective-permute-start | bytes 2359304 | tf_op jit(solution)/shard_map/ppermute | solution.py:43
  61.3 6.2 %collective-permute-start.12 = (f32[3,2,8,128]{3,2,1,0:T(8,128)S(1)}, f32[3,2,8,128]{3,2,1,0:T(8,128)S(1)}, u32[]{:S(2)}, u32[]{:S(2)}) collective-permute-start(f32[3,2,8,128]{3,2,1,0:T(8,128)S(1)} %pad_maximum_fusion.mid_ref), channel_id=1, source_target_pairs={{0,3},{1,4},{2,5},{3,6},{4,7},{5,0},{6,1},{7,2},{16,19},{17,20},{1... | collective-permute-start | bytes 73736 | tf_op jit(solution)/shard_map/ppermute | solution.py:43
  67.5 0.0 collective-permute-start.13
  67.5 1.5 %collective-permute-done.12.up_ref = f32[3,2,8,128]{3,2,1,0:T(8,128)S(1)} collective-permute-done((f32[3,2,8,128]{3,2,1,0:T(8,128)S(1)}, f32[3,2,8,128]{3,2,1,0:T(8,128)S(1)}, u32[]{:S(2)}, u32[]{:S(2)}) %collective-permute-start.12) | collective-permute-done | bytes 24608 | tf_op jit(solution)/shard_map/ppermute | solution.py:43
  69.0 0.1 pad_add_fusion.2.place_ref
  69.1 5.3 %collective-permute-done.13.down_ref = f32[2,2,8,128]{3,2,1,0:T(8,128)S(1)} collective-permute-done((f32[2,2,8,128]{3,2,1,0:T(8,128)S(1)}, f32[2,2,8,128]{3,2,1,0:T(8,128)S(1)}, u32[]{:S(2)}, u32[]{:S(2)}) %collective-permute-start.13) | collective-permute-done | bytes 16416 | tf_op jit(solution)/shard_map/ppermute | solution.py:43
  74.3 0.8 merge.1
  75.1 0.0 collective-permute-done.14.r_ref
  75.1 0.5 mix.1
  75.6 0.5 collective-permute-start.15
  76.1 1.6 %collective-permute-start.16 = (bf16[16,10240]{1,0:T(8,128)(2,1)S(1)}, bf16[16,10240]{1,0:T(8,128)(2,1)S(1)}, u32[]{:S(2)}, u32[]{:S(2)}) collective-permute-start(bf16[16,10240]{1,0:T(8,128)(2,1)S(1)} %get-tuple-element.74), channel_id=1, source_target_pairs={{0,7},{1,0},{2,1},{3,2},{4,3},{5,4},{6,5},{7,6},{16,23},{17,16},{1... | collective-permute-start | bytes 983048 | tf_op jit(solution)/shard_map/ppermute | solution.py:43
  77.7 2.8 %collective-permute-start.17 = (f32[8,128]{1,0:T(8,128)S(1)}, f32[8,128]{1,0:T(8,128)S(1)}, u32[]{:S(2)}, u32[]{:S(2)}) collective-permute-start(f32[8,128]{1,0:T(8,128)S(1)} %get-tuple-element.75), channel_id=1, source_target_pairs={{0,40},{1,41},{2,42},{3,43},{4,44},{5,45},{6,46},{7,47},{16,24},{1... | collective-permute-start | bytes 12296 | tf_op jit(solution)/shard_map/ppermute | solution.py:43
  80.6 2.0 %collective-permute-done.17 = f32[8,128]{1,0:T(8,128)S(1)} collective-permute-done((f32[8,128]{1,0:T(8,128)S(1)}, f32[8,128]{1,0:T(8,128)S(1)}, u32[]{:S(2)}, u32[]{:S(2)}) %collective-permute-start.17) | collective-permute-done | bytes 4128 | tf_op jit(solution)/shard_map/ppermute | solution.py:43
  82.6 0.0 collective-permute-start.18
  82.6 1.2 %collective-permute-done.18 = f32[8,128]{1,0:T(8,128)S(1)} collective-permute-done((f32[8,128]{1,0:T(8,128)S(1)}, f32[8,128]{1,0:T(8,128)S(1)}, u32[]{:S(2)}, u32[]{:S(2)}) %collective-permute-start.18) | collective-permute-done | bytes 4128 | tf_op jit(solution)/shard_map/ppermute | solution.py:43
  83.7 0.0 collective-permute-done.19.r_ref
  83.7 0.3 rest.1
  84.1 0.0 collective-permute-done.15
  84.1 0.0 collective-permute-done.16
  84.1 0.1 add_convert_fusion
  84.2 1.5 %collective-permute-start.20 = (bf16[16,4096]{1,0:T(8,128)(2,1)S(1)}, bf16[16,4096]{1,0:T(8,128)(2,1)S(1)}, u32[]{:S(2)}, u32[]{:S(2)}) collective-permute-start(bf16[16,4096]{1,0:T(8,128)(2,1)S(1)} %get-tuple-element.85), channel_id=1, source_target_pairs={{0,3},{1,4},{2,5},{3,6},{4,7},{5,0},{6,1},{7,2},{16,19},{17,20},{1... | collective-permute-start | bytes 393224 | tf_op jit(solution)/shard_map/ppermute | solution.py:43
  85.7 3.6 %collective-permute-start.21 = (bf16[16,4096]{1,0:T(8,128)(2,1)S(1)}, bf16[16,4096]{1,0:T(8,128)(2,1)S(1)}, u32[]{:S(2)}, u32[]{:S(2)}) collective-permute-start(bf16[16,4096]{1,0:T(8,128)(2,1)S(1)} %get-tuple-element.88), channel_id=1, source_target_pairs={{0,5},{1,6},{2,7},{3,0},{4,1},{5,2},{6,3},{7,4},{16,21},{17,22},{1... | collective-permute-start | bytes 393224 | tf_op jit(solution)/shard_map/ppermute | solution.py:43
  89.3 1.6 %collective-permute-start.22 = (f32[8,128]{1,0:T(8,128)S(1)}, f32[8,128]{1,0:T(8,128)S(1)}, u32[]{:S(2)}, u32[]{:S(2)}) collective-permute-start(f32[8,128]{1,0:T(8,128)S(1)} %add.79), channel_id=1, source_target_pairs={{0,64},{1,65},{2,66},{3,67},{4,68},{5,69},{6,70},{7,71},{16,80},{1... | collective-permute-start | bytes 12296 | tf_op jit(solution)/shard_map/ppermute | solution.py:43
  90.9 2.0 %collective-permute-done.22 = f32[8,128]{1,0:T(8,128)S(1)} collective-permute-done((f32[8,128]{1,0:T(8,128)S(1)}, f32[8,128]{1,0:T(8,128)S(1)}, u32[]{:S(2)}, u32[]{:S(2)}) %collective-permute-start.22) | collective-permute-done | bytes 4128 | tf_op jit(solution)/shard_map/ppermute | solution.py:43
  92.9 3.2 %collective-permute-start.23 = (f32[8,128]{1,0:T(8,128)S(1)}, f32[8,128]{1,0:T(8,128)S(1)}, u32[]{:S(2)}, u32[]{:S(2)}) collective-permute-start(f32[8,128]{1,0:T(8,128)S(1)} %add.89), channel_id=1, source_target_pairs={{0,128},{1,129},{2,130},{3,131},{4,132},{5,133},{6,134},{7,135},{1... | collective-permute-start | bytes 12296 | tf_op jit(solution)/shard_map/ppermute | solution.py:43
  96.1 1.9 %collective-permute-done.23 = f32[8,128]{1,0:T(8,128)S(1)} collective-permute-done((f32[8,128]{1,0:T(8,128)S(1)}, f32[8,128]{1,0:T(8,128)S(1)}, u32[]{:S(2)}, u32[]{:S(2)}) %collective-permute-start.23) | collective-permute-done | bytes 4128 | tf_op jit(solution)/shard_map/ppermute | solution.py:43
  98.0 0.5 slice.53
  99.2 0.0 collective-permute-done.20
  99.2 0.1 dynamic-slice_multiply_fusion
  99.3 0.1 collective-permute-done.21
  99.4 0.7 multiply_convert_fusion
  (19 shorter events, 0.1 us)
Async XLA Ops:
  0.6 42.3 %copy-start = (s32[2048]{0:T(1024)S(1)}, s32[2048]{0:T(1024)}, u32[]{:S(2)}) copy-start(s32[2048]{0:T(1024)} %param.10) | copy-start | bytes 24580
  0.6 14.8 %collective-permute-start = (bf16[16,4096]{1,0:T(8,128)(2,1)}, bf16[16,4096]{1,0:T(8,128)(2,1)S(1)}, u32[]{:S(2)}, u32[]{:S(2)}) collective-permute-start(bf16[16,4096]{1,0:T(8,128)(2,1)} %own_ref), channel_id=1, source_target_pairs={{0,3},{1,4},{2,5},{3,6},{4,7},{5,0},{6,1},{7,2},{16,19},{17,20},{1... | collective-permute-start | bytes 393224 | tf_op jit(solution)/shard_map/ppermute | solution.py:43
  6.6 12.1 %collective-permute-start.1 = (bf16[16,4096]{1,0:T(8,128)(2,1)}, bf16[16,4096]{1,0:T(8,128)(2,1)S(1)}, u32[]{:S(2)}, u32[]{:S(2)}) collective-permute-start(bf16[16,4096]{1,0:T(8,128)(2,1)} %own_ref), channel_id=1, source_target_pairs={{0,5},{1,6},{2,7},{3,0},{4,1},{5,2},{6,3},{7,4},{16,21},{17,22},{1... | collective-permute-start | bytes 393224 | tf_op jit(solution)/shard_map/ppermute | solution.py:43
  19.6 6.5 %collective-permute-start.4 = (bf16[16,8320]{1,0:T(8,128)(2,1)S(1)}, bf16[16,8320]{1,0:T(8,128)(2,1)S(1)}, u32[]{:S(2)}, u32[]{:S(2)}) collective-permute-start(bf16[16,8320]{1,0:T(8,128)(2,1)S(1)} %get-tuple-element.49.two), channel_id=1, source_target_pairs={{0,8},{1,9},{2,10},{3,11},{4,12},{5,13},{6,14},{7,15},{16,56},{17,... | collective-permute-start | bytes 798728 | tf_op jit(solution)/shard_map/ppermute | solution.py:43
  21.2 21.2 %collective-permute-start.5 = (bf16[16,4096]{1,0:T(8,128)(2,1)}, bf16[16,4096]{1,0:T(8,128)(2,1)S(1)}, u32[]{:S(2)}, u32[]{:S(2)}) collective-permute-start(bf16[16,4096]{1,0:T(8,128)(2,1)} %own_ref), channel_id=1, source_target_pairs={{0,8},{1,9},{2,10},{3,11},{4,12},{5,13},{6,14},{7,15},{16,56},{17,... | collective-permute-start | bytes 393224 | tf_op jit(solution)/shard_map/ppermute | solution.py:43
  22.4 9.8 %collective-permute-start.3 = (bf16[16,10240]{1,0:T(8,128)(2,1)S(1)}, bf16[16,10240]{1,0:T(8,128)(2,1)S(1)}, u32[]{:S(2)}, u32[]{:S(2)}) collective-permute-start(bf16[16,10240]{1,0:T(8,128)(2,1)S(1)} %get-tuple-element.50), channel_id=1, source_target_pairs={{0,7},{1,0},{2,1},{3,2},{4,3},{5,4},{6,5},{7,6},{16,23},{17,16},{1... | collective-permute-start | bytes 983048 | tf_op jit(solution)/shard_map/ppermute | solution.py:43
  22.5 9.8 %collective-permute-start.2 = (bf16[16,10240]{1,0:T(8,128)(2,1)S(1)}, bf16[16,10240]{1,0:T(8,128)(2,1)S(1)}, u32[]{:S(2)}, u32[]{:S(2)}) collective-permute-start(bf16[16,10240]{1,0:T(8,128)(2,1)S(1)} %get-tuple-element.48.own), channel_id=1, source_target_pairs={{0,1},{1,2},{2,3},{3,4},{4,5},{5,6},{6,7},{7,0},{16,17},{17,18},{1... | collective-permute-start | bytes 983048 | tf_op jit(solution)/shard_map/ppermute | solution.py:43
  32.4 10.0 %collective-permute-start.6 = (bf16[16,10240]{1,0:T(8,128)(2,1)S(1)}, bf16[16,10240]{1,0:T(8,128)(2,1)S(1)}, u32[]{:S(2)}, u32[]{:S(2)}) collective-permute-start(bf16[16,10240]{1,0:T(8,128)(2,1)S(1)} %collective-permute-done.2.up), channel_id=1, source_target_pairs={{0,8},{1,9},{2,10},{3,11},{4,12},{5,13},{6,14},{7,15},{16,56},{17,... | collective-permute-start | bytes 983048 | tf_op jit(solution)/shard_map/ppermute | solution.py:43
  32.7 10.3 %collective-permute-start.7 = (bf16[16,10240]{1,0:T(8,128)(2,1)S(1)}, bf16[16,10240]{1,0:T(8,128)(2,1)S(1)}, u32[]{:S(2)}, u32[]{:S(2)}) collective-permute-start(bf16[16,10240]{1,0:T(8,128)(2,1)S(1)} %collective-permute-done.3.down), channel_id=1, source_target_pairs={{0,8},{1,9},{2,10},{3,11},{4,12},{5,13},{6,14},{7,15},{16,56},{17,... | collective-permute-start | bytes 983048 | tf_op jit(solution)/shard_map/ppermute | solution.py:43
  41.8 12.4 %collective-permute-start.9 = (bf16[80,4096]{1,0:T(8,128)(2,1)S(1)}, bf16[80,4096]{1,0:T(8,128)(2,1)S(1)}, u32[]{:S(2)}, u32[]{:S(2)}) collective-permute-start(bf16[80,4096]{1,0:T(8,128)(2,1)S(1)} %get-tuple-element.60), channel_id=1, source_target_pairs={{0,8},{1,9},{2,10},{3,11},{4,12},{5,13},{6,14},{7,15},{16,56},{17,... | collective-permute-start | bytes 1966088 | tf_op jit(solution)/shard_map/ppermute | solution.py:43
  48.4 50.8 %copy-start.1 = (f32[256]{0:T(256)S(1)}, f32[256]{0:T(256)}, u32[]{:S(2)}) copy-start(f32[256]{0:T(256)} %param.11) | copy-start | bytes 3076
  48.5 5.7 %collective-permute-start.8 = (f32[8,128]{1,0:T(8,128)S(1)}, f32[8,128]{1,0:T(8,128)S(1)}, u32[]{:S(2)}, u32[]{:S(2)}) collective-permute-start(f32[8,128]{1,0:T(8,128)S(1)} %get-tuple-element.55), channel_id=1, source_target_pairs={{0,8},{1,9},{2,10},{3,11},{4,12},{5,13},{6,14},{7,15},{16,56},{17,... | collective-permute-start | bytes 12296 | tf_op jit(solution)/shard_map/ppermute | solution.py:43
  54.2 20.9 %collective-permute-start.14 = (bf16[80,4096]{1,0:T(8,128)(2,1)S(1)}, bf16[80,4096]{1,0:T(8,128)(2,1)S(1)}, u32[]{:S(2)}, u32[]{:S(2)}) collective-permute-start(bf16[80,4096]{1,0:T(8,128)(2,1)S(1)} %get-tuple-element.70), channel_id=1, source_target_pairs={{0,8},{1,9},{2,10},{3,11},{4,12},{5,13},{6,14},{7,15},{16,56},{17,... | collective-permute-start | bytes 1966088 | tf_op jit(solution)/shard_map/ppermute | solution.py:43
  55.1 3.7 %collective-permute-start.11 = (f32[2,8,128]{2,1,0:T(8,128)S(1)}, f32[2,8,128]{2,1,0:T(8,128)S(1)}, u32[]{:S(2)}, u32[]{:S(2)}) collective-permute-start(f32[2,8,128]{2,1,0:T(8,128)S(1)} %get-tuple-element.93), channel_id=1, source_target_pairs={{0,7},{1,0},{2,1},{3,2},{4,3},{5,4},{6,5},{7,6},{16,23},{17,16},{1... | collective-permute-start | bytes 24584 | tf_op jit(solution)/shard_map/ppermute | solution.py:43
  56.4 3.7 %collective-permute-start.10 = (f32[2,8,128]{2,1,0:T(8,128)S(1)}, f32[2,8,128]{2,1,0:T(8,128)S(1)}, u32[]{:S(2)}, u32[]{:S(2)}) collective-permute-start(f32[2,8,128]{2,1,0:T(8,128)S(1)} %get-tuple-element.93), channel_id=1, source_target_pairs={{0,1},{1,2},{2,3},{3,4},{4,5},{5,6},{6,7},{7,0},{16,17},{17,18},{1... | collective-permute-start | bytes 24584 | tf_op jit(solution)/shard_map/ppermute | solution.py:43
  60.1 23.7 %collective-permute-start.19 = (bf16[96,4096]{1,0:T(8,128)(2,1)S(1)}, bf16[96,4096]{1,0:T(8,128)(2,1)S(1)}, u32[]{:S(2)}, u32[]{:S(2)}) collective-permute-start(bf16[96,4096]{1,0:T(8,128)(2,1)S(1)} %get-tuple-element.76), channel_id=1, source_target_pairs={{0,8},{1,9},{2,10},{3,11},{4,12},{5,13},{6,14},{7,15},{16,56},{17,... | collective-permute-start | bytes 2359304 | tf_op jit(solution)/shard_map/ppermute | solution.py:43
  61.3 7.7 %collective-permute-start.12 = (f32[3,2,8,128]{3,2,1,0:T(8,128)S(1)}, f32[3,2,8,128]{3,2,1,0:T(8,128)S(1)}, u32[]{:S(2)}, u32[]{:S(2)}) collective-permute-start(f32[3,2,8,128]{3,2,1,0:T(8,128)S(1)} %pad_maximum_fusion.mid_ref), channel_id=1, source_target_pairs={{0,3},{1,4},{2,5},{3,6},{4,7},{5,0},{6,1},{7,2},{16,19},{17,20},{1... | collective-permute-start | bytes 73736 | tf_op jit(solution)/shard_map/ppermute | solution.py:43
  67.5 6.9 %collective-permute-start.13 = (f32[2,2,8,128]{3,2,1,0:T(8,128)S(1)}, f32[2,2,8,128]{3,2,1,0:T(8,128)S(1)}, u32[]{:S(2)}, u32[]{:S(2)}) collective-permute-start(f32[2,2,8,128]{3,2,1,0:T(8,128)S(1)} %pad_maximum_fusion.1), channel_id=1, source_target_pairs={{0,5},{1,6},{2,7},{3,0},{4,1},{5,2},{6,3},{7,4},{16,21},{17,22},{1... | collective-permute-start | bytes 49160 | tf_op jit(solution)/shard_map/ppermute | solution.py:43
  75.6 8.4 %collective-permute-start.15 = (bf16[16,10240]{1,0:T(8,128)(2,1)S(1)}, bf16[16,10240]{1,0:T(8,128)(2,1)S(1)}, u32[]{:S(2)}, u32[]{:S(2)}) collective-permute-start(bf16[16,10240]{1,0:T(8,128)(2,1)S(1)} %get-tuple-element.73), channel_id=1, source_target_pairs={{0,1},{1,2},{2,3},{3,4},{4,5},{5,6},{6,7},{7,0},{16,17},{17,18},{1... | collective-permute-start | bytes 983048 | tf_op jit(solution)/shard_map/ppermute | solution.py:43
  76.1 8.0 %collective-permute-start.16 = (bf16[16,10240]{1,0:T(8,128)(2,1)S(1)}, bf16[16,10240]{1,0:T(8,128)(2,1)S(1)}, u32[]{:S(2)}, u32[]{:S(2)}) collective-permute-start(bf16[16,10240]{1,0:T(8,128)(2,1)S(1)} %get-tuple-element.74), channel_id=1, source_target_pairs={{0,7},{1,0},{2,1},{3,2},{4,3},{5,4},{6,5},{7,6},{16,23},{17,16},{1... | collective-permute-start | bytes 983048 | tf_op jit(solution)/shard_map/ppermute | solution.py:43
  77.7 4.8 %collective-permute-start.17 = (f32[8,128]{1,0:T(8,128)S(1)}, f32[8,128]{1,0:T(8,128)S(1)}, u32[]{:S(2)}, u32[]{:S(2)}) collective-permute-start(f32[8,128]{1,0:T(8,128)S(1)} %get-tuple-element.75), channel_id=1, source_target_pairs={{0,40},{1,41},{2,42},{3,43},{4,44},{5,45},{6,46},{7,47},{16,24},{1... | collective-permute-start | bytes 12296 | tf_op jit(solution)/shard_map/ppermute | solution.py:43
  82.6 1.2 %collective-permute-start.18 = (f32[8,128]{1,0:T(8,128)S(1)}, f32[8,128]{1,0:T(8,128)S(1)}, u32[]{:S(2)}, u32[]{:S(2)}) collective-permute-start(f32[8,128]{1,0:T(8,128)S(1)} %add.78), channel_id=1, source_target_pairs={{0,16},{1,17},{2,18},{3,19},{4,20},{5,21},{6,22},{7,23},{16,0},{17... | collective-permute-start | bytes 12296 | tf_op jit(solution)/shard_map/ppermute | solution.py:43
  84.2 15.0 %collective-permute-start.20 = (bf16[16,4096]{1,0:T(8,128)(2,1)S(1)}, bf16[16,4096]{1,0:T(8,128)(2,1)S(1)}, u32[]{:S(2)}, u32[]{:S(2)}) collective-permute-start(bf16[16,4096]{1,0:T(8,128)(2,1)S(1)} %get-tuple-element.85), channel_id=1, source_target_pairs={{0,3},{1,4},{2,5},{3,6},{4,7},{5,0},{6,1},{7,2},{16,19},{17,20},{1... | collective-permute-start | bytes 393224 | tf_op jit(solution)/shard_map/ppermute | solution.py:43
  85.7 13.7 %collective-permute-start.21 = (bf16[16,4096]{1,0:T(8,128)(2,1)S(1)}, bf16[16,4096]{1,0:T(8,128)(2,1)S(1)}, u32[]{:S(2)}, u32[]{:S(2)}) collective-permute-start(bf16[16,4096]{1,0:T(8,128)(2,1)S(1)} %get-tuple-element.88), channel_id=1, source_target_pairs={{0,5},{1,6},{2,7},{3,0},{4,1},{5,2},{6,3},{7,4},{16,21},{17,22},{1... | collective-permute-start | bytes 393224 | tf_op jit(solution)/shard_map/ppermute | solution.py:43
  89.3 3.6 %collective-permute-start.22 = (f32[8,128]{1,0:T(8,128)S(1)}, f32[8,128]{1,0:T(8,128)S(1)}, u32[]{:S(2)}, u32[]{:S(2)}) collective-permute-start(f32[8,128]{1,0:T(8,128)S(1)} %add.79), channel_id=1, source_target_pairs={{0,64},{1,65},{2,66},{3,67},{4,68},{5,69},{6,70},{7,71},{16,80},{1... | collective-permute-start | bytes 12296 | tf_op jit(solution)/shard_map/ppermute | solution.py:43
  92.9 5.1 %collective-permute-start.23 = (f32[8,128]{1,0:T(8,128)S(1)}, f32[8,128]{1,0:T(8,128)S(1)}, u32[]{:S(2)}, u32[]{:S(2)}) collective-permute-start(f32[8,128]{1,0:T(8,128)S(1)} %add.89), channel_id=1, source_target_pairs={{0,128},{1,129},{2,130},{3,131},{4,132},{5,133},{6,134},{7,135},{1... | collective-permute-start | bytes 12296 | tf_op jit(solution)/shard_map/ppermute | solution.py:43

commit v4 on v3

--- a/solution.py
+++ b/solution.py
@@ -48,11 +48,12 @@
     return send(up, along_z(k)), down
 
 
-def fill(q_scr, first, own, two, up, down):
+def fill(q_scr, first, three, up, down):
     depth = q_scr.shape[1]
     half = depth // 2
     near, next_, last = slice(0, depth), slice(depth, 2 * depth), slice(2 * depth, 2 * depth + half)
-    places = (down, next_), (up, near), (own, near), (down, near), (up, next_), (two, next_), None, (two, near)
+    third = slice(2 * depth, 3 * depth)
+    places = (down, next_), (up, near), (three, near), (down, near), (up, next_), (three, third), None, (three, next_)
     for k, place in enumerate(places):
         if place is not None:
             q_scr[first + 16 * k:first + 16 * k + 16, :] = place[0][:, place[1]]
@@ -60,12 +61,12 @@
     q_scr[first + 96:first + 112, half:] = down[:, last]
 
 
-def pack_kernel(own_ref, up3_ref, down3_ref, lab_ref, cot_ref, up_ref, down_ref, two_ref, sems):
+def pack_kernel(own_ref, up3_ref, down3_ref, lab_ref, cot_ref, up_ref, down_ref, three_ref, sems):
     f32, bf16 = jnp.float32, jnp.bfloat16
     depth = up3_ref.shape[1]
     half = depth // 2
     copies = [
-        pltpu.make_async_copy(own_ref, ref.at[:, pl.ds(0, depth)], sems.at[k]) for k, ref in enumerate((up_ref, down_ref))
+        pltpu.make_async_copy(own_ref, ref.at[:, pl.ds(0, depth)], sems.at[k]) for k, ref in enumerate((up_ref, down_ref, three_ref))
     ]
     for copy in copies:
         copy.start()
@@ -73,8 +74,8 @@
     up_ref[:, 2 * depth:] = up3_ref[:, :half]
     down_ref[:, depth:2 * depth] = up3_ref[...]
     down_ref[:, 2 * depth:] = down3_ref[:, half:]
-    two_ref[:, :depth] = up3_ref[...]
-    two_ref[:, depth:2 * depth] = down3_ref[...]
+    three_ref[:, depth:2 * depth] = up3_ref[...]
+    three_ref[:, 2 * depth:3 * depth] = down3_ref[...]
     label = lab_ref[...]
     high = lax.shift_right_logical(label, 8)
     rest = cot_ref[...]
@@ -87,7 +88,7 @@
     note = jnp.zeros((16, 128), f32)
     for k, term in enumerate(terms):
         note = jnp.where(row == k, term, note)
-    two_ref[:, 2 * depth:] = note.astype(bf16)
+    three_ref[:, 3 * depth:] = note.astype(bf16)
     for copy in copies:
         copy.wait()
 
@@ -99,17 +100,17 @@
         pack_kernel,
         in_specs=[hbm()] + [vmem()] * 4,
         out_specs=[vmem()] * 3,
-        out_shape=[jax.ShapeDtypeStruct((rows, k), jnp.bfloat16) for k in (wide, wide, 2 * depth + 128)],
-        scratch_shapes=[pltpu.SemaphoreType.DMA((2,))],
+        out_shape=[jax.ShapeDtypeStruct((rows, k), jnp.bfloat16) for k in (wide, wide, 3 * depth + 128)],
+        scratch_shapes=[pltpu.SemaphoreType.DMA((3,))],
         compiler_params=params(4),
         name="pack",
     )(pltpu.with_memory_space_constraint(own, pltpu.HBM), up3, down3, lab, cot)
 
 
-def logits_kernel(scale_ref, shift_ref, own, two, up, down, own_x, two_x, up_x, down_x,
+def logits_kernel(scale_ref, shift_ref, three, up, down, three_x, up_x, down_x,
                   mem_ref, lab_ref, valid_ref, e_ref, stat_ref, q_scr, l_scr):
-    fill(q_scr, 0, own, two, up, down)
-    fill(q_scr, 128, own_x, two_x, up_x, down_x)
+    fill(q_scr, 0, three, up, down)
+    fill(q_scr, 128, three_x, up_x, down_x)
     rows, n = l_scr.shape
     scale = scale_ref[0]
     top = jnp.full((rows, 1), NEG, jnp.float32)
@@ -256,9 +257,7 @@
         ],
         scratch_shapes=[pltpu.VMEM((rows, n), jnp.bfloat16), pltpu.SemaphoreType.DMA((depth // COLS,))],
         compiler_params=params(8),
-        cost_estimate=pl.CostEstimate(
-            flops=2 * rows * n * depth, bytes_accessed=2 * n * depth, transcendentals=0
-        ),
+        cost_estimate=pl.CostEstimate(flops=1024, bytes_accessed=1024, transcendentals=0),
         name="label_rows",
     )(lab, pltpu.with_memory_space_constraint(memory, pltpu.HBM))
 
@@ -308,6 +307,7 @@
         out_shape=[jax.ShapeDtypeStruct((128, 8), jnp.float32), jax.ShapeDtypeStruct((8, 128), jnp.float32)],
         scratch_shapes=[pltpu.VMEM((8, 2, 8, 128), jnp.float32)],
         compiler_params=params(4),
+        cost_estimate=pl.CostEstimate(flops=5 * 10**9, bytes_accessed=1024, transcendentals=0),
         name="merge",
     )(place, cot, up, mid, down)
 
@@ -383,9 +383,8 @@
     up3, late_queries = together(up3, queries)
     to_up, to_down, to_x = pack_call(late_queries, up3, down3, rolled[None, :], own_cot[None, :])
     up, down = both(to_up, to_down, 1)
-    own_x = send(queries, PARTNER)
-    two_x = send(to_x, PARTNER)
-    note = two_x[:, 2 * depth:].astype(f32)
+    three_x = send(to_x, PARTNER)
+    note = three_x[:, 3 * depth:].astype(f32)
     lab = (jnp.concatenate([rolled, (note[0] * 256.0 + note[1]).astype(jnp.int32)]) - start_row)[:, None]
     cots = jnp.stack([own_cot, (note[2] + note[3]) + note[4]])
     up, down, lab = together(up, down, lab)
@@ -393,7 +392,7 @@
     resident, g, g_first, g_second = labels_call(lab, memory)
     resident = pltpu.with_memory_space_constraint(resident, pltpu.VMEM)
     g_first_x = send(g_first, PARTNER)
-    blocks = (to_up, to_x, up, down, own_x, two_x, up_x, down_x)
+    blocks = (to_x, up, down, three_x, up_x, down_x)
 
     e, stat = logits_call(scale, roll_by.reshape(1), blocks, resident, lab, valid[None, :])
     stat_other = send(stat, PARTNER)
@@ -402,12 +401,11 @@
     r_first = send(o_first, PARTNER)
     pair = jnp.stack([stat, stat_other])
     s_up, s_down = both(pair, pair, 1)
-    s_up, s_down, o_second = together(s_up, s_down, o_second)
-    r_second = send(o_second, PARTNER)
     three = jnp.stack([s_up, pair, s_down])
     t_up, t_down = both(three, three[:2], 3)
-    t_up, late_z, late_x = together(t_up, z, x_lo)
-    coef, part = merge_call(jnp.stack([late_z, late_x]), cots, t_up, three, t_down)
+    t_up, t_down, o_second = together(t_up, t_down, o_second)
+    coef, part = merge_call(jnp.stack([z, x_lo]), cots, t_up, three, t_down)
+    r_second = send(o_second, PARTNER)
     pu, pd = mix_call(coef, o, r_first, g, g_first_x)
     au, ad = both(pu, pd, 1)
     p0, p3, p5 = rest_call(coef, o, r_second, g)

time: 103 us -> 99.7 us (0.968); the launches traced: 101 us -> 99.5 us
  starting transfers between devices: 39.2 us -> 34.1 us
  waiting for transfers between devices: 35.6 us -> 38.7 us
    ppermute x24 -> x23, starting transfers between devices: 39.2 us -> 34.1 us  [send(): return lax.ppermute(x, AXES, pairs)]
    ppermute x24 -> x23, waiting for transfers between devices: 35.6 us -> 38.7 us  [send(): return lax.ppermute(x, AXES, pairs)]
  transfers between devices with their start and end apart: 24 -> 23, of which waited for: 15 -> 16; matrix products, arithmetic and copies ran while one was open for 2% -> 2% of each run, Pallas kernels for 19% -> 19%
where the time goes in v4:
time: 99.7 us; the launch traced here: 99.5 us
  waiting for transfers between devices  38.7 us (39%)
  starting transfers between devices  34.1 us (34%)
  Pallas kernels  20.1 us (20%)
  between operations  3.27 us (3%)
  local copies, waits for them, and re-layouts  2.24 us (2%)
  other arithmetic  1.05 us (1%)
    ppermute x23, waiting for transfers between devices, send(): return lax.ppermute(x, AXES, pairs)  38.7 us
    ppermute x23, starting transfers between devices, send(): return lax.ppermute(x, AXES, pairs)  34.1 us
    pallas_call x1, Pallas kernels, labels_call(): pl.pallas_call(labels_kernel, in_specs=[vmem(), hbm()], out_specs=[vmem()...  7.41 us
    pallas_call x1, Pallas kernels, logits_call(): pl.pallas_call(logits_kernel, in_specs=[smem(), smem()] + [vmem()] * (len...  5.47 us
    pallas_call x1, Pallas kernels, weighted_call(): pl.pallas_call(weighted_kernel, in_specs=[vmem()] * 3, out_specs=[vmem()]...  4.52 us
  transfers between devices with their start and end apart: 23, of which 16 were waited for; matrix products, arithmetic and copies ran while one was open for 2% of the time, Pallas kernels for 19%

profile of v4, /device:TPU:32, one launch (start us, length us, event | category | flops | bytes accessed | tf_op | source)
XLA Modules:
  0.0 99.5 jit_solution(10216671820997180501)
XLA Ops:
  0.6 5.9 %collective-permute-start = (bf16[16,4096]{1,0:T(8,128)(2,1)}, bf16[16,4096]{1,0:T(8,128)(2,1)S(1)}, u32[]{:S(2)}, u32[]{:S(2)}) collective-permute-start(bf16[16,4096]{1,0:T(8,128)(2,1)} %own_ref), channel_id=1, source_target_pairs={{0,3},{1,4},{2,5},{3,6},{4,7},{5,0},{6,1},{7,2},{16,19},{17,20},{1... | collective-permute-start | bytes 393224 | tf_op jit(solution)/shard_map/ppermute | solution.py:43
  6.6 0.1 collective-permute-start.1
  6.7 0.8 dynamic_slice.13
  7.4 0.8 dynamic-slice_bitcast_fusion.cot_ref
  8.2 0.1 dynamic-slice_bitcast_fusion.1
  8.2 7.2 %collective-permute-done.up3_ref = bf16[16,4096]{1,0:T(8,128)(2,1)S(1)} collective-permute-done((bf16[16,4096]{1,0:T(8,128)(2,1)}, bf16[16,4096]{1,0:T(8,128)(2,1)S(1)}, u32[]{:S(2)}, u32[]{:S(2)}) %collective-permute-start) | collective-permute-done | bytes 131104 | tf_op jit(solution)/shard_map/ppermute | solution.py:43
  15.4 3.2 %collective-permute-done.1.down3_ref = bf16[16,4096]{1,0:T(8,128)(2,1)S(1)} collective-permute-done((bf16[16,4096]{1,0:T(8,128)(2,1)}, bf16[16,4096]{1,0:T(8,128)(2,1)S(1)}, u32[]{:S(2)}, u32[]{:S(2)}) %collective-permute-start.1) | collective-permute-done | bytes 131104 | tf_op jit(solution)/shard_map/ppermute | solution.py:43
  18.6 1.1 %pack.1 = (bf16[16,10240]{1,0:T(8,128)(2,1)S(1)}, bf16[16,10240]{1,0:T(8,128)(2,1)S(1)}, bf16[16,12416]{1,0:T(8,128)(2,1)S(1)}) custom-call(bf16[16,4096]{1,0:T(8,128)(2,1)} %own_ref, bf16[16,4096]{1,0:T(8,128)(2,1)S(1)} %collective-permute-done.up3_ref, bf16[16,4096]{1,0:T(8,128)(2,1)S(1)} %collective-permute-done.1.down3_ref, ...), custom_call_target="tpu_custom_call" | custom-call | tf_op jit(solution)/shard_map/pack/pallas_call | solution.py:99
  19.7 1.6 %collective-permute-start.2 = (bf16[16,12416]{1,0:T(8,128)(2,1)S(1)}, bf16[16,12416]{1,0:T(8,128)(2,1)S(1)}, u32[]{:S(2)}, u32[]{:S(2)}) collective-permute-start(bf16[16,12416]{1,0:T(8,128)(2,1)S(1)} %get-tuple-element.45.three), channel_id=1, source_target_pairs={{0,8},{1,9},{2,10},{3,11},{4,12},{5,13},{6,14},{7,15},{16,56},{17,... | collective-permute-start | bytes 1191944 | tf_op jit(solution)/shard_map/ppermute | solution.py:43
  21.3 0.0 collective-permute-start.3
  21.3 2.0 %collective-permute-start.4 = (bf16[16,10240]{1,0:T(8,128)(2,1)S(1)}, bf16[16,10240]{1,0:T(8,128)(2,1)S(1)}, u32[]{:S(2)}, u32[]{:S(2)}) collective-permute-start(bf16[16,10240]{1,0:T(8,128)(2,1)S(1)} %get-tuple-element.47), channel_id=1, source_target_pairs={{0,7},{1,0},{2,1},{3,2},{4,3},{5,4},{6,5},{7,6},{16,23},{17,16},{1... | collective-permute-start | bytes 983048 | tf_op jit(solution)/shard_map/ppermute | solution.py:43
  23.3 4.3 %collective-permute-done.2.three_x = bf16[16,12416]{1,0:T(8,128)(2,1)S(1)} collective-permute-done((bf16[16,12416]{1,0:T(8,128)(2,1)S(1)}, bf16[16,12416]{1,0:T(8,128)(2,1)S(1)}, u32[]{:S(2)}, u32[]{:S(2)}) %collective-permute-start.2) | collective-permute-done | bytes 397344 | tf_op jit(solution)/shard_map/ppermute | solution.py:43
  27.7 0.1 copy.10
  27.8 3.6 %collective-permute-done.3.up = bf16[16,10240]{1,0:T(8,128)(2,1)S(1)} collective-permute-done((bf16[16,10240]{1,0:T(8,128)(2,1)S(1)}, bf16[16,10240]{1,0:T(8,128)(2,1)S(1)}, u32[]{:S(2)}, u32[]{:S(2)}) %collective-permute-start.3) | collective-permute-done | bytes 327712 | tf_op jit(solution)/shard_map/ppermute | solution.py:43
  31.4 0.9 collective-permute-done.4.down
  32.4 0.2 collective-permute-start.5
  32.6 1.8 %collective-permute-start.6 = (bf16[16,10240]{1,0:T(8,128)(2,1)S(1)}, bf16[16,10240]{1,0:T(8,128)(2,1)S(1)}, u32[]{:S(2)}, u32[]{:S(2)}) collective-permute-start(bf16[16,10240]{1,0:T(8,128)(2,1)S(1)} %collective-permute-done.4.down), channel_id=1, source_target_pairs={{0,8},{1,9},{2,10},{3,11},{4,12},{5,13},{6,14},{7,15},{16,56},{17,... | collective-permute-start | bytes 983048 | tf_op jit(solution)/shard_map/ppermute | solution.py:43
  35.1 7.4 %label_rows.1 = (bf16[2048,4096]{1,0:T(8,128)(2,1)S(1)}, bf16[128,4096]{1,0:T(8,128)(2,1)S(1)}, bf16[80,4096]{1,0:T(8,128)(2,1)S(1)}, bf16[48,4096]{1,0:T(8,128)(2,1)S(1)}) custom-call(s32[256,1]{1,0:T(8,128)S(1)} %broadcast_subtract_fusion.lab_ref, bf16[2048,4096]{1,0:T(8,128)(2,1)} %mem_ref.1), custom_call_target="tpu_custom_call" | custom-call | flops 1024 | bytes 1024 | tf_op jit(solution)/shard_map/label_rows/pallas_call | solution.py:248
  42.5 0.5 collective-permute-start.8
  43.0 0.0 collective-permute-done.5.up_x
  43.0 0.0 collective-permute-done.6.down_x
  43.0 0.0 copy-done
  43.0 5.5 %logits.1 = (bf16[256,2048]{1,0:T(8,128)(2,1)S(1)}, f32[8,128]{1,0:T(8,128)S(1)}) custom-call(f32[1]{0:T(128)} %exp.3.scale_ref, s32[1]{0:T(128)} %bitcast.5.shift_ref, bf16[16,12416]{1,0:T(8,128)(2,1)S(1)} %get-tuple-element.45.three, bf16[16,10240]{1,0:T(8,128)(2,1)S(1)} %collective-permute-done.3.up, bf16[16,10240]{1,0:T(8,128)(2,1)S(1)} %collective-permute-done.4.down, ...), custom_call_target="tpu_custom_call" | custom-call | flops 4294967296 | bytes 16777216 | tf_op jit(solution)/shard_map/logits/pallas_call | solution.py:164
  48.5 1.8 %collective-permute-start.7 = (f32[8,128]{1,0:T(8,128)S(1)}, f32[8,128]{1,0:T(8,128)S(1)}, u32[]{:S(2)}, u32[]{:S(2)}) collective-permute-start(f32[8,128]{1,0:T(8,128)S(1)} %get-tuple-element.52), channel_id=1, source_target_pairs={{0,8},{1,9},{2,10},{3,11},{4,12},{5,13},{6,14},{7,15},{16,56},{17,... | collective-permute-start | bytes 12296 | tf_op jit(solution)/shard_map/ppermute | solution.py:43
  50.3 4.5 %weighted.1 = (f32[128,4096]{1,0:T(8,128)S(1)}, bf16[80,4096]{1,0:T(8,128)(2,1)S(1)}, bf16[96,4096]{1,0:T(8,128)(2,1)S(1)}) custom-call(bf16[256,2048]{1,0:T(8,128)(2,1)S(1)} %get-tuple-element.53.e_ref, bf16[2048,4096]{1,0:T(8,128)(2,1)S(1)} %get-tuple-element.51.mem_ref, bf16[48,4096]{1,0:T(8,128)(2,1)S(1)} %get-tuple-element.54.g_ref), custom_call_target="tpu_custom_call" | custom-call | flops 4294967296 | bytes 16777216 | tf_op jit(solution)/shard_map/weighted/pallas_call | solution.py:206
  54.8 0.0 copy-start.1
  54.8 0.0 collective-permute-done.7
  54.8 0.0 collective-permute-done.8.gr_ref
  54.9 1.8 %collective-permute-start.9 = (f32[2,8,128]{2,1,0:T(8,128)S(1)}, f32[2,8,128]{2,1,0:T(8,128)S(1)}, u32[]{:S(2)}, u32[]{:S(2)}) collective-permute-start(f32[2,8,128]{2,1,0:T(8,128)S(1)} %get-tuple-element.85), channel_id=1, source_target_pairs={{0,1},{1,2},{2,3},{3,4},{4,5},{5,6},{6,7},{7,0},{16,17},{17,18},{1... | collective-permute-start | bytes 24584 | tf_op jit(solution)/shard_map/ppermute | solution.py:43
  56.7 0.1 pad_add_fusion.2.place_ref
  56.8 0.3 collective-permute-start.10
  57.1 0.2 collective-permute-start.13
  57.3 1.3 %collective-permute-done.9 = f32[2,8,128]{2,1,0:T(8,128)S(1)} collective-permute-done((f32[2,8,128]{2,1,0:T(8,128)S(1)}, f32[2,8,128]{2,1,0:T(8,128)S(1)}, u32[]{:S(2)}, u32[]{:S(2)}) %collective-permute-start.9) | collective-permute-done | bytes 8224 | tf_op jit(solution)/shard_map/ppermute | solution.py:43
  58.6 1.2 %collective-permute-start.12 = (f32[2,2,8,128]{3,2,1,0:T(8,128)S(1)}, f32[2,2,8,128]{3,2,1,0:T(8,128)S(1)}, u32[]{:S(2)}, u32[]{:S(2)}) collective-permute-start(f32[2,2,8,128]{3,2,1,0:T(8,128)S(1)} %pad_maximum_fusion.1), channel_id=1, source_target_pairs={{0,5},{1,6},{2,7},{3,0},{4,1},{5,2},{6,3},{7,4},{16,21},{17,22},{1... | collective-permute-start | bytes 49160 | tf_op jit(solution)/shard_map/ppermute | solution.py:43
  59.8 0.6 collective-permute-done.10
  60.4 3.2 %collective-permute-start.11 = (f32[3,2,8,128]{3,2,1,0:T(8,128)S(1)}, f32[3,2,8,128]{3,2,1,0:T(8,128)S(1)}, u32[]{:S(2)}, u32[]{:S(2)}) collective-permute-start(f32[3,2,8,128]{3,2,1,0:T(8,128)S(1)} %pad_maximum_fusion.mid_ref), channel_id=1, source_target_pairs={{0,3},{1,4},{2,5},{3,6},{4,7},{5,0},{6,1},{7,2},{16,19},{17,20},{1... | collective-permute-start | bytes 73736 | tf_op jit(solution)/shard_map/ppermute | solution.py:43
  63.7 1.7 %collective-permute-done.12.down_ref = f32[2,2,8,128]{3,2,1,0:T(8,128)S(1)} collective-permute-done((f32[2,2,8,128]{3,2,1,0:T(8,128)S(1)}, f32[2,2,8,128]{3,2,1,0:T(8,128)S(1)}, u32[]{:S(2)}, u32[]{:S(2)}) %collective-permute-start.12) | collective-permute-done | bytes 16416 | tf_op jit(solution)/shard_map/ppermute | solution.py:43
  65.3 1.9 %collective-permute-done.11.up_ref = f32[3,2,8,128]{3,2,1,0:T(8,128)S(1)} collective-permute-done((f32[3,2,8,128]{3,2,1,0:T(8,128)S(1)}, f32[3,2,8,128]{3,2,1,0:T(8,128)S(1)}, u32[]{:S(2)}, u32[]{:S(2)}) %collective-permute-start.11) | collective-permute-done | bytes 24608 | tf_op jit(solution)/shard_map/ppermute | solution.py:43
  67.3 0.4 collective-permute-start.18
  67.6 0.8 merge.1
  68.4 0.0 collective-permute-done.13.r_ref
  68.4 0.5 mix.1
  68.9 1.8 %collective-permute-start.14 = (bf16[16,10240]{1,0:T(8,128)(2,1)S(1)}, bf16[16,10240]{1,0:T(8,128)(2,1)S(1)}, u32[]{:S(2)}, u32[]{:S(2)}) collective-permute-start(bf16[16,10240]{1,0:T(8,128)(2,1)S(1)} %get-tuple-element.67), channel_id=1, source_target_pairs={{0,1},{1,2},{2,3},{3,4},{4,5},{5,6},{6,7},{7,0},{16,17},{17,18},{1... | collective-permute-start | bytes 983048 | tf_op jit(solution)/shard_map/ppermute | solution.py:43
  70.7 0.3 collective-permute-start.15
  71.0 1.0 %collective-permute-start.16 = (f32[8,128]{1,0:T(8,128)S(1)}, f32[8,128]{1,0:T(8,128)S(1)}, u32[]{:S(2)}, u32[]{:S(2)}) collective-permute-start(f32[8,128]{1,0:T(8,128)S(1)} %get-tuple-element.69), channel_id=1, source_target_pairs={{0,40},{1,41},{2,42},{3,43},{4,44},{5,45},{6,46},{7,47},{16,24},{1... | collective-permute-start | bytes 12296 | tf_op jit(solution)/shard_map/ppermute | solution.py:43
  72.0 3.9 %collective-permute-done.16 = f32[8,128]{1,0:T(8,128)S(1)} collective-permute-done((f32[8,128]{1,0:T(8,128)S(1)}, f32[8,128]{1,0:T(8,128)S(1)}, u32[]{:S(2)}, u32[]{:S(2)}) %collective-permute-start.16) | collective-permute-done | bytes 4128 | tf_op jit(solution)/shard_map/ppermute | solution.py:43
  76.0 0.0 collective-permute-start.17
  76.0 1.2 %collective-permute-done.17 = f32[8,128]{1,0:T(8,128)S(1)} collective-permute-done((f32[8,128]{1,0:T(8,128)S(1)}, f32[8,128]{1,0:T(8,128)S(1)}, u32[]{:S(2)}, u32[]{:S(2)}) %collective-permute-start.17) | collective-permute-done | bytes 4128 | tf_op jit(solution)/shard_map/ppermute | solution.py:43
  77.1 2.2 %collective-permute-done.18.r_ref = bf16[96,4096]{1,0:T(8,128)(2,1)S(1)} collective-permute-done((bf16[96,4096]{1,0:T(8,128)(2,1)S(1)}, bf16[96,4096]{1,0:T(8,128)(2,1)S(1)}, u32[]{:S(2)}, u32[]{:S(2)}) %collective-permute-start.18) | collective-permute-done | bytes 786464 | tf_op jit(solution)/shard_map/ppermute | solution.py:43
  79.3 0.3 rest.1
  79.6 0.0 collective-permute-done.14
  79.6 1.3 %collective-permute-done.15 = bf16[16,10240]{1,0:T(8,128)(2,1)S(1)} collective-permute-done((bf16[16,10240]{1,0:T(8,128)(2,1)S(1)}, bf16[16,10240]{1,0:T(8,128)(2,1)S(1)}, u32[]{:S(2)}, u32[]{:S(2)}) %collective-permute-start.15) | collective-permute-done | bytes 327712 | tf_op jit(solution)/shard_map/ppermute | solution.py:43
  80.9 0.1 add_convert_fusion
  81.0 3.4 %collective-permute-start.19 = (bf16[16,4096]{1,0:T(8,128)(2,1)S(1)}, bf16[16,4096]{1,0:T(8,128)(2,1)S(1)}, u32[]{:S(2)}, u32[]{:S(2)}) collective-permute-start(bf16[16,4096]{1,0:T(8,128)(2,1)S(1)} %get-tuple-element.79), channel_id=1, source_target_pairs={{0,3},{1,4},{2,5},{3,6},{4,7},{5,0},{6,1},{7,2},{16,19},{17,20},{1... | collective-permute-start | bytes 393224 | tf_op jit(solution)/shard_map/ppermute | solution.py:43
  84.4 1.7 %collective-permute-start.20 = (bf16[16,4096]{1,0:T(8,128)(2,1)S(1)}, bf16[16,4096]{1,0:T(8,128)(2,1)S(1)}, u32[]{:S(2)}, u32[]{:S(2)}) collective-permute-start(bf16[16,4096]{1,0:T(8,128)(2,1)S(1)} %get-tuple-element.82), channel_id=1, source_target_pairs={{0,5},{1,6},{2,7},{3,0},{4,1},{5,2},{6,3},{7,4},{16,21},{17,22},{1... | collective-permute-start | bytes 393224 | tf_op jit(solution)/shard_map/ppermute | solution.py:43
  86.1 1.6 %collective-permute-start.21 = (f32[8,128]{1,0:T(8,128)S(1)}, f32[8,128]{1,0:T(8,128)S(1)}, u32[]{:S(2)}, u32[]{:S(2)}) collective-permute-start(f32[8,128]{1,0:T(8,128)S(1)} %add.79), channel_id=1, source_target_pairs={{0,64},{1,65},{2,66},{3,67},{4,68},{5,69},{6,70},{7,71},{16,80},{1... | collective-permute-start | bytes 12296 | tf_op jit(solution)/shard_map/ppermute | solution.py:43
  87.7 2.0 %collective-permute-done.21 = f32[8,128]{1,0:T(8,128)S(1)} collective-permute-done((f32[8,128]{1,0:T(8,128)S(1)}, f32[8,128]{1,0:T(8,128)S(1)}, u32[]{:S(2)}, u32[]{:S(2)}) %collective-permute-start.21) | collective-permute-done | bytes 4128 | tf_op jit(solution)/shard_map/ppermute | solution.py:43
  89.7 3.2 %collective-permute-start.22 = (f32[8,128]{1,0:T(8,128)S(1)}, f32[8,128]{1,0:T(8,128)S(1)}, u32[]{:S(2)}, u32[]{:S(2)}) collective-permute-start(f32[8,128]{1,0:T(8,128)S(1)} %add.89), channel_id=1, source_target_pairs={{0,128},{1,129},{2,130},{3,131},{4,132},{5,133},{6,134},{7,135},{1... | collective-permute-start | bytes 12296 | tf_op jit(solution)/shard_map/ppermute | solution.py:43
  92.9 1.9 %collective-permute-done.22 = f32[8,128]{1,0:T(8,128)S(1)} collective-permute-done((f32[8,128]{1,0:T(8,128)S(1)}, f32[8,128]{1,0:T(8,128)S(1)}, u32[]{:S(2)}, u32[]{:S(2)}) %collective-permute-start.22) | collective-permute-done | bytes 4128 | tf_op jit(solution)/shard_map/ppermute | solution.py:43
  94.9 0.5 slice.53
  96.0 0.0 collective-permute-done.19
  96.0 0.1 dynamic-slice_multiply_fusion
  96.1 1.5 %collective-permute-done.20 = bf16[16,4096]{1,0:T(8,128)(2,1)S(1)} collective-permute-done((bf16[16,4096]{1,0:T(8,128)(2,1)S(1)}, bf16[16,4096]{1,0:T(8,128)(2,1)S(1)}, u32[]{:S(2)}, u32[]{:S(2)}) %collective-permute-start.20) | collective-permute-done | bytes 131104 | tf_op jit(solution)/shard_map/ppermute | solution.py:43
  97.6 0.7 multiply_convert_fusion
  (17 shorter events, 0.1 us)
Async XLA Ops:
  0.6 42.4 %copy-start = (s32[2048]{0:T(1024)S(1)}, s32[2048]{0:T(1024)}, u32[]{:S(2)}) copy-start(s32[2048]{0:T(1024)} %param.10) | copy-start | bytes 24580
  0.6 14.8 %collective-permute-start = (bf16[16,4096]{1,0:T(8,128)(2,1)}, bf16[16,4096]{1,0:T(8,128)(2,1)S(1)}, u32[]{:S(2)}, u32[]{:S(2)}) collective-permute-start(bf16[16,4096]{1,0:T(8,128)(2,1)} %own_ref), channel_id=1, source_target_pairs={{0,3},{1,4},{2,5},{3,6},{4,7},{5,0},{6,1},{7,2},{16,19},{17,20},{1... | collective-permute-start | bytes 393224 | tf_op jit(solution)/shard_map/ppermute | solution.py:43
  6.6 12.1 %collective-permute-start.1 = (bf16[16,4096]{1,0:T(8,128)(2,1)}, bf16[16,4096]{1,0:T(8,128)(2,1)S(1)}, u32[]{:S(2)}, u32[]{:S(2)}) collective-permute-start(bf16[16,4096]{1,0:T(8,128)(2,1)} %own_ref), channel_id=1, source_target_pairs={{0,5},{1,6},{2,7},{3,0},{4,1},{5,2},{6,3},{7,4},{16,21},{17,22},{1... | collective-permute-start | bytes 393224 | tf_op jit(solution)/shard_map/ppermute | solution.py:43
  19.7 7.9 %collective-permute-start.2 = (bf16[16,12416]{1,0:T(8,128)(2,1)S(1)}, bf16[16,12416]{1,0:T(8,128)(2,1)S(1)}, u32[]{:S(2)}, u32[]{:S(2)}) collective-permute-start(bf16[16,12416]{1,0:T(8,128)(2,1)S(1)} %get-tuple-element.45.three), channel_id=1, source_target_pairs={{0,8},{1,9},{2,10},{3,11},{4,12},{5,13},{6,14},{7,15},{16,56},{17,... | collective-permute-start | bytes 1191944 | tf_op jit(solution)/shard_map/ppermute | solution.py:43
  21.3 10.1 %collective-permute-start.3 = (bf16[16,10240]{1,0:T(8,128)(2,1)S(1)}, bf16[16,10240]{1,0:T(8,128)(2,1)S(1)}, u32[]{:S(2)}, u32[]{:S(2)}) collective-permute-start(bf16[16,10240]{1,0:T(8,128)(2,1)S(1)} %get-tuple-element.46), channel_id=1, source_target_pairs={{0,1},{1,2},{2,3},{3,4},{4,5},{5,6},{6,7},{7,0},{16,17},{17,18},{1... | collective-permute-start | bytes 983048 | tf_op jit(solution)/shard_map/ppermute | solution.py:43
  21.3 11.0 %collective-permute-start.4 = (bf16[16,10240]{1,0:T(8,128)(2,1)S(1)}, bf16[16,10240]{1,0:T(8,128)(2,1)S(1)}, u32[]{:S(2)}, u32[]{:S(2)}) collective-permute-start(bf16[16,10240]{1,0:T(8,128)(2,1)S(1)} %get-tuple-element.47), channel_id=1, source_target_pairs={{0,7},{1,0},{2,1},{3,2},{4,3},{5,4},{6,5},{7,6},{16,23},{17,16},{1... | collective-permute-start | bytes 983048 | tf_op jit(solution)/shard_map/ppermute | solution.py:43
  32.4 10.6 %collective-permute-start.5 = (bf16[16,10240]{1,0:T(8,128)(2,1)S(1)}, bf16[16,10240]{1,0:T(8,128)(2,1)S(1)}, u32[]{:S(2)}, u32[]{:S(2)}) collective-permute-start(bf16[16,10240]{1,0:T(8,128)(2,1)S(1)} %collective-permute-done.3.up), channel_id=1, source_target_pairs={{0,8},{1,9},{2,10},{3,11},{4,12},{5,13},{6,14},{7,15},{16,56},{17,... | collective-permute-start | bytes 983048 | tf_op jit(solution)/shard_map/ppermute | solution.py:43
  32.6 10.4 %collective-permute-start.6 = (bf16[16,10240]{1,0:T(8,128)(2,1)S(1)}, bf16[16,10240]{1,0:T(8,128)(2,1)S(1)}, u32[]{:S(2)}, u32[]{:S(2)}) collective-permute-start(bf16[16,10240]{1,0:T(8,128)(2,1)S(1)} %collective-permute-done.4.down), channel_id=1, source_target_pairs={{0,8},{1,9},{2,10},{3,11},{4,12},{5,13},{6,14},{7,15},{16,56},{17,... | collective-permute-start | bytes 983048 | tf_op jit(solution)/shard_map/ppermute | solution.py:43
  42.5 12.4 %collective-permute-start.8 = (bf16[80,4096]{1,0:T(8,128)(2,1)S(1)}, bf16[80,4096]{1,0:T(8,128)(2,1)S(1)}, u32[]{:S(2)}, u32[]{:S(2)}) collective-permute-start(bf16[80,4096]{1,0:T(8,128)(2,1)S(1)} %get-tuple-element.57), channel_id=1, source_target_pairs={{0,8},{1,9},{2,10},{3,11},{4,12},{5,13},{6,14},{7,15},{16,56},{17,... | collective-permute-start | bytes 1966088 | tf_op jit(solution)/shard_map/ppermute | solution.py:43
  48.5 6.4 %collective-permute-start.7 = (f32[8,128]{1,0:T(8,128)S(1)}, f32[8,128]{1,0:T(8,128)S(1)}, u32[]{:S(2)}, u32[]{:S(2)}) collective-permute-start(f32[8,128]{1,0:T(8,128)S(1)} %get-tuple-element.52), channel_id=1, source_target_pairs={{0,8},{1,9},{2,10},{3,11},{4,12},{5,13},{6,14},{7,15},{16,56},{17,... | collective-permute-start | bytes 12296 | tf_op jit(solution)/shard_map/ppermute | solution.py:43
  54.8 41.2 %copy-start.1 = (f32[256]{0:T(256)S(1)}, f32[256]{0:T(256)}, u32[]{:S(2)}) copy-start(f32[256]{0:T(256)} %param.11) | copy-start | bytes 3076
  54.9 3.7 %collective-permute-start.9 = (f32[2,8,128]{2,1,0:T(8,128)S(1)}, f32[2,8,128]{2,1,0:T(8,128)S(1)}, u32[]{:S(2)}, u32[]{:S(2)}) collective-permute-start(f32[2,8,128]{2,1,0:T(8,128)S(1)} %get-tuple-element.85), channel_id=1, source_target_pairs={{0,1},{1,2},{2,3},{3,4},{4,5},{5,6},{6,7},{7,0},{16,17},{17,18},{1... | collective-permute-start | bytes 24584 | tf_op jit(solution)/shard_map/ppermute | solution.py:43
  56.8 3.7 %collective-permute-start.10 = (f32[2,8,128]{2,1,0:T(8,128)S(1)}, f32[2,8,128]{2,1,0:T(8,128)S(1)}, u32[]{:S(2)}, u32[]{:S(2)}) collective-permute-start(f32[2,8,128]{2,1,0:T(8,128)S(1)} %get-tuple-element.85), channel_id=1, source_target_pairs={{0,7},{1,0},{2,1},{3,2},{4,3},{5,4},{6,5},{7,6},{16,23},{17,16},{1... | collective-permute-start | bytes 24584 | tf_op jit(solution)/shard_map/ppermute | solution.py:43
  57.1 11.4 %collective-permute-start.13 = (bf16[80,4096]{1,0:T(8,128)(2,1)S(1)}, bf16[80,4096]{1,0:T(8,128)(2,1)S(1)}, u32[]{:S(2)}, u32[]{:S(2)}) collective-permute-start(bf16[80,4096]{1,0:T(8,128)(2,1)S(1)} %get-tuple-element.64), channel_id=1, source_target_pairs={{0,8},{1,9},{2,10},{3,11},{4,12},{5,13},{6,14},{7,15},{16,56},{17,... | collective-permute-start | bytes 1966088 | tf_op jit(solution)/shard_map/ppermute | solution.py:43
  58.6 6.7 %collective-permute-start.12 = (f32[2,2,8,128]{3,2,1,0:T(8,128)S(1)}, f32[2,2,8,128]{3,2,1,0:T(8,128)S(1)}, u32[]{:S(2)}, u32[]{:S(2)}) collective-permute-start(f32[2,2,8,128]{3,2,1,0:T(8,128)S(1)} %pad_maximum_fusion.1), channel_id=1, source_target_pairs={{0,5},{1,6},{2,7},{3,0},{4,1},{5,2},{6,3},{7,4},{16,21},{17,22},{1... | collective-permute-start | bytes 49160 | tf_op jit(solution)/shard_map/ppermute | solution.py:43
  60.4 6.9 %collective-permute-start.11 = (f32[3,2,8,128]{3,2,1,0:T(8,128)S(1)}, f32[3,2,8,128]{3,2,1,0:T(8,128)S(1)}, u32[]{:S(2)}, u32[]{:S(2)}) collective-permute-start(f32[3,2,8,128]{3,2,1,0:T(8,128)S(1)} %pad_maximum_fusion.mid_ref), channel_id=1, source_target_pairs={{0,3},{1,4},{2,5},{3,6},{4,7},{5,0},{6,1},{7,2},{16,19},{17,20},{1... | collective-permute-start | bytes 73736 | tf_op jit(solution)/shard_map/ppermute | solution.py:43
  67.3 12.0 %collective-permute-start.18 = (bf16[96,4096]{1,0:T(8,128)(2,1)S(1)}, bf16[96,4096]{1,0:T(8,128)(2,1)S(1)}, u32[]{:S(2)}, u32[]{:S(2)}) collective-permute-start(bf16[96,4096]{1,0:T(8,128)(2,1)S(1)} %get-tuple-element.70), channel_id=1, source_target_pairs={{0,8},{1,9},{2,10},{3,11},{4,12},{5,13},{6,14},{7,15},{16,56},{17,... | collective-permute-start | bytes 2359304 | tf_op jit(solution)/shard_map/ppermute | solution.py:43
  68.9 10.7 %collective-permute-start.14 = (bf16[16,10240]{1,0:T(8,128)(2,1)S(1)}, bf16[16,10240]{1,0:T(8,128)(2,1)S(1)}, u32[]{:S(2)}, u32[]{:S(2)}) collective-permute-start(bf16[16,10240]{1,0:T(8,128)(2,1)S(1)} %get-tuple-element.67), channel_id=1, source_target_pairs={{0,1},{1,2},{2,3},{3,4},{4,5},{5,6},{6,7},{7,0},{16,17},{17,18},{1... | collective-permute-start | bytes 983048 | tf_op jit(solution)/shard_map/ppermute | solution.py:43
  70.7 10.2 %collective-permute-start.15 = (bf16[16,10240]{1,0:T(8,128)(2,1)S(1)}, bf16[16,10240]{1,0:T(8,128)(2,1)S(1)}, u32[]{:S(2)}, u32[]{:S(2)}) collective-permute-start(bf16[16,10240]{1,0:T(8,128)(2,1)S(1)} %get-tuple-element.68), channel_id=1, source_target_pairs={{0,7},{1,0},{2,1},{3,2},{4,3},{5,4},{6,5},{7,6},{16,23},{17,16},{1... | collective-permute-start | bytes 983048 | tf_op jit(solution)/shard_map/ppermute | solution.py:43
  71.0 4.9 %collective-permute-start.16 = (f32[8,128]{1,0:T(8,128)S(1)}, f32[8,128]{1,0:T(8,128)S(1)}, u32[]{:S(2)}, u32[]{:S(2)}) collective-permute-start(f32[8,128]{1,0:T(8,128)S(1)} %get-tuple-element.69), channel_id=1, source_target_pairs={{0,40},{1,41},{2,42},{3,43},{4,44},{5,45},{6,46},{7,47},{16,24},{1... | collective-permute-start | bytes 12296 | tf_op jit(solution)/shard_map/ppermute | solution.py:43
  76.0 1.2 %collective-permute-start.17 = (f32[8,128]{1,0:T(8,128)S(1)}, f32[8,128]{1,0:T(8,128)S(1)}, u32[]{:S(2)}, u32[]{:S(2)}) collective-permute-start(f32[8,128]{1,0:T(8,128)S(1)} %add.78), channel_id=1, source_target_pairs={{0,16},{1,17},{2,18},{3,19},{4,20},{5,21},{6,22},{7,23},{16,0},{17... | collective-permute-start | bytes 12296 | tf_op jit(solution)/shard_map/ppermute | solution.py:43
  81.0 15.0 %collective-permute-start.19 = (bf16[16,4096]{1,0:T(8,128)(2,1)S(1)}, bf16[16,4096]{1,0:T(8,128)(2,1)S(1)}, u32[]{:S(2)}, u32[]{:S(2)}) collective-permute-start(bf16[16,4096]{1,0:T(8,128)(2,1)S(1)} %get-tuple-element.79), channel_id=1, source_target_pairs={{0,3},{1,4},{2,5},{3,6},{4,7},{5,0},{6,1},{7,2},{16,19},{17,20},{1... | collective-permute-start | bytes 393224 | tf_op jit(solution)/shard_map/ppermute | solution.py:43
  84.4 13.2 %collective-permute-start.20 = (bf16[16,4096]{1,0:T(8,128)(2,1)S(1)}, bf16[16,4096]{1,0:T(8,128)(2,1)S(1)}, u32[]{:S(2)}, u32[]{:S(2)}) collective-permute-start(bf16[16,4096]{1,0:T(8,128)(2,1)S(1)} %get-tuple-element.82), channel_id=1, source_target_pairs={{0,5},{1,6},{2,7},{3,0},{4,1},{5,2},{6,3},{7,4},{16,21},{17,22},{1... | collective-permute-start | bytes 393224 | tf_op jit(solution)/shard_map/ppermute | solution.py:43
  86.1 3.6 %collective-permute-start.21 = (f32[8,128]{1,0:T(8,128)S(1)}, f32[8,128]{1,0:T(8,128)S(1)}, u32[]{:S(2)}, u32[]{:S(2)}) collective-permute-start(f32[8,128]{1,0:T(8,128)S(1)} %add.79), channel_id=1, source_target_pairs={{0,64},{1,65},{2,66},{3,67},{4,68},{5,69},{6,70},{7,71},{16,80},{1... | collective-permute-start | bytes 12296 | tf_op jit(solution)/shard_map/ppermute | solution.py:43
  89.7 5.1 %collective-permute-start.22 = (f32[8,128]{1,0:T(8,128)S(1)}, f32[8,128]{1,0:T(8,128)S(1)}, u32[]{:S(2)}, u32[]{:S(2)}) collective-permute-start(f32[8,128]{1,0:T(8,128)S(1)} %add.89), channel_id=1, source_target_pairs={{0,128},{1,129},{2,130},{3,131},{4,132},{5,133},{6,134},{7,135},{1... | collective-permute-start | bytes 12296 | tf_op jit(solution)/shard_map/ppermute | solution.py:43

commit v5 on v4

--- a/solution.py
+++ b/solution.py
@@ -48,12 +48,11 @@
     return send(up, along_z(k)), down
 
 
-def fill(q_scr, first, three, up, down):
+def fill(q_scr, first, own, two, up, down):
     depth = q_scr.shape[1]
     half = depth // 2
     near, next_, last = slice(0, depth), slice(depth, 2 * depth), slice(2 * depth, 2 * depth + half)
-    third = slice(2 * depth, 3 * depth)
-    places = (down, next_), (up, near), (three, near), (down, near), (up, next_), (three, third), None, (three, next_)
+    places = (down, next_), (up, near), (own, near), (down, near), (up, next_), (two, next_), None, (two, near)
     for k, place in enumerate(places):
         if place is not None:
             q_scr[first + 16 * k:first + 16 * k + 16, :] = place[0][:, place[1]]
@@ -61,21 +60,36 @@
     q_scr[first + 96:first + 112, half:] = down[:, last]
 
 
-def pack_kernel(own_ref, up3_ref, down3_ref, lab_ref, cot_ref, up_ref, down_ref, three_ref, sems):
+def stage_kernel(own_ref, lab_ref, out_ref, sem):
+    copy = pltpu.make_async_copy(own_ref, out_ref, sem)
+    copy.start()
+    copy.wait()
+
+
+def stage_call(own, lab):
+    return pl.pallas_call(
+        stage_kernel,
+        in_specs=[hbm(), vmem()],
+        out_specs=vmem(),
+        out_shape=pltpu.VMEM(own.shape, own.dtype),
+        scratch_shapes=[pltpu.SemaphoreType.DMA],
+        compiler_params=params(4),
+        name="stage",
+    )(pltpu.with_memory_space_constraint(own, pltpu.HBM), lab)
+
+
+def pack_kernel(own_ref, up3_ref, down3_ref, lab_ref, cot_ref, up_ref, down_ref, three_ref, two_ref):
     f32, bf16 = jnp.float32, jnp.bfloat16
     depth = up3_ref.shape[1]
     half = depth // 2
-    copies = [
-        pltpu.make_async_copy(own_ref, ref.at[:, pl.ds(0, depth)], sems.at[k]) for k, ref in enumerate((up_ref, down_ref, three_ref))
-    ]
-    for copy in copies:
-        copy.start()
+    for ref in (up_ref, down_ref, three_ref, two_ref):
+        ref[:, :depth] = own_ref[...]
     up_ref[:, depth:2 * depth] = down3_ref[...]
     up_ref[:, 2 * depth:] = up3_ref[:, :half]
     down_ref[:, depth:2 * depth] = up3_ref[...]
     down_ref[:, 2 * depth:] = down3_ref[:, half:]
-    three_ref[:, depth:2 * depth] = up3_ref[...]
-    three_ref[:, 2 * depth:3 * depth] = down3_ref[...]
+    two_ref[:, :depth] = up3_ref[...]
+    two_ref[:, depth:] = down3_ref[...]
     label = lab_ref[...]
     high = lax.shift_right_logical(label, 8)
     rest = cot_ref[...]
@@ -88,9 +102,7 @@
     note = jnp.zeros((16, 128), f32)
     for k, term in enumerate(terms):
         note = jnp.where(row == k, term, note)
-    three_ref[:, 3 * depth:] = note.astype(bf16)
-    for copy in copies:
-        copy.wait()
+    three_ref[:, depth:] = note.astype(bf16)
 
 
 def pack_call(own, up3, down3, lab, cot):
@@ -98,19 +110,18 @@
     wide = 2 * depth + depth // 2
     return pl.pallas_call(
         pack_kernel,
-        in_specs=[hbm()] + [vmem()] * 4,
-        out_specs=[vmem()] * 3,
-        out_shape=[jax.ShapeDtypeStruct((rows, k), jnp.bfloat16) for k in (wide, wide, 3 * depth + 128)],
-        scratch_shapes=[pltpu.SemaphoreType.DMA((3,))],
+        in_specs=[vmem()] * 5,
+        out_specs=[vmem()] * 4,
+        out_shape=[jax.ShapeDtypeStruct((rows, k), jnp.bfloat16) for k in (wide, wide, depth + 128, 2 * depth)],
         compiler_params=params(4),
         name="pack",
-    )(pltpu.with_memory_space_constraint(own, pltpu.HBM), up3, down3, lab, cot)
-
-
-def logits_kernel(scale_ref, shift_ref, three, up, down, three_x, up_x, down_x,
+    )(own, up3, down3, lab, cot)
+
+
+def logits_kernel(scale_ref, shift_ref, own, two, up, down, own_x, two_x, up_x, down_x,
                   mem_ref, lab_ref, valid_ref, e_ref, stat_ref, q_scr, l_scr):
-    fill(q_scr, 0, three, up, down)
-    fill(q_scr, 128, three_x, up_x, down_x)
+    fill(q_scr, 0, own, two, up, down)
+    fill(q_scr, 128, own_x, two_x, up_x, down_x)
     rows, n = l_scr.shape
     scale = scale_ref[0]
     top = jnp.full((rows, 1), NEG, jnp.float32)
@@ -380,19 +391,21 @@
     own_labels = lax.dynamic_slice_in_dim(labels, x_lo * 128, 128)
     own_cot = lax.dynamic_slice_in_dim(cotangent, x_lo * 128, 128)
     rolled = lax.dynamic_slice_in_dim(jnp.concatenate([own_labels, own_labels]), roll_by, 128)
-    up3, late_queries = together(up3, queries)
-    to_up, to_down, to_x = pack_call(late_queries, up3, down3, rolled[None, :], own_cot[None, :])
+    staged = stage_call(queries, rolled[None, :])
+    up3, staged = together(up3, staged)
+    to_up, to_down, to_x, to_x2 = pack_call(staged, up3, down3, rolled[None, :], own_cot[None, :])
     up, down = both(to_up, to_down, 1)
     three_x = send(to_x, PARTNER)
-    note = three_x[:, 3 * depth:].astype(f32)
+    two_x = send(to_x2, PARTNER)
+    up, down, three_x, two_x = together(up, down, three_x, two_x)
+    note = three_x[:, depth:].astype(f32)
     lab = (jnp.concatenate([rolled, (note[0] * 256.0 + note[1]).astype(jnp.int32)]) - start_row)[:, None]
     cots = jnp.stack([own_cot, (note[2] + note[3]) + note[4]])
-    up, down, lab = together(up, down, lab)
     up_x, down_x = send(up, PARTNER), send(down, PARTNER)
     resident, g, g_first, g_second = labels_call(lab, memory)
     resident = pltpu.with_memory_space_constraint(resident, pltpu.VMEM)
     g_first_x = send(g_first, PARTNER)
-    blocks = (to_x, up, down, three_x, up_x, down_x)
+    blocks = (to_x, to_x2, up, down, three_x, two_x, up_x, down_x)
 
     e, stat = logits_call(scale, roll_by.reshape(1), blocks, resident, lab, valid[None, :])
     stat_other = send(stat, PARTNER)

time: 99.7 us -> 95.1 us (0.954)
  waiting for transfers between devices: 38.7 us -> 29.4 us
  starting transfers between devices: 34.1 us -> 38.6 us
    ppermute x23 -> x24, waiting for transfers between devices: 38.7 us -> 29.4 us  [send(): return lax.ppermute(x, AXES, pairs)]
    ppermute x23 -> x24, starting transfers between devices: 34.1 us -> 38.6 us  [send(): return lax.ppermute(x, AXES, pairs)]
  transfers between devices with their start and end apart: 23 -> 24, of which waited for: 16 -> 13; matrix products, arithmetic and copies ran while one was open for 2% -> 3% of each run, Pallas kernels for 19% -> 21%
where the time goes in v5:
time: 95.1 us; the launch traced here: 94.6 us
  starting transfers between devices  38.6 us (41%)
  waiting for transfers between devices  29.4 us (31%)
  Pallas kernels  20 us (21%)
  between operations  3.28 us (3%)
  local copies, waits for them, and re-layouts  2.26 us (2%)
  other arithmetic  1.04 us (1%)
    ppermute x24, starting transfers between devices, send(): return lax.ppermute(x, AXES, pairs)  38.6 us
    ppermute x24, waiting for transfers between devices, send(): return lax.ppermute(x, AXES, pairs)  29.4 us
    pallas_call x1, Pallas kernels, labels_call(): pl.pallas_call(labels_kernel, in_specs=[vmem(), hbm()], out_specs=[vmem()...  7.41 us
    pallas_call x1, Pallas kernels, logits_call(): pl.pallas_call(logits_kernel, in_specs=[smem(), smem()] + [vmem()] * (len...  5.48 us
    pallas_call x1, Pallas kernels, weighted_call(): pl.pallas_call(weighted_kernel, in_specs=[vmem()] * 3, out_specs=[vmem()]...  4.52 us
  transfers between devices with their start and end apart: 24, of which 13 were waited for; matrix products, arithmetic and copies ran while one was open for 3% of the time, Pallas kernels for 21%

profile of v5, /device:TPU:32, one launch (start us, length us, event | category | flops | bytes accessed | tf_op | source)
XLA Modules:
  0.0 94.6 jit_solution(17475831092114258918)
XLA Ops:
  0.6 5.9 %collective-permute-start = (bf16[16,4096]{1,0:T(8,128)(2,1)}, bf16[16,4096]{1,0:T(8,128)(2,1)S(1)}, u32[]{:S(2)}, u32[]{:S(2)}) collective-permute-start(bf16[16,4096]{1,0:T(8,128)(2,1)} %own_ref.1), channel_id=1, source_target_pairs={{0,3},{1,4},{2,5},{3,6},{4,7},{5,0},{6,1},{7,2},{16,19},{17,20},{1... | collective-permute-start | bytes 393224 | tf_op jit(solution)/shard_map/ppermute | solution.py:43
  6.6 0.1 collective-permute-start.1
  6.7 0.8 dynamic_slice.13
  7.4 0.1 dynamic-slice_bitcast_fusion.1
  7.5 0.9 stage.1.own_ref
  8.4 0.8 dynamic-slice_bitcast_fusion.cot_ref
  9.2 6.2 %collective-permute-done.up3_ref = bf16[16,4096]{1,0:T(8,128)(2,1)S(1)} collective-permute-done((bf16[16,4096]{1,0:T(8,128)(2,1)}, bf16[16,4096]{1,0:T(8,128)(2,1)S(1)}, u32[]{:S(2)}, u32[]{:S(2)}) %collective-permute-start) | collective-permute-done | bytes 131104 | tf_op jit(solution)/shard_map/ppermute | solution.py:43
  15.4 3.2 %collective-permute-done.1.down3_ref = bf16[16,4096]{1,0:T(8,128)(2,1)S(1)} collective-permute-done((bf16[16,4096]{1,0:T(8,128)(2,1)}, bf16[16,4096]{1,0:T(8,128)(2,1)S(1)}, u32[]{:S(2)}, u32[]{:S(2)}) %collective-permute-start.1) | collective-permute-done | bytes 131104 | tf_op jit(solution)/shard_map/ppermute | solution.py:43
  18.6 0.1 pack.1
  18.7 0.1 collective-permute-start.2
  18.8 2.0 %collective-permute-start.3 = (bf16[16,10240]{1,0:T(8,128)(2,1)S(1)}, bf16[16,10240]{1,0:T(8,128)(2,1)S(1)}, u32[]{:S(2)}, u32[]{:S(2)}) collective-permute-start(bf16[16,10240]{1,0:T(8,128)(2,1)S(1)} %get-tuple-element.48), channel_id=1, source_target_pairs={{0,7},{1,0},{2,1},{3,2},{4,3},{5,4},{6,5},{7,6},{16,23},{17,16},{1... | collective-permute-start | bytes 983048 | tf_op jit(solution)/shard_map/ppermute | solution.py:43
  20.8 1.5 %collective-permute-start.5 = (bf16[16,8192]{1,0:T(8,128)(2,1)S(1)}, bf16[16,8192]{1,0:T(8,128)(2,1)S(1)}, u32[]{:S(2)}, u32[]{:S(2)}) collective-permute-start(bf16[16,8192]{1,0:T(8,128)(2,1)S(1)} %get-tuple-element.50.two), channel_id=1, source_target_pairs={{0,8},{1,9},{2,10},{3,11},{4,12},{5,13},{6,14},{7,15},{16,56},{17,... | collective-permute-start | bytes 786440 | tf_op jit(solution)/shard_map/ppermute | solution.py:43
  22.3 0.5 collective-permute-start.4
  23.5 5.1 %collective-permute-done.4.own_x = bf16[16,4224]{1,0:T(8,128)(2,1)S(1)} collective-permute-done((bf16[16,4224]{1,0:T(8,128)(2,1)S(1)}, bf16[16,4224]{1,0:T(8,128)(2,1)S(1)}, u32[]{:S(2)}, u32[]{:S(2)}) %collective-permute-start.4) | collective-permute-done | bytes 135200 | tf_op jit(solution)/shard_map/ppermute | solution.py:43
  28.6 0.0 collective-permute-done.5.two_x
  28.6 0.0 collective-permute-done.2.up
  28.6 0.2 collective-permute-done.3.down
  28.9 1.6 %collective-permute-start.6 = (bf16[16,10240]{1,0:T(8,128)(2,1)S(1)}, bf16[16,10240]{1,0:T(8,128)(2,1)S(1)}, u32[]{:S(2)}, u32[]{:S(2)}) collective-permute-start(bf16[16,10240]{1,0:T(8,128)(2,1)S(1)} %collective-permute-done.2.up), channel_id=1, source_target_pairs={{0,8},{1,9},{2,10},{3,11},{4,12},{5,13},{6,14},{7,15},{16,56},{17,... | collective-permute-start | bytes 983048 | tf_op jit(solution)/shard_map/ppermute | solution.py:43
  30.4 0.5 collective-permute-start.7
  31.0 0.1 copy.10
  31.1 7.4 %label_rows.1 = (bf16[2048,4096]{1,0:T(8,128)(2,1)S(1)}, bf16[128,4096]{1,0:T(8,128)(2,1)S(1)}, bf16[80,4096]{1,0:T(8,128)(2,1)S(1)}, bf16[48,4096]{1,0:T(8,128)(2,1)S(1)}) custom-call(s32[256,1]{1,0:T(8,128)S(1)} %broadcast_subtract_fusion.lab_ref, bf16[2048,4096]{1,0:T(8,128)(2,1)} %mem_ref.1), custom_call_target="tpu_custom_call" | custom-call | flops 1024 | bytes 1024 | tf_op jit(solution)/shard_map/label_rows/pallas_call | solution.py:259
  38.6 1.8 %collective-permute-start.9 = (bf16[80,4096]{1,0:T(8,128)(2,1)S(1)}, bf16[80,4096]{1,0:T(8,128)(2,1)S(1)}, u32[]{:S(2)}, u32[]{:S(2)}) collective-permute-start(bf16[80,4096]{1,0:T(8,128)(2,1)S(1)} %get-tuple-element.61), channel_id=1, source_target_pairs={{0,8},{1,9},{2,10},{3,11},{4,12},{5,13},{6,14},{7,15},{16,56},{17,... | collective-permute-start | bytes 1966088 | tf_op jit(solution)/shard_map/ppermute | solution.py:43
  40.3 0.0 collective-permute-done.6.up_x
  40.3 0.0 collective-permute-done.7.down_x
  40.3 5.5 %logits.1 = (bf16[256,2048]{1,0:T(8,128)(2,1)S(1)}, f32[8,128]{1,0:T(8,128)S(1)}) custom-call(f32[1]{0:T(128)} %exp.3.scale_ref, s32[1]{0:T(128)} %bitcast.5.shift_ref, bf16[16,4224]{1,0:T(8,128)(2,1)S(1)} %get-tuple-element.49.own, bf16[16,8192]{1,0:T(8,128)(2,1)S(1)} %get-tuple-element.50.two, bf16[16,10240]{1,0:T(8,128)(2,1)S(1)} %collective-permute-done.2.up, ...), custom_call_target="tpu_custom_call" | custom-call | flops 4294967296 | bytes 16777216 | tf_op jit(solution)/shard_map/logits/pallas_call | solution.py:175
  45.8 0.7 collective-permute-start.8
  46.5 4.5 %weighted.1 = (f32[128,4096]{1,0:T(8,128)S(1)}, bf16[80,4096]{1,0:T(8,128)(2,1)S(1)}, bf16[96,4096]{1,0:T(8,128)(2,1)S(1)}) custom-call(bf16[256,2048]{1,0:T(8,128)(2,1)S(1)} %get-tuple-element.57.e_ref, bf16[2048,4096]{1,0:T(8,128)(2,1)S(1)} %get-tuple-element.55.mem_ref, bf16[48,4096]{1,0:T(8,128)(2,1)S(1)} %get-tuple-element.58.g_ref), custom_call_target="tpu_custom_call" | custom-call | flops 4294967296 | bytes 16777216 | tf_op jit(solution)/shard_map/weighted/pallas_call | solution.py:217
  51.0 0.0 copy-start.1
  51.1 0.0 collective-permute-done.8
  51.1 0.0 collective-permute-done.9.gr_ref
  51.1 1.8 %collective-permute-start.10 = (f32[2,8,128]{2,1,0:T(8,128)S(1)}, f32[2,8,128]{2,1,0:T(8,128)S(1)}, u32[]{:S(2)}, u32[]{:S(2)}) collective-permute-start(f32[2,8,128]{2,1,0:T(8,128)S(1)} %get-tuple-element.89), channel_id=1, source_target_pairs={{0,1},{1,2},{2,3},{3,4},{4,5},{5,6},{6,7},{7,0},{16,17},{17,18},{1... | collective-permute-start | bytes 24584 | tf_op jit(solution)/shard_map/ppermute | solution.py:43
  52.9 0.1 pad_add_fusion.2.place_ref
  53.0 0.3 collective-permute-start.11
  53.3 1.3 %collective-permute-start.14 = (bf16[80,4096]{1,0:T(8,128)(2,1)S(1)}, bf16[80,4096]{1,0:T(8,128)(2,1)S(1)}, u32[]{:S(2)}, u32[]{:S(2)}) collective-permute-start(bf16[80,4096]{1,0:T(8,128)(2,1)S(1)} %get-tuple-element.68), channel_id=1, source_target_pairs={{0,8},{1,9},{2,10},{3,11},{4,12},{5,13},{6,14},{7,15},{16,56},{17,... | collective-permute-start | bytes 1966088 | tf_op jit(solution)/shard_map/ppermute | solution.py:43
  54.6 0.2 collective-permute-done.10
  54.8 1.9 %collective-permute-start.13 = (f32[2,2,8,128]{3,2,1,0:T(8,128)S(1)}, f32[2,2,8,128]{3,2,1,0:T(8,128)S(1)}, u32[]{:S(2)}, u32[]{:S(2)}) collective-permute-start(f32[2,2,8,128]{3,2,1,0:T(8,128)S(1)} %pad_maximum_fusion.1), channel_id=1, source_target_pairs={{0,5},{1,6},{2,7},{3,0},{4,1},{5,2},{6,3},{7,4},{16,21},{17,22},{1... | collective-permute-start | bytes 49160 | tf_op jit(solution)/shard_map/ppermute | solution.py:43
  56.8 3.1 %collective-permute-start.12 = (f32[3,2,8,128]{3,2,1,0:T(8,128)S(1)}, f32[3,2,8,128]{3,2,1,0:T(8,128)S(1)}, u32[]{:S(2)}, u32[]{:S(2)}) collective-permute-start(f32[3,2,8,128]{3,2,1,0:T(8,128)S(1)} %pad_maximum_fusion.mid_ref), channel_id=1, source_target_pairs={{0,3},{1,4},{2,5},{3,6},{4,7},{5,0},{6,1},{7,2},{16,19},{17,20},{1... | collective-permute-start | bytes 73736 | tf_op jit(solution)/shard_map/ppermute | solution.py:43
  59.9 1.7 %collective-permute-done.13.down_ref = f32[2,2,8,128]{3,2,1,0:T(8,128)S(1)} collective-permute-done((f32[2,2,8,128]{3,2,1,0:T(8,128)S(1)}, f32[2,2,8,128]{3,2,1,0:T(8,128)S(1)}, u32[]{:S(2)}, u32[]{:S(2)}) %collective-permute-start.13) | collective-permute-done | bytes 16416 | tf_op jit(solution)/shard_map/ppermute | solution.py:43
  61.6 2.1 %collective-permute-done.12.up_ref = f32[3,2,8,128]{3,2,1,0:T(8,128)S(1)} collective-permute-done((f32[3,2,8,128]{3,2,1,0:T(8,128)S(1)}, f32[3,2,8,128]{3,2,1,0:T(8,128)S(1)}, u32[]{:S(2)}, u32[]{:S(2)}) %collective-permute-start.12) | collective-permute-done | bytes 24608 | tf_op jit(solution)/shard_map/ppermute | solution.py:43
  63.7 1.4 %collective-permute-start.19 = (bf16[96,4096]{1,0:T(8,128)(2,1)S(1)}, bf16[96,4096]{1,0:T(8,128)(2,1)S(1)}, u32[]{:S(2)}, u32[]{:S(2)}) collective-permute-start(bf16[96,4096]{1,0:T(8,128)(2,1)S(1)} %get-tuple-element.74), channel_id=1, source_target_pairs={{0,8},{1,9},{2,10},{3,11},{4,12},{5,13},{6,14},{7,15},{16,56},{17,... | collective-permute-start | bytes 2359304 | tf_op jit(solution)/shard_map/ppermute | solution.py:43
  65.1 0.8 merge.1
  65.9 0.5 mix.1
  66.4 1.8 %collective-permute-start.15 = (bf16[16,10240]{1,0:T(8,128)(2,1)S(1)}, bf16[16,10240]{1,0:T(8,128)(2,1)S(1)}, u32[]{:S(2)}, u32[]{:S(2)}) collective-permute-start(bf16[16,10240]{1,0:T(8,128)(2,1)S(1)} %get-tuple-element.71), channel_id=1, source_target_pairs={{0,1},{1,2},{2,3},{3,4},{4,5},{5,6},{6,7},{7,0},{16,17},{17,18},{1... | collective-permute-start | bytes 983048 | tf_op jit(solution)/shard_map/ppermute | solution.py:43
  68.2 0.3 collective-permute-start.16
  68.5 2.0 %collective-permute-start.17 = (f32[8,128]{1,0:T(8,128)S(1)}, f32[8,128]{1,0:T(8,128)S(1)}, u32[]{:S(2)}, u32[]{:S(2)}) collective-permute-start(f32[8,128]{1,0:T(8,128)S(1)} %get-tuple-element.73), channel_id=1, source_target_pairs={{0,40},{1,41},{2,42},{3,43},{4,44},{5,45},{6,46},{7,47},{16,24},{1... | collective-permute-start | bytes 12296 | tf_op jit(solution)/shard_map/ppermute | solution.py:43
  70.6 2.9 %collective-permute-done.17 = f32[8,128]{1,0:T(8,128)S(1)} collective-permute-done((f32[8,128]{1,0:T(8,128)S(1)}, f32[8,128]{1,0:T(8,128)S(1)}, u32[]{:S(2)}, u32[]{:S(2)}) %collective-permute-start.17) | collective-permute-done | bytes 4128 | tf_op jit(solution)/shard_map/ppermute | solution.py:43
  73.5 0.0 collective-permute-start.18
  73.5 1.2 %collective-permute-done.18 = f32[8,128]{1,0:T(8,128)S(1)} collective-permute-done((f32[8,128]{1,0:T(8,128)S(1)}, f32[8,128]{1,0:T(8,128)S(1)}, u32[]{:S(2)}, u32[]{:S(2)}) %collective-permute-start.18) | collective-permute-done | bytes 4128 | tf_op jit(solution)/shard_map/ppermute | solution.py:43
  74.6 1.1 %collective-permute-done.19.r_ref = bf16[96,4096]{1,0:T(8,128)(2,1)S(1)} collective-permute-done((bf16[96,4096]{1,0:T(8,128)(2,1)S(1)}, bf16[96,4096]{1,0:T(8,128)(2,1)S(1)}, u32[]{:S(2)}, u32[]{:S(2)}) %collective-permute-start.19) | collective-permute-done | bytes 786464 | tf_op jit(solution)/shard_map/ppermute | solution.py:43
  75.7 0.3 rest.1
  76.1 0.0 collective-permute-done.15
  76.1 0.0 collective-permute-done.16
  76.1 0.1 add_convert_fusion
  76.2 3.6 %collective-permute-start.20 = (bf16[16,4096]{1,0:T(8,128)(2,1)S(1)}, bf16[16,4096]{1,0:T(8,128)(2,1)S(1)}, u32[]{:S(2)}, u32[]{:S(2)}) collective-permute-start(bf16[16,4096]{1,0:T(8,128)(2,1)S(1)} %get-tuple-element.83), channel_id=1, source_target_pairs={{0,3},{1,4},{2,5},{3,6},{4,7},{5,0},{6,1},{7,2},{16,19},{17,20},{1... | collective-permute-start | bytes 393224 | tf_op jit(solution)/shard_map/ppermute | solution.py:43
  79.9 1.5 %collective-permute-start.21 = (bf16[16,4096]{1,0:T(8,128)(2,1)S(1)}, bf16[16,4096]{1,0:T(8,128)(2,1)S(1)}, u32[]{:S(2)}, u32[]{:S(2)}) collective-permute-start(bf16[16,4096]{1,0:T(8,128)(2,1)S(1)} %get-tuple-element.86), channel_id=1, source_target_pairs={{0,5},{1,6},{2,7},{3,0},{4,1},{5,2},{6,3},{7,4},{16,21},{17,22},{1... | collective-permute-start | bytes 393224 | tf_op jit(solution)/shard_map/ppermute | solution.py:43
  81.3 1.6 %collective-permute-start.22 = (f32[8,128]{1,0:T(8,128)S(1)}, f32[8,128]{1,0:T(8,128)S(1)}, u32[]{:S(2)}, u32[]{:S(2)}) collective-permute-start(f32[8,128]{1,0:T(8,128)S(1)} %add.79), channel_id=1, source_target_pairs={{0,64},{1,65},{2,66},{3,67},{4,68},{5,69},{6,70},{7,71},{16,80},{1... | collective-permute-start | bytes 12296 | tf_op jit(solution)/shard_map/ppermute | solution.py:43
  82.9 2.0 %collective-permute-done.22 = f32[8,128]{1,0:T(8,128)S(1)} collective-permute-done((f32[8,128]{1,0:T(8,128)S(1)}, f32[8,128]{1,0:T(8,128)S(1)}, u32[]{:S(2)}, u32[]{:S(2)}) %collective-permute-start.22) | collective-permute-done | bytes 4128 | tf_op jit(solution)/shard_map/ppermute | solution.py:43
  84.9 3.2 %collective-permute-start.23 = (f32[8,128]{1,0:T(8,128)S(1)}, f32[8,128]{1,0:T(8,128)S(1)}, u32[]{:S(2)}, u32[]{:S(2)}) collective-permute-start(f32[8,128]{1,0:T(8,128)S(1)} %add.89), channel_id=1, source_target_pairs={{0,128},{1,129},{2,130},{3,131},{4,132},{5,133},{6,134},{7,135},{1... | collective-permute-start | bytes 12296 | tf_op jit(solution)/shard_map/ppermute | solution.py:43
  88.1 1.9 %collective-permute-done.23 = f32[8,128]{1,0:T(8,128)S(1)} collective-permute-done((f32[8,128]{1,0:T(8,128)S(1)}, f32[8,128]{1,0:T(8,128)S(1)}, u32[]{:S(2)}, u32[]{:S(2)}) %collective-permute-start.23) | collective-permute-done | bytes 4128 | tf_op jit(solution)/shard_map/ppermute | solution.py:43
  90.1 0.5 slice.53
  91.2 0.0 collective-permute-done.20
  91.2 0.1 dynamic-slice_multiply_fusion
  91.3 1.4 %collective-permute-done.21 = bf16[16,4096]{1,0:T(8,128)(2,1)S(1)} collective-permute-done((bf16[16,4096]{1,0:T(8,128)(2,1)S(1)}, bf16[16,4096]{1,0:T(8,128)(2,1)S(1)}, u32[]{:S(2)}, u32[]{:S(2)}) %collective-permute-start.21) | collective-permute-done | bytes 131104 | tf_op jit(solution)/shard_map/ppermute | solution.py:43
  92.7 0.7 multiply_convert_fusion
  (20 shorter events, 0.1 us)
Async XLA Ops:
  0.6 39.7 %copy-start = (s32[2048]{0:T(1024)S(1)}, s32[2048]{0:T(1024)}, u32[]{:S(2)}) copy-start(s32[2048]{0:T(1024)} %param.10) | copy-start | bytes 24580
  0.6 14.8 %collective-permute-start = (bf16[16,4096]{1,0:T(8,128)(2,1)}, bf16[16,4096]{1,0:T(8,128)(2,1)S(1)}, u32[]{:S(2)}, u32[]{:S(2)}) collective-permute-start(bf16[16,4096]{1,0:T(8,128)(2,1)} %own_ref.1), channel_id=1, source_target_pairs={{0,3},{1,4},{2,5},{3,6},{4,7},{5,0},{6,1},{7,2},{16,19},{17,20},{1... | collective-permute-start | bytes 393224 | tf_op jit(solution)/shard_map/ppermute | solution.py:43
  6.6 12.1 %collective-permute-start.1 = (bf16[16,4096]{1,0:T(8,128)(2,1)}, bf16[16,4096]{1,0:T(8,128)(2,1)S(1)}, u32[]{:S(2)}, u32[]{:S(2)}) collective-permute-start(bf16[16,4096]{1,0:T(8,128)(2,1)} %own_ref.1), channel_id=1, source_target_pairs={{0,5},{1,6},{2,7},{3,0},{4,1},{5,2},{6,3},{7,4},{16,21},{17,22},{1... | collective-permute-start | bytes 393224 | tf_op jit(solution)/shard_map/ppermute | solution.py:43
  18.7 9.9 %collective-permute-start.2 = (bf16[16,10240]{1,0:T(8,128)(2,1)S(1)}, bf16[16,10240]{1,0:T(8,128)(2,1)S(1)}, u32[]{:S(2)}, u32[]{:S(2)}) collective-permute-start(bf16[16,10240]{1,0:T(8,128)(2,1)S(1)} %get-tuple-element.47), channel_id=1, source_target_pairs={{0,1},{1,2},{2,3},{3,4},{4,5},{5,6},{6,7},{7,0},{16,17},{17,18},{1... | collective-permute-start | bytes 983048 | tf_op jit(solution)/shard_map/ppermute | solution.py:43
  18.8 10.0 %collective-permute-start.3 = (bf16[16,10240]{1,0:T(8,128)(2,1)S(1)}, bf16[16,10240]{1,0:T(8,128)(2,1)S(1)}, u32[]{:S(2)}, u32[]{:S(2)}) collective-permute-start(bf16[16,10240]{1,0:T(8,128)(2,1)S(1)} %get-tuple-element.48), channel_id=1, source_target_pairs={{0,7},{1,0},{2,1},{3,2},{4,3},{5,4},{6,5},{7,6},{16,23},{17,16},{1... | collective-permute-start | bytes 983048 | tf_op jit(solution)/shard_map/ppermute | solution.py:43
  20.8 7.8 %collective-permute-start.5 = (bf16[16,8192]{1,0:T(8,128)(2,1)S(1)}, bf16[16,8192]{1,0:T(8,128)(2,1)S(1)}, u32[]{:S(2)}, u32[]{:S(2)}) collective-permute-start(bf16[16,8192]{1,0:T(8,128)(2,1)S(1)} %get-tuple-element.50.two), channel_id=1, source_target_pairs={{0,8},{1,9},{2,10},{3,11},{4,12},{5,13},{6,14},{7,15},{16,56},{17,... | collective-permute-start | bytes 786440 | tf_op jit(solution)/shard_map/ppermute | solution.py:43
  22.3 6.3 %collective-permute-start.4 = (bf16[16,4224]{1,0:T(8,128)(2,1)S(1)}, bf16[16,4224]{1,0:T(8,128)(2,1)S(1)}, u32[]{:S(2)}, u32[]{:S(2)}) collective-permute-start(bf16[16,4224]{1,0:T(8,128)(2,1)S(1)} %get-tuple-element.49.own), channel_id=1, source_target_pairs={{0,8},{1,9},{2,10},{3,11},{4,12},{5,13},{6,14},{7,15},{16,56},{17,... | collective-permute-start | bytes 405512 | tf_op jit(solution)/shard_map/ppermute | solution.py:43
  28.9 11.5 %collective-permute-start.6 = (bf16[16,10240]{1,0:T(8,128)(2,1)S(1)}, bf16[16,10240]{1,0:T(8,128)(2,1)S(1)}, u32[]{:S(2)}, u32[]{:S(2)}) collective-permute-start(bf16[16,10240]{1,0:T(8,128)(2,1)S(1)} %collective-permute-done.2.up), channel_id=1, source_target_pairs={{0,8},{1,9},{2,10},{3,11},{4,12},{5,13},{6,14},{7,15},{16,56},{17,... | collective-permute-start | bytes 983048 | tf_op jit(solution)/shard_map/ppermute | solution.py:43
  30.4 9.9 %collective-permute-start.7 = (bf16[16,10240]{1,0:T(8,128)(2,1)S(1)}, bf16[16,10240]{1,0:T(8,128)(2,1)S(1)}, u32[]{:S(2)}, u32[]{:S(2)}) collective-permute-start(bf16[16,10240]{1,0:T(8,128)(2,1)S(1)} %collective-permute-done.3.down), channel_id=1, source_target_pairs={{0,8},{1,9},{2,10},{3,11},{4,12},{5,13},{6,14},{7,15},{16,56},{17,... | collective-permute-start | bytes 983048 | tf_op jit(solution)/shard_map/ppermute | solution.py:43
  38.6 12.5 %collective-permute-start.9 = (bf16[80,4096]{1,0:T(8,128)(2,1)S(1)}, bf16[80,4096]{1,0:T(8,128)(2,1)S(1)}, u32[]{:S(2)}, u32[]{:S(2)}) collective-permute-start(bf16[80,4096]{1,0:T(8,128)(2,1)S(1)} %get-tuple-element.61), channel_id=1, source_target_pairs={{0,8},{1,9},{2,10},{3,11},{4,12},{5,13},{6,14},{7,15},{16,56},{17,... | collective-permute-start | bytes 1966088 | tf_op jit(solution)/shard_map/ppermute | solution.py:43
  45.8 5.2 %collective-permute-start.8 = (f32[8,128]{1,0:T(8,128)S(1)}, f32[8,128]{1,0:T(8,128)S(1)}, u32[]{:S(2)}, u32[]{:S(2)}) collective-permute-start(f32[8,128]{1,0:T(8,128)S(1)} %get-tuple-element.56), channel_id=1, source_target_pairs={{0,8},{1,9},{2,10},{3,11},{4,12},{5,13},{6,14},{7,15},{16,56},{17,... | collective-permute-start | bytes 12296 | tf_op jit(solution)/shard_map/ppermute | solution.py:43
  51.0 40.2 %copy-start.1 = (f32[256]{0:T(256)S(1)}, f32[256]{0:T(256)}, u32[]{:S(2)}) copy-start(f32[256]{0:T(256)} %param.11) | copy-start | bytes 3076
  51.1 3.7 %collective-permute-start.10 = (f32[2,8,128]{2,1,0:T(8,128)S(1)}, f32[2,8,128]{2,1,0:T(8,128)S(1)}, u32[]{:S(2)}, u32[]{:S(2)}) collective-permute-start(f32[2,8,128]{2,1,0:T(8,128)S(1)} %get-tuple-element.89), channel_id=1, source_target_pairs={{0,1},{1,2},{2,3},{3,4},{4,5},{5,6},{6,7},{7,0},{16,17},{17,18},{1... | collective-permute-start | bytes 24584 | tf_op jit(solution)/shard_map/ppermute | solution.py:43
  53.0 3.8 %collective-permute-start.11 = (f32[2,8,128]{2,1,0:T(8,128)S(1)}, f32[2,8,128]{2,1,0:T(8,128)S(1)}, u32[]{:S(2)}, u32[]{:S(2)}) collective-permute-start(f32[2,8,128]{2,1,0:T(8,128)S(1)} %get-tuple-element.89), channel_id=1, source_target_pairs={{0,7},{1,0},{2,1},{3,2},{4,3},{5,4},{6,5},{7,6},{16,23},{17,16},{1... | collective-permute-start | bytes 24584 | tf_op jit(solution)/shard_map/ppermute | solution.py:43
  53.3 12.7 %collective-permute-start.14 = (bf16[80,4096]{1,0:T(8,128)(2,1)S(1)}, bf16[80,4096]{1,0:T(8,128)(2,1)S(1)}, u32[]{:S(2)}, u32[]{:S(2)}) collective-permute-start(bf16[80,4096]{1,0:T(8,128)(2,1)S(1)} %get-tuple-element.68), channel_id=1, source_target_pairs={{0,8},{1,9},{2,10},{3,11},{4,12},{5,13},{6,14},{7,15},{16,56},{17,... | collective-permute-start | bytes 1966088 | tf_op jit(solution)/shard_map/ppermute | solution.py:43
  54.8 6.7 %collective-permute-start.13 = (f32[2,2,8,128]{3,2,1,0:T(8,128)S(1)}, f32[2,2,8,128]{3,2,1,0:T(8,128)S(1)}, u32[]{:S(2)}, u32[]{:S(2)}) collective-permute-start(f32[2,2,8,128]{3,2,1,0:T(8,128)S(1)} %pad_maximum_fusion.1), channel_id=1, source_target_pairs={{0,5},{1,6},{2,7},{3,0},{4,1},{5,2},{6,3},{7,4},{16,21},{17,22},{1... | collective-permute-start | bytes 49160 | tf_op jit(solution)/shard_map/ppermute | solution.py:43
  56.8 6.9 %collective-permute-start.12 = (f32[3,2,8,128]{3,2,1,0:T(8,128)S(1)}, f32[3,2,8,128]{3,2,1,0:T(8,128)S(1)}, u32[]{:S(2)}, u32[]{:S(2)}) collective-permute-start(f32[3,2,8,128]{3,2,1,0:T(8,128)S(1)} %pad_maximum_fusion.mid_ref), channel_id=1, source_target_pairs={{0,3},{1,4},{2,5},{3,6},{4,7},{5,0},{6,1},{7,2},{16,19},{17,20},{1... | collective-permute-start | bytes 73736 | tf_op jit(solution)/shard_map/ppermute | solution.py:43
  63.7 12.0 %collective-permute-start.19 = (bf16[96,4096]{1,0:T(8,128)(2,1)S(1)}, bf16[96,4096]{1,0:T(8,128)(2,1)S(1)}, u32[]{:S(2)}, u32[]{:S(2)}) collective-permute-start(bf16[96,4096]{1,0:T(8,128)(2,1)S(1)} %get-tuple-element.74), channel_id=1, source_target_pairs={{0,8},{1,9},{2,10},{3,11},{4,12},{5,13},{6,14},{7,15},{16,56},{17,... | collective-permute-start | bytes 2359304 | tf_op jit(solution)/shard_map/ppermute | solution.py:43
  66.4 9.6 %collective-permute-start.15 = (bf16[16,10240]{1,0:T(8,128)(2,1)S(1)}, bf16[16,10240]{1,0:T(8,128)(2,1)S(1)}, u32[]{:S(2)}, u32[]{:S(2)}) collective-permute-start(bf16[16,10240]{1,0:T(8,128)(2,1)S(1)} %get-tuple-element.71), channel_id=1, source_target_pairs={{0,1},{1,2},{2,3},{3,4},{4,5},{5,6},{6,7},{7,0},{16,17},{17,18},{1... | collective-permute-start | bytes 983048 | tf_op jit(solution)/shard_map/ppermute | solution.py:43
  68.2 7.9 %collective-permute-start.16 = (bf16[16,10240]{1,0:T(8,128)(2,1)S(1)}, bf16[16,10240]{1,0:T(8,128)(2,1)S(1)}, u32[]{:S(2)}, u32[]{:S(2)}) collective-permute-start(bf16[16,10240]{1,0:T(8,128)(2,1)S(1)} %get-tuple-element.72), channel_id=1, source_target_pairs={{0,7},{1,0},{2,1},{3,2},{4,3},{5,4},{6,5},{7,6},{16,23},{17,16},{1... | collective-permute-start | bytes 983048 | tf_op jit(solution)/shard_map/ppermute | solution.py:43
  68.5 4.9 %collective-permute-start.17 = (f32[8,128]{1,0:T(8,128)S(1)}, f32[8,128]{1,0:T(8,128)S(1)}, u32[]{:S(2)}, u32[]{:S(2)}) collective-permute-start(f32[8,128]{1,0:T(8,128)S(1)} %get-tuple-element.73), channel_id=1, source_target_pairs={{0,40},{1,41},{2,42},{3,43},{4,44},{5,45},{6,46},{7,47},{16,24},{1... | collective-permute-start | bytes 12296 | tf_op jit(solution)/shard_map/ppermute | solution.py:43
  73.5 1.2 %collective-permute-start.18 = (f32[8,128]{1,0:T(8,128)S(1)}, f32[8,128]{1,0:T(8,128)S(1)}, u32[]{:S(2)}, u32[]{:S(2)}) collective-permute-start(f32[8,128]{1,0:T(8,128)S(1)} %add.78), channel_id=1, source_target_pairs={{0,16},{1,17},{2,18},{3,19},{4,20},{5,21},{6,22},{7,23},{16,0},{17... | collective-permute-start | bytes 12296 | tf_op jit(solution)/shard_map/ppermute | solution.py:43
  76.2 15.0 %collective-permute-start.20 = (bf16[16,4096]{1,0:T(8,128)(2,1)S(1)}, bf16[16,4096]{1,0:T(8,128)(2,1)S(1)}, u32[]{:S(2)}, u32[]{:S(2)}) collective-permute-start(bf16[16,4096]{1,0:T(8,128)(2,1)S(1)} %get-tuple-element.83), channel_id=1, source_target_pairs={{0,3},{1,4},{2,5},{3,6},{4,7},{5,0},{6,1},{7,2},{16,19},{17,20},{1... | collective-permute-start | bytes 393224 | tf_op jit(solution)/shard_map/ppermute | solution.py:43
  79.9 12.8 %collective-permute-start.21 = (bf16[16,4096]{1,0:T(8,128)(2,1)S(1)}, bf16[16,4096]{1,0:T(8,128)(2,1)S(1)}, u32[]{:S(2)}, u32[]{:S(2)}) collective-permute-start(bf16[16,4096]{1,0:T(8,128)(2,1)S(1)} %get-tuple-element.86), channel_id=1, source_target_pairs={{0,5},{1,6},{2,7},{3,0},{4,1},{5,2},{6,3},{7,4},{16,21},{17,22},{1... | collective-permute-start | bytes 393224 | tf_op jit(solution)/shard_map/ppermute | solution.py:43
  81.3 3.6 %collective-permute-start.22 = (f32[8,128]{1,0:T(8,128)S(1)}, f32[8,128]{1,0:T(8,128)S(1)}, u32[]{:S(2)}, u32[]{:S(2)}) collective-permute-start(f32[8,128]{1,0:T(8,128)S(1)} %add.79), channel_id=1, source_target_pairs={{0,64},{1,65},{2,66},{3,67},{4,68},{5,69},{6,70},{7,71},{16,80},{1... | collective-permute-start | bytes 12296 | tf_op jit(solution)/shard_map/ppermute | solution.py:43
  84.9 5.1 %collective-permute-start.23 = (f32[8,128]{1,0:T(8,128)S(1)}, f32[8,128]{1,0:T(8,128)S(1)}, u32[]{:S(2)}, u32[]{:S(2)}) collective-permute-start(f32[8,128]{1,0:T(8,128)S(1)} %add.89), channel_id=1, source_target_pairs={{0,128},{1,129},{2,130},{3,131},{4,132},{5,133},{6,134},{7,135},{1... | collective-permute-start | bytes 12296 | tf_op jit(solution)/shard_map/ppermute | solution.py:43

commit v6 on v5

--- a/solution.py
+++ b/solution.py
@@ -1,3 +1,5 @@
+import functools
+
 import jax
 import jax.numpy as jnp
 from jax import lax
@@ -36,6 +38,7 @@
 CORE = table(lambda y, x, c, z: (y, x, 1 - c, z))
 CROSS = table(lambda y, x, c, z: (y, partner_of(x, 1 - c), c, z))
 Y1 = table(lambda y, x, c, z: (y ^ 1, x, c, z))
+Y3 = table(lambda y, x, c, z: (y ^ 3, x, c, z))
 Y2 = table(lambda y, x, c, z: (y ^ 2, x, c, z))
 
 
@@ -375,6 +378,32 @@
     )(coef, o, r, g)
 
 
+def final_kernel(count, factor_ref, p0_ref, au_ref, ad_ref, a3_ref, a5_ref, s0, s2, s1, s3, out_ref, sum_ref):
+    f32 = jnp.float32
+    depth = out_ref.shape[1]
+    for c in range(0, depth, 512):
+        at = slice(c, c + 512)
+        near = au_ref[:, at].astype(f32) + ad_ref[:, at].astype(f32)
+        wide = a3_ref[:, at].astype(f32) + a5_ref[:, at].astype(f32)
+        out_ref[:, at] = (factor_ref[...] * (p0_ref[:, at] + near + wide)).astype(out_ref.dtype)
+
+
+    total = ((s0[...] + s2[...]) + (s1[...] + s3[...])) / count
+    sum_ref[0] = total[0, 0]
+
+
+def final_call(count, factor, p0, au, ad, a3, a5, *parts):
+    return pl.pallas_call(
+        functools.partial(final_kernel, count),
+        in_specs=[vmem()] * 10,
+        out_specs=[vmem(), smem()],
+        out_shape=[jax.ShapeDtypeStruct(a3.shape, a3.dtype), jax.ShapeDtypeStruct((1,), jnp.float32)],
+        compiler_params=params(4),
+        cost_estimate=pl.CostEstimate(flops=5 * 10**9, bytes_accessed=1024, transcendentals=0),
+        name="final",
+    )(factor, p0, au, ad, a3, a5, *parts)
+
+
 def shards(queries, memory, log_scale, labels, valid, cotangent):
     f32, bf16 = jnp.float32, jnp.bfloat16
     together = lambda *arrays: lax.optimization_barrier(arrays)
@@ -414,9 +443,9 @@
     r_first = send(o_first, PARTNER)
     pair = jnp.stack([stat, stat_other])
     s_up, s_down = both(pair, pair, 1)
+    s_up, o_second = together(s_up, o_second)
     three = jnp.stack([s_up, pair, s_down])
     t_up, t_down = both(three, three[:2], 3)
-    t_up, t_down, o_second = together(t_up, t_down, o_second)
     coef, part = merge_call(jnp.stack([z, x_lo]), cots, t_up, three, t_down)
     r_second = send(o_second, PARTNER)
     pu, pd = mix_call(coef, o, r_first, g, g_first_x)
@@ -431,17 +460,11 @@
     p5 = p5 + au[:, next_].astype(f32) + jnp.concatenate([zero, ad[:, last].astype(f32)], axis=1)
     p3, p5, part = together(p3.astype(bf16), p5.astype(bf16), part)
     a3, a5 = both(p3, p5, 3)
-    for pairs in (Y1, Y2):
-        part = part + send(part, pairs)
-    summed = p0 + (au[:, near].astype(f32) + ad[:, near].astype(f32)) + (a3.astype(f32) + a5.astype(f32))
+    parts = part, send(part, Y2), send(part, Y1), send(part, Y3)
     q_rows = queries.shape[0]
-    a3, last_cot = together(a3, cotangent)
-    my_cot = lax.dynamic_slice_in_dim(last_cot, where * q_rows, q_rows)
-    grad_queries = (scale * my_cot[:, None] * summed).astype(bf16)
-
+    my_cot = lax.dynamic_slice_in_dim(cotangent, where * q_rows, q_rows)
     count = cotangent.shape[0] * lax.axis_size("dp")
-    scale_grad = part[0, 0:1] / count
-    return (grad_queries, scale_grad)
+    return final_call(count, (scale * my_cot)[:, None], p0, au, ad, a3, a5, *parts)
 
 
 def solution(mesh):

time: 95.1 us -> 94 us (0.988)
  between operations: 3.28 us -> 1.65 us
    ppermute x24 -> x25, waiting for transfers between devices: 29.4 us -> 30 us  [send(): return lax.ppermute(x, AXES, pairs)]
    ppermute x24 -> x25, starting transfers between devices: 38.6 us -> 38.6 us  [send(): return lax.ppermute(x, AXES, pairs)]
  transfers between devices with their start and end apart: 24 -> 25, of which waited for: 13 -> 15; matrix products, arithmetic and copies ran while one was open for 3% -> 2% of each run, Pallas kernels for 21% -> 21%
where the time goes in v6:
time: 94 us; the launch traced here: 93.2 us
  starting transfers between devices  38.6 us (41%)
  waiting for transfers between devices  30 us (32%)
  Pallas kernels  20.8 us (22%)
  local copies, waits for them, and re-layouts  1.83 us (2%)
  between operations  1.65 us (2%)
    ppermute x25, starting transfers between devices, send(): return lax.ppermute(x, AXES, pairs)  38.6 us
    ppermute x25, waiting for transfers between devices, send(): return lax.ppermute(x, AXES, pairs)  30 us
    pallas_call x1, Pallas kernels, labels_call(): pl.pallas_call(labels_kernel, in_specs=[vmem(), hbm()], out_specs=[vmem()...  7.41 us
    pallas_call x1, Pallas kernels, logits_call(): pl.pallas_call(logits_kernel, in_specs=[smem(), smem()] + [vmem()] * (len...  5.48 us
    pallas_call x1, Pallas kernels, weighted_call(): pl.pallas_call(weighted_kernel, in_specs=[vmem()] * 3, out_specs=[vmem()]...  4.52 us
  transfers between devices with their start and end apart: 25, of which 15 were waited for; matrix products, arithmetic and copies ran while one was open for 2% of the time, Pallas kernels for 21%

profile of v6, /device:TPU:32, one launch (start us, length us, event | category | flops | bytes accessed | tf_op | source)
XLA Modules:
  0.0 93.2 jit_solution(14658654879579383851)
XLA Ops:
  0.6 5.9 %collective-permute-start = (bf16[16,4096]{1,0:T(8,128)(2,1)}, bf16[16,4096]{1,0:T(8,128)(2,1)S(1)}, u32[]{:S(2)}, u32[]{:S(2)}) collective-permute-start(bf16[16,4096]{1,0:T(8,128)(2,1)} %own_ref.1), channel_id=1, source_target_pairs={{0,3},{1,4},{2,5},{3,6},{4,7},{5,0},{6,1},{7,2},{16,19},{17,20},{1... | collective-permute-start | bytes 393224 | tf_op jit(solution)/shard_map/ppermute | solution.py:46
  6.6 0.1 collective-permute-start.1
  6.7 0.8 dynamic_slice.14
  7.4 0.1 dynamic-slice_bitcast_fusion.1
  7.5 0.9 stage.1.own_ref
  8.4 0.8 dynamic-slice_bitcast_fusion.cot_ref
  9.2 6.2 %collective-permute-done.up3_ref = bf16[16,4096]{1,0:T(8,128)(2,1)S(1)} collective-permute-done((bf16[16,4096]{1,0:T(8,128)(2,1)}, bf16[16,4096]{1,0:T(8,128)(2,1)S(1)}, u32[]{:S(2)}, u32[]{:S(2)}) %collective-permute-start) | collective-permute-done | bytes 131104 | tf_op jit(solution)/shard_map/ppermute | solution.py:46
  15.4 3.2 %collective-permute-done.1.down3_ref = bf16[16,4096]{1,0:T(8,128)(2,1)S(1)} collective-permute-done((bf16[16,4096]{1,0:T(8,128)(2,1)}, bf16[16,4096]{1,0:T(8,128)(2,1)S(1)}, u32[]{:S(2)}, u32[]{:S(2)}) %collective-permute-start.1) | collective-permute-done | bytes 131104 | tf_op jit(solution)/shard_map/ppermute | solution.py:46
  18.6 0.1 pack.1
  18.7 0.1 collective-permute-start.2
  18.8 2.0 %collective-permute-start.3 = (bf16[16,10240]{1,0:T(8,128)(2,1)S(1)}, bf16[16,10240]{1,0:T(8,128)(2,1)S(1)}, u32[]{:S(2)}, u32[]{:S(2)}) collective-permute-start(bf16[16,10240]{1,0:T(8,128)(2,1)S(1)} %get-tuple-element.46), channel_id=1, source_target_pairs={{0,7},{1,0},{2,1},{3,2},{4,3},{5,4},{6,5},{7,6},{16,23},{17,16},{1... | collective-permute-start | bytes 983048 | tf_op jit(solution)/shard_map/ppermute | solution.py:46
  20.8 1.5 %collective-permute-start.5 = (bf16[16,8192]{1,0:T(8,128)(2,1)S(1)}, bf16[16,8192]{1,0:T(8,128)(2,1)S(1)}, u32[]{:S(2)}, u32[]{:S(2)}) collective-permute-start(bf16[16,8192]{1,0:T(8,128)(2,1)S(1)} %get-tuple-element.48.two), channel_id=1, source_target_pairs={{0,8},{1,9},{2,10},{3,11},{4,12},{5,13},{6,14},{7,15},{16,56},{17,... | collective-permute-start | bytes 786440 | tf_op jit(solution)/shard_map/ppermute | solution.py:46
  22.3 0.5 collective-permute-start.4
  23.5 5.1 %collective-permute-done.4.own_x = bf16[16,4224]{1,0:T(8,128)(2,1)S(1)} collective-permute-done((bf16[16,4224]{1,0:T(8,128)(2,1)S(1)}, bf16[16,4224]{1,0:T(8,128)(2,1)S(1)}, u32[]{:S(2)}, u32[]{:S(2)}) %collective-permute-start.4) | collective-permute-done | bytes 135200 | tf_op jit(solution)/shard_map/ppermute | solution.py:46
  28.6 0.0 collective-permute-done.2.up
  28.6 0.2 collective-permute-done.3.down
  28.9 1.6 %collective-permute-start.6 = (bf16[16,10240]{1,0:T(8,128)(2,1)S(1)}, bf16[16,10240]{1,0:T(8,128)(2,1)S(1)}, u32[]{:S(2)}, u32[]{:S(2)}) collective-permute-start(bf16[16,10240]{1,0:T(8,128)(2,1)S(1)} %collective-permute-done.2.up), channel_id=1, source_target_pairs={{0,8},{1,9},{2,10},{3,11},{4,12},{5,13},{6,14},{7,15},{16,56},{17,... | collective-permute-start | bytes 983048 | tf_op jit(solution)/shard_map/ppermute | solution.py:46
  30.4 0.5 collective-permute-start.7
  31.0 0.1 copy.11
  31.1 7.4 %label_rows.1 = (bf16[2048,4096]{1,0:T(8,128)(2,1)S(1)}, bf16[128,4096]{1,0:T(8,128)(2,1)S(1)}, bf16[80,4096]{1,0:T(8,128)(2,1)S(1)}, bf16[48,4096]{1,0:T(8,128)(2,1)S(1)}) custom-call(s32[256,1]{1,0:T(8,128)S(1)} %broadcast_subtract_fusion.lab_ref, bf16[2048,4096]{1,0:T(8,128)(2,1)} %mem_ref.1), custom_call_target="tpu_custom_call" | custom-call | flops 1024 | bytes 1024 | tf_op jit(solution)/shard_map/label_rows/pallas_call | solution.py:262
  38.6 1.8 %collective-permute-start.9 = (bf16[80,4096]{1,0:T(8,128)(2,1)S(1)}, bf16[80,4096]{1,0:T(8,128)(2,1)S(1)}, u32[]{:S(2)}, u32[]{:S(2)}) collective-permute-start(bf16[80,4096]{1,0:T(8,128)(2,1)S(1)} %get-tuple-element.59), channel_id=1, source_target_pairs={{0,8},{1,9},{2,10},{3,11},{4,12},{5,13},{6,14},{7,15},{16,56},{17,... | collective-permute-start | bytes 1966088 | tf_op jit(solution)/shard_map/ppermute | solution.py:46
  40.3 0.0 collective-permute-done.6.up_x
  40.3 0.0 collective-permute-done.7.down_x
  40.3 5.5 %logits.1 = (bf16[256,2048]{1,0:T(8,128)(2,1)S(1)}, f32[8,128]{1,0:T(8,128)S(1)}) custom-call(f32[1]{0:T(128)} %exp.3.scale_ref, s32[1]{0:T(128)} %bitcast.6.shift_ref, bf16[16,4224]{1,0:T(8,128)(2,1)S(1)} %get-tuple-element.47.own, bf16[16,8192]{1,0:T(8,128)(2,1)S(1)} %get-tuple-element.48.two, bf16[16,10240]{1,0:T(8,128)(2,1)S(1)} %collective-permute-done.2.up, ...), custom_call_target="tpu_custom_call" | custom-call | flops 4294967296 | bytes 16777216 | tf_op jit(solution)/shard_map/logits/pallas_call | solution.py:178
  45.8 0.7 collective-permute-start.8
  46.5 4.5 %weighted.1 = (f32[128,4096]{1,0:T(8,128)S(1)}, bf16[80,4096]{1,0:T(8,128)(2,1)S(1)}, bf16[96,4096]{1,0:T(8,128)(2,1)S(1)}) custom-call(bf16[256,2048]{1,0:T(8,128)(2,1)S(1)} %get-tuple-element.55.e_ref, bf16[2048,4096]{1,0:T(8,128)(2,1)S(1)} %get-tuple-element.53.mem_ref, bf16[48,4096]{1,0:T(8,128)(2,1)S(1)} %get-tuple-element.56.g_ref), custom_call_target="tpu_custom_call" | custom-call | flops 4294967296 | bytes 16777216 | tf_op jit(solution)/shard_map/weighted/pallas_call | solution.py:220
  51.0 0.0 copy-start.1
  51.1 0.0 collective-permute-done.8
  51.1 0.0 collective-permute-done.9.gr_ref
  51.1 1.8 %collective-permute-start.10 = (f32[2,8,128]{2,1,0:T(8,128)S(1)}, f32[2,8,128]{2,1,0:T(8,128)S(1)}, u32[]{:S(2)}, u32[]{:S(2)}) collective-permute-start(f32[2,8,128]{2,1,0:T(8,128)S(1)} %get-tuple-element.85), channel_id=1, source_target_pairs={{0,1},{1,2},{2,3},{3,4},{4,5},{5,6},{6,7},{7,0},{16,17},{17,18},{1... | collective-permute-start | bytes 24584 | tf_op jit(solution)/shard_map/ppermute | solution.py:46
  52.9 0.1 pad_add_fusion.2.place_ref
  53.0 0.3 collective-permute-start.11
  53.3 1.3 %collective-permute-start.14 = (bf16[80,4096]{1,0:T(8,128)(2,1)S(1)}, bf16[80,4096]{1,0:T(8,128)(2,1)S(1)}, u32[]{:S(2)}, u32[]{:S(2)}) collective-permute-start(bf16[80,4096]{1,0:T(8,128)(2,1)S(1)} %get-tuple-element.65), channel_id=1, source_target_pairs={{0,8},{1,9},{2,10},{3,11},{4,12},{5,13},{6,14},{7,15},{16,56},{17,... | collective-permute-start | bytes 1966088 | tf_op jit(solution)/shard_map/ppermute | solution.py:46
  54.6 0.2 collective-permute-done.10
  54.8 1.9 %collective-permute-start.13 = (f32[2,2,8,128]{3,2,1,0:T(8,128)S(1)}, f32[2,2,8,128]{3,2,1,0:T(8,128)S(1)}, u32[]{:S(2)}, u32[]{:S(2)}) collective-permute-start(f32[2,2,8,128]{3,2,1,0:T(8,128)S(1)} %pad_maximum_fusion.1), channel_id=1, source_target_pairs={{0,5},{1,6},{2,7},{3,0},{4,1},{5,2},{6,3},{7,4},{16,21},{17,22},{1... | collective-permute-start | bytes 49160 | tf_op jit(solution)/shard_map/ppermute | solution.py:46
  56.8 3.1 %collective-permute-start.12 = (f32[3,2,8,128]{3,2,1,0:T(8,128)S(1)}, f32[3,2,8,128]{3,2,1,0:T(8,128)S(1)}, u32[]{:S(2)}, u32[]{:S(2)}) collective-permute-start(f32[3,2,8,128]{3,2,1,0:T(8,128)S(1)} %pad_maximum_fusion.mid_ref), channel_id=1, source_target_pairs={{0,3},{1,4},{2,5},{3,6},{4,7},{5,0},{6,1},{7,2},{16,19},{17,20},{1... | collective-permute-start | bytes 73736 | tf_op jit(solution)/shard_map/ppermute | solution.py:46
  59.9 1.3 %collective-permute-start.19 = (bf16[96,4096]{1,0:T(8,128)(2,1)S(1)}, bf16[96,4096]{1,0:T(8,128)(2,1)S(1)}, u32[]{:S(2)}, u32[]{:S(2)}) collective-permute-start(bf16[96,4096]{1,0:T(8,128)(2,1)S(1)} %get-tuple-element.71), channel_id=1, source_target_pairs={{0,8},{1,9},{2,10},{3,11},{4,12},{5,13},{6,14},{7,15},{16,56},{17,... | collective-permute-start | bytes 2359304 | tf_op jit(solution)/shard_map/ppermute | solution.py:46
  61.2 0.4 collective-permute-done.13.down_ref
  61.6 2.1 %collective-permute-done.12.up_ref = f32[3,2,8,128]{3,2,1,0:T(8,128)S(1)} collective-permute-done((f32[3,2,8,128]{3,2,1,0:T(8,128)S(1)}, f32[3,2,8,128]{3,2,1,0:T(8,128)S(1)}, u32[]{:S(2)}, u32[]{:S(2)}) %collective-permute-start.12) | collective-permute-done | bytes 24608 | tf_op jit(solution)/shard_map/ppermute | solution.py:46
  63.7 0.8 merge.1
  64.5 0.5 mix.1
  65.0 1.7 %collective-permute-start.15 = (bf16[16,10240]{1,0:T(8,128)(2,1)S(1)}, bf16[16,10240]{1,0:T(8,128)(2,1)S(1)}, u32[]{:S(2)}, u32[]{:S(2)}) collective-permute-start(bf16[16,10240]{1,0:T(8,128)(2,1)S(1)} %get-tuple-element.68), channel_id=1, source_target_pairs={{0,1},{1,2},{2,3},{3,4},{4,5},{5,6},{6,7},{7,0},{16,17},{17,18},{1... | collective-permute-start | bytes 983048 | tf_op jit(solution)/shard_map/ppermute | solution.py:46
  66.7 0.4 collective-permute-start.16
  67.1 2.6 %collective-permute-start.17 = (f32[8,128]{1,0:T(8,128)S(1)}, f32[8,128]{1,0:T(8,128)S(1)}, u32[]{:S(2)}, u32[]{:S(2)}) collective-permute-start(f32[8,128]{1,0:T(8,128)S(1)} %get-tuple-element.70), channel_id=1, source_target_pairs={{0,40},{1,41},{2,42},{3,43},{4,44},{5,45},{6,46},{7,47},{16,24},{1... | collective-permute-start | bytes 12296 | tf_op jit(solution)/shard_map/ppermute | solution.py:46
  69.7 2.3 %collective-permute-done.17 = f32[8,128]{1,0:T(8,128)S(1)} collective-permute-done((f32[8,128]{1,0:T(8,128)S(1)}, f32[8,128]{1,0:T(8,128)S(1)}, u32[]{:S(2)}, u32[]{:S(2)}) %collective-permute-start.17) | collective-permute-done | bytes 4128 | tf_op jit(solution)/shard_map/ppermute | solution.py:46
  72.0 0.0 collective-permute-start.18
  72.0 1.2 %collective-permute-done.18 = f32[8,128]{1,0:T(8,128)S(1)} collective-permute-done((f32[8,128]{1,0:T(8,128)S(1)}, f32[8,128]{1,0:T(8,128)S(1)}, u32[]{:S(2)}, u32[]{:S(2)}) %collective-permute-start.18) | collective-permute-done | bytes 4128 | tf_op jit(solution)/shard_map/ppermute | solution.py:46
  73.2 0.0 collective-permute-done.19.r_ref
  73.2 0.3 rest.1
  73.5 0.8 collective-permute-done.15.au_ref
  74.4 0.8 collective-permute-done.16.ad_ref
  75.2 0.1 add_convert_fusion
  75.3 4.6 %collective-permute-start.20 = (bf16[16,4096]{1,0:T(8,128)(2,1)S(1)}, bf16[16,4096]{1,0:T(8,128)(2,1)S(1)}, u32[]{:S(2)}, u32[]{:S(2)}) collective-permute-start(bf16[16,4096]{1,0:T(8,128)(2,1)S(1)} %get-tuple-element.81), channel_id=1, source_target_pairs={{0,3},{1,4},{2,5},{3,6},{4,7},{5,0},{6,1},{7,2},{16,19},{17,20},{1... | collective-permute-start | bytes 393224 | tf_op jit(solution)/shard_map/ppermute | solution.py:46
  79.9 0.5 collective-permute-start.21
  80.4 3.2 %collective-permute-start.22 = (f32[8,128]{1,0:T(8,128)S(1)}, f32[8,128]{1,0:T(8,128)S(1)}, u32[]{:S(2)}, u32[]{:S(2)}) collective-permute-start(f32[8,128]{1,0:T(8,128)S(1)} %add.62.s0), channel_id=1, source_target_pairs={{0,128},{1,129},{2,130},{3,131},{4,132},{5,133},{6,134},{7,135},{1... | collective-permute-start | bytes 12296 | tf_op jit(solution)/shard_map/ppermute | solution.py:46
  83.6 0.7 collective-permute-start.23
  84.2 0.4 collective-permute-start.24
  84.6 0.1 multiply_bitcast_fusion
  84.7 0.1 copy.12.factor_ref
  84.8 0.7 collective-permute-done.22.s2
  85.5 1.7 %collective-permute-done.23.s1 = f32[8,128]{1,0:T(8,128)S(1)} collective-permute-done((f32[8,128]{1,0:T(8,128)S(1)}, f32[8,128]{1,0:T(8,128)S(1)}, u32[]{:S(2)}, u32[]{:S(2)}) %collective-permute-start.23) | collective-permute-done | bytes 4128 | tf_op jit(solution)/shard_map/ppermute | solution.py:46
  87.2 1.9 %collective-permute-done.24.s3 = f32[8,128]{1,0:T(8,128)S(1)} collective-permute-done((f32[8,128]{1,0:T(8,128)S(1)}, f32[8,128]{1,0:T(8,128)S(1)}, u32[]{:S(2)}, u32[]{:S(2)}) %collective-permute-start.24) | collective-permute-done | bytes 4128 | tf_op jit(solution)/shard_map/ppermute | solution.py:46
  89.1 3.2 %collective-permute-done.21.a5_ref = bf16[16,4096]{1,0:T(8,128)(2,1)S(1)} collective-permute-done((bf16[16,4096]{1,0:T(8,128)(2,1)S(1)}, bf16[16,4096]{1,0:T(8,128)(2,1)S(1)}, u32[]{:S(2)}, u32[]{:S(2)}) %collective-permute-start.21) | collective-permute-done | bytes 131104 | tf_op jit(solution)/shard_map/ppermute | solution.py:46
  92.2 0.8 final.1
  (20 shorter events, 0.1 us)
Async XLA Ops:
  0.6 39.7 %copy-start = (s32[2048]{0:T(1024)S(1)}, s32[2048]{0:T(1024)}, u32[]{:S(2)}) copy-start(s32[2048]{0:T(1024)} %param.10) | copy-start | bytes 24580
  0.6 14.8 %collective-permute-start = (bf16[16,4096]{1,0:T(8,128)(2,1)}, bf16[16,4096]{1,0:T(8,128)(2,1)S(1)}, u32[]{:S(2)}, u32[]{:S(2)}) collective-permute-start(bf16[16,4096]{1,0:T(8,128)(2,1)} %own_ref.1), channel_id=1, source_target_pairs={{0,3},{1,4},{2,5},{3,6},{4,7},{5,0},{6,1},{7,2},{16,19},{17,20},{1... | collective-permute-start | bytes 393224 | tf_op jit(solution)/shard_map/ppermute | solution.py:46
  6.6 12.1 %collective-permute-start.1 = (bf16[16,4096]{1,0:T(8,128)(2,1)}, bf16[16,4096]{1,0:T(8,128)(2,1)S(1)}, u32[]{:S(2)}, u32[]{:S(2)}) collective-permute-start(bf16[16,4096]{1,0:T(8,128)(2,1)} %own_ref.1), channel_id=1, source_target_pairs={{0,5},{1,6},{2,7},{3,0},{4,1},{5,2},{6,3},{7,4},{16,21},{17,22},{1... | collective-permute-start | bytes 393224 | tf_op jit(solution)/shard_map/ppermute | solution.py:46
  18.7 9.9 %collective-permute-start.2 = (bf16[16,10240]{1,0:T(8,128)(2,1)S(1)}, bf16[16,10240]{1,0:T(8,128)(2,1)S(1)}, u32[]{:S(2)}, u32[]{:S(2)}) collective-permute-start(bf16[16,10240]{1,0:T(8,128)(2,1)S(1)} %get-tuple-element.45), channel_id=1, source_target_pairs={{0,1},{1,2},{2,3},{3,4},{4,5},{5,6},{6,7},{7,0},{16,17},{17,18},{1... | collective-permute-start | bytes 983048 | tf_op jit(solution)/shard_map/ppermute | solution.py:46
  18.8 10.0 %collective-permute-start.3 = (bf16[16,10240]{1,0:T(8,128)(2,1)S(1)}, bf16[16,10240]{1,0:T(8,128)(2,1)S(1)}, u32[]{:S(2)}, u32[]{:S(2)}) collective-permute-start(bf16[16,10240]{1,0:T(8,128)(2,1)S(1)} %get-tuple-element.46), channel_id=1, source_target_pairs={{0,7},{1,0},{2,1},{3,2},{4,3},{5,4},{6,5},{7,6},{16,23},{17,16},{1... | collective-permute-start | bytes 983048 | tf_op jit(solution)/shard_map/ppermute | solution.py:46
  20.8 7.8 %collective-permute-start.5 = (bf16[16,8192]{1,0:T(8,128)(2,1)S(1)}, bf16[16,8192]{1,0:T(8,128)(2,1)S(1)}, u32[]{:S(2)}, u32[]{:S(2)}) collective-permute-start(bf16[16,8192]{1,0:T(8,128)(2,1)S(1)} %get-tuple-element.48.two), channel_id=1, source_target_pairs={{0,8},{1,9},{2,10},{3,11},{4,12},{5,13},{6,14},{7,15},{16,56},{17,... | collective-permute-start | bytes 786440 | tf_op jit(solution)/shard_map/ppermute | solution.py:46
  22.3 6.3 %collective-permute-start.4 = (bf16[16,4224]{1,0:T(8,128)(2,1)S(1)}, bf16[16,4224]{1,0:T(8,128)(2,1)S(1)}, u32[]{:S(2)}, u32[]{:S(2)}) collective-permute-start(bf16[16,4224]{1,0:T(8,128)(2,1)S(1)} %get-tuple-element.47.own), channel_id=1, source_target_pairs={{0,8},{1,9},{2,10},{3,11},{4,12},{5,13},{6,14},{7,15},{16,56},{17,... | collective-permute-start | bytes 405512 | tf_op jit(solution)/shard_map/ppermute | solution.py:46
  28.9 11.5 %collective-permute-start.6 = (bf16[16,10240]{1,0:T(8,128)(2,1)S(1)}, bf16[16,10240]{1,0:T(8,128)(2,1)S(1)}, u32[]{:S(2)}, u32[]{:S(2)}) collective-permute-start(bf16[16,10240]{1,0:T(8,128)(2,1)S(1)} %collective-permute-done.2.up), channel_id=1, source_target_pairs={{0,8},{1,9},{2,10},{3,11},{4,12},{5,13},{6,14},{7,15},{16,56},{17,... | collective-permute-start | bytes 983048 | tf_op jit(solution)/shard_map/ppermute | solution.py:46
  30.4 9.9 %collective-permute-start.7 = (bf16[16,10240]{1,0:T(8,128)(2,1)S(1)}, bf16[16,10240]{1,0:T(8,128)(2,1)S(1)}, u32[]{:S(2)}, u32[]{:S(2)}) collective-permute-start(bf16[16,10240]{1,0:T(8,128)(2,1)S(1)} %collective-permute-done.3.down), channel_id=1, source_target_pairs={{0,8},{1,9},{2,10},{3,11},{4,12},{5,13},{6,14},{7,15},{16,56},{17,... | collective-permute-start | bytes 983048 | tf_op jit(solution)/shard_map/ppermute | solution.py:46
  38.6 12.5 %collective-permute-start.9 = (bf16[80,4096]{1,0:T(8,128)(2,1)S(1)}, bf16[80,4096]{1,0:T(8,128)(2,1)S(1)}, u32[]{:S(2)}, u32[]{:S(2)}) collective-permute-start(bf16[80,4096]{1,0:T(8,128)(2,1)S(1)} %get-tuple-element.59), channel_id=1, source_target_pairs={{0,8},{1,9},{2,10},{3,11},{4,12},{5,13},{6,14},{7,15},{16,56},{17,... | collective-permute-start | bytes 1966088 | tf_op jit(solution)/shard_map/ppermute | solution.py:46
  45.8 5.2 %collective-permute-start.8 = (f32[8,128]{1,0:T(8,128)S(1)}, f32[8,128]{1,0:T(8,128)S(1)}, u32[]{:S(2)}, u32[]{:S(2)}) collective-permute-start(f32[8,128]{1,0:T(8,128)S(1)} %get-tuple-element.54), channel_id=1, source_target_pairs={{0,8},{1,9},{2,10},{3,11},{4,12},{5,13},{6,14},{7,15},{16,56},{17,... | collective-permute-start | bytes 12296 | tf_op jit(solution)/shard_map/ppermute | solution.py:46
  51.0 33.6 %copy-start.1 = (f32[256]{0:T(256)S(1)}, f32[256]{0:T(256)}, u32[]{:S(2)}) copy-start(f32[256]{0:T(256)} %param.11) | copy-start | bytes 3076
  51.1 3.7 %collective-permute-start.10 = (f32[2,8,128]{2,1,0:T(8,128)S(1)}, f32[2,8,128]{2,1,0:T(8,128)S(1)}, u32[]{:S(2)}, u32[]{:S(2)}) collective-permute-start(f32[2,8,128]{2,1,0:T(8,128)S(1)} %get-tuple-element.85), channel_id=1, source_target_pairs={{0,1},{1,2},{2,3},{3,4},{4,5},{5,6},{6,7},{7,0},{16,17},{17,18},{1... | collective-permute-start | bytes 24584 | tf_op jit(solution)/shard_map/ppermute | solution.py:46
  53.0 3.8 %collective-permute-start.11 = (f32[2,8,128]{2,1,0:T(8,128)S(1)}, f32[2,8,128]{2,1,0:T(8,128)S(1)}, u32[]{:S(2)}, u32[]{:S(2)}) collective-permute-start(f32[2,8,128]{2,1,0:T(8,128)S(1)} %get-tuple-element.85), channel_id=1, source_target_pairs={{0,7},{1,0},{2,1},{3,2},{4,3},{5,4},{6,5},{7,6},{16,23},{17,16},{1... | collective-permute-start | bytes 24584 | tf_op jit(solution)/shard_map/ppermute | solution.py:46
  53.3 11.2 %collective-permute-start.14 = (bf16[80,4096]{1,0:T(8,128)(2,1)S(1)}, bf16[80,4096]{1,0:T(8,128)(2,1)S(1)}, u32[]{:S(2)}, u32[]{:S(2)}) collective-permute-start(bf16[80,4096]{1,0:T(8,128)(2,1)S(1)} %get-tuple-element.65), channel_id=1, source_target_pairs={{0,8},{1,9},{2,10},{3,11},{4,12},{5,13},{6,14},{7,15},{16,56},{17,... | collective-permute-start | bytes 1966088 | tf_op jit(solution)/shard_map/ppermute | solution.py:46
  54.8 6.7 %collective-permute-start.13 = (f32[2,2,8,128]{3,2,1,0:T(8,128)S(1)}, f32[2,2,8,128]{3,2,1,0:T(8,128)S(1)}, u32[]{:S(2)}, u32[]{:S(2)}) collective-permute-start(f32[2,2,8,128]{3,2,1,0:T(8,128)S(1)} %pad_maximum_fusion.1), channel_id=1, source_target_pairs={{0,5},{1,6},{2,7},{3,0},{4,1},{5,2},{6,3},{7,4},{16,21},{17,22},{1... | collective-permute-start | bytes 49160 | tf_op jit(solution)/shard_map/ppermute | solution.py:46
  56.8 6.9 %collective-permute-start.12 = (f32[3,2,8,128]{3,2,1,0:T(8,128)S(1)}, f32[3,2,8,128]{3,2,1,0:T(8,128)S(1)}, u32[]{:S(2)}, u32[]{:S(2)}) collective-permute-start(f32[3,2,8,128]{3,2,1,0:T(8,128)S(1)} %pad_maximum_fusion.mid_ref), channel_id=1, source_target_pairs={{0,3},{1,4},{2,5},{3,6},{4,7},{5,0},{6,1},{7,2},{16,19},{17,20},{1... | collective-permute-start | bytes 73736 | tf_op jit(solution)/shard_map/ppermute | solution.py:46
  59.9 13.3 %collective-permute-start.19 = (bf16[96,4096]{1,0:T(8,128)(2,1)S(1)}, bf16[96,4096]{1,0:T(8,128)(2,1)S(1)}, u32[]{:S(2)}, u32[]{:S(2)}) collective-permute-start(bf16[96,4096]{1,0:T(8,128)(2,1)S(1)} %get-tuple-element.71), channel_id=1, source_target_pairs={{0,8},{1,9},{2,10},{3,11},{4,12},{5,13},{6,14},{7,15},{16,56},{17,... | collective-permute-start | bytes 2359304 | tf_op jit(solution)/shard_map/ppermute | solution.py:46
  65.0 9.4 %collective-permute-start.15 = (bf16[16,10240]{1,0:T(8,128)(2,1)S(1)}, bf16[16,10240]{1,0:T(8,128)(2,1)S(1)}, u32[]{:S(2)}, u32[]{:S(2)}) collective-permute-start(bf16[16,10240]{1,0:T(8,128)(2,1)S(1)} %get-tuple-element.68), channel_id=1, source_target_pairs={{0,1},{1,2},{2,3},{3,4},{4,5},{5,6},{6,7},{7,0},{16,17},{17,18},{1... | collective-permute-start | bytes 983048 | tf_op jit(solution)/shard_map/ppermute | solution.py:46
  66.7 8.5 %collective-permute-start.16 = (bf16[16,10240]{1,0:T(8,128)(2,1)S(1)}, bf16[16,10240]{1,0:T(8,128)(2,1)S(1)}, u32[]{:S(2)}, u32[]{:S(2)}) collective-permute-start(bf16[16,10240]{1,0:T(8,128)(2,1)S(1)} %get-tuple-element.69), channel_id=1, source_target_pairs={{0,7},{1,0},{2,1},{3,2},{4,3},{5,4},{6,5},{7,6},{16,23},{17,16},{1... | collective-permute-start | bytes 983048 | tf_op jit(solution)/shard_map/ppermute | solution.py:46
  67.1 4.9 %collective-permute-start.17 = (f32[8,128]{1,0:T(8,128)S(1)}, f32[8,128]{1,0:T(8,128)S(1)}, u32[]{:S(2)}, u32[]{:S(2)}) collective-permute-start(f32[8,128]{1,0:T(8,128)S(1)} %get-tuple-element.70), channel_id=1, source_target_pairs={{0,40},{1,41},{2,42},{3,43},{4,44},{5,45},{6,46},{7,47},{16,24},{1... | collective-permute-start | bytes 12296 | tf_op jit(solution)/shard_map/ppermute | solution.py:46
  72.0 1.2 %collective-permute-start.18 = (f32[8,128]{1,0:T(8,128)S(1)}, f32[8,128]{1,0:T(8,128)S(1)}, u32[]{:S(2)}, u32[]{:S(2)}) collective-permute-start(f32[8,128]{1,0:T(8,128)S(1)} %add.61), channel_id=1, source_target_pairs={{0,16},{1,17},{2,18},{3,19},{4,20},{5,21},{6,22},{7,23},{16,0},{17... | collective-permute-start | bytes 12296 | tf_op jit(solution)/shard_map/ppermute | solution.py:46
  75.3 13.8 %collective-permute-start.20 = (bf16[16,4096]{1,0:T(8,128)(2,1)S(1)}, bf16[16,4096]{1,0:T(8,128)(2,1)S(1)}, u32[]{:S(2)}, u32[]{:S(2)}) collective-permute-start(bf16[16,4096]{1,0:T(8,128)(2,1)S(1)} %get-tuple-element.81), channel_id=1, source_target_pairs={{0,3},{1,4},{2,5},{3,6},{4,7},{5,0},{6,1},{7,2},{16,19},{17,20},{1... | collective-permute-start | bytes 393224 | tf_op jit(solution)/shard_map/ppermute | solution.py:46
  79.9 12.4 %collective-permute-start.21 = (bf16[16,4096]{1,0:T(8,128)(2,1)S(1)}, bf16[16,4096]{1,0:T(8,128)(2,1)S(1)}, u32[]{:S(2)}, u32[]{:S(2)}) collective-permute-start(bf16[16,4096]{1,0:T(8,128)(2,1)S(1)} %get-tuple-element.82), channel_id=1, source_target_pairs={{0,5},{1,6},{2,7},{3,0},{4,1},{5,2},{6,3},{7,4},{16,21},{17,22},{1... | collective-permute-start | bytes 393224 | tf_op jit(solution)/shard_map/ppermute | solution.py:46
  80.4 5.1 %collective-permute-start.22 = (f32[8,128]{1,0:T(8,128)S(1)}, f32[8,128]{1,0:T(8,128)S(1)}, u32[]{:S(2)}, u32[]{:S(2)}) collective-permute-start(f32[8,128]{1,0:T(8,128)S(1)} %add.62.s0), channel_id=1, source_target_pairs={{0,128},{1,129},{2,130},{3,131},{4,132},{5,133},{6,134},{7,135},{1... | collective-permute-start | bytes 12296 | tf_op jit(solution)/shard_map/ppermute | solution.py:46
  83.6 3.6 %collective-permute-start.23 = (f32[8,128]{1,0:T(8,128)S(1)}, f32[8,128]{1,0:T(8,128)S(1)}, u32[]{:S(2)}, u32[]{:S(2)}) collective-permute-start(f32[8,128]{1,0:T(8,128)S(1)} %add.62.s0), channel_id=1, source_target_pairs={{0,64},{1,65},{2,66},{3,67},{4,68},{5,69},{6,70},{7,71},{16,80},{1... | collective-permute-start | bytes 12296 | tf_op jit(solution)/shard_map/ppermute | solution.py:46
  84.2 4.8 %collective-permute-start.24 = (f32[8,128]{1,0:T(8,128)S(1)}, f32[8,128]{1,0:T(8,128)S(1)}, u32[]{:S(2)}, u32[]{:S(2)}) collective-permute-start(f32[8,128]{1,0:T(8,128)S(1)} %add.62.s0), channel_id=1, source_target_pairs={{0,192},{1,193},{2,194},{3,195},{4,196},{5,197},{6,198},{7,199},{1... | collective-permute-start | bytes 12296 | tf_op jit(solution)/shard_map/ppermute | solution.py:46

commit v7 on v6

--- a/solution.py
+++ b/solution.py
@@ -378,7 +378,7 @@
     )(coef, o, r, g)
 
 
-def final_kernel(count, factor_ref, p0_ref, au_ref, ad_ref, a3_ref, a5_ref, s0, s2, s1, s3, out_ref, sum_ref):
+def final_kernel(count, factor_ref, p0_ref, au_ref, ad_ref, a3_ref, a5_ref, part_ref, out_ref, sum_ref):
     f32 = jnp.float32
     depth = out_ref.shape[1]
     for c in range(0, depth, 512):
@@ -388,20 +388,20 @@
         out_ref[:, at] = (factor_ref[...] * (p0_ref[:, at] + near + wide)).astype(out_ref.dtype)
 
 
-    total = ((s0[...] + s2[...]) + (s1[...] + s3[...])) / count
+    total = part_ref[...] / count
     sum_ref[0] = total[0, 0]
 
 
-def final_call(count, factor, p0, au, ad, a3, a5, *parts):
+def final_call(count, factor, p0, au, ad, a3, a5, part):
     return pl.pallas_call(
         functools.partial(final_kernel, count),
-        in_specs=[vmem()] * 10,
+        in_specs=[vmem()] * 7,
         out_specs=[vmem(), smem()],
         out_shape=[jax.ShapeDtypeStruct(a3.shape, a3.dtype), jax.ShapeDtypeStruct((1,), jnp.float32)],
         compiler_params=params(4),
         cost_estimate=pl.CostEstimate(flops=5 * 10**9, bytes_accessed=1024, transcendentals=0),
         name="final",
-    )(factor, p0, au, ad, a3, a5, *parts)
+    )(factor, p0, au, ad, a3, a5, part)
 
 
 def shards(queries, memory, log_scale, labels, valid, cotangent):
@@ -451,8 +451,7 @@
     pu, pd = mix_call(coef, o, r_first, g, g_first_x)
     au, ad = both(pu, pd, 1)
     p0, p3, p5 = rest_call(coef, o, r_second, g)
-    for pairs in (CROSS, CORE):
-        part = part + send(part, pairs)
+    part = (part + send(part, Y2)) + (send(part, Y1) + send(part, Y3))
     au, ad, part, p0, p3, p5 = together(au, ad, part, p0, p3, p5)
     zero = jnp.zeros((16, half), f32)
     near, next_, last = slice(0, depth), slice(depth, 2 * depth), slice(2 * depth, 2 * depth + half)
@@ -460,11 +459,12 @@
     p5 = p5 + au[:, next_].astype(f32) + jnp.concatenate([zero, ad[:, last].astype(f32)], axis=1)
     p3, p5, part = together(p3.astype(bf16), p5.astype(bf16), part)
     a3, a5 = both(p3, p5, 3)
-    parts = part, send(part, Y2), send(part, Y1), send(part, Y3)
+    for pairs in (CROSS, CORE):
+        part = part + send(part, pairs)
     q_rows = queries.shape[0]
     my_cot = lax.dynamic_slice_in_dim(cotangent, where * q_rows, q_rows)
     count = cotangent.shape[0] * lax.axis_size("dp")
-    return final_call(count, (scale * my_cot)[:, None], p0, au, ad, a3, a5, *parts)
+    return final_call(count, (scale * my_cot)[:, None], p0, au, ad, a3, a5, part)
 
 
 def solution(mesh):

time: 94 us -> 94.6 us (level)
  starting transfers between devices: 38.6 us -> 41.2 us
  waiting for transfers between devices: 30 us -> 28.6 us
    ppermute x25, starting transfers between devices: 38.6 us -> 41.2 us  [send(): return lax.ppermute(x, AXES, pairs)]
    ppermute x25, waiting for transfers between devices: 30 us -> 28.6 us  [send(): return lax.ppermute(x, AXES, pairs)]
  transfers between devices with their start and end apart: 25 -> 25, of which waited for: 15 -> 12; matrix products, arithmetic and copies ran while one was open for 2% -> 2% of each run, Pallas kernels for 21% -> 21%
where the time goes in v7:
time: 94.6 us; the launch traced here: 94.4 us
  starting transfers between devices  41.2 us (44%)
  waiting for transfers between devices  28.6 us (30%)
  Pallas kernels  20.8 us (22%)
  local copies, waits for them, and re-layouts  1.83 us (2%)
  between operations  1.68 us (2%)
    ppermute x25, starting transfers between devices, send(): return lax.ppermute(x, AXES, pairs)  41.2 us
    ppermute x25, waiting for transfers between devices, send(): return lax.ppermute(x, AXES, pairs)  28.6 us
    pallas_call x1, Pallas kernels, labels_call(): pl.pallas_call(labels_kernel, in_specs=[vmem(), hbm()], out_specs=[vmem()...  7.41 us
    pallas_call x1, Pallas kernels, logits_call(): pl.pallas_call(logits_kernel, in_specs=[smem(), smem()] + [vmem()] * (len...  5.48 us
    pallas_call x1, Pallas kernels, weighted_call(): pl.pallas_call(weighted_kernel, in_specs=[vmem()] * 3, out_specs=[vmem()]...  4.52 us
  transfers between devices with their start and end apart: 25, of which 12 were waited for; matrix products, arithmetic and copies ran while one was open for 2% of the time, Pallas kernels for 21%

profile of v7, /device:TPU:32, one launch (start us, length us, event | category | flops | bytes accessed | tf_op | source)
XLA Modules:
  0.0 94.4 jit_solution(8056158416996596025)
XLA Ops:
  0.6 5.9 %collective-permute-start = (bf16[16,4096]{1,0:T(8,128)(2,1)}, bf16[16,4096]{1,0:T(8,128)(2,1)S(1)}, u32[]{:S(2)}, u32[]{:S(2)}) collective-permute-start(bf16[16,4096]{1,0:T(8,128)(2,1)} %own_ref.1), channel_id=1, source_target_pairs={{0,3},{1,4},{2,5},{3,6},{4,7},{5,0},{6,1},{7,2},{16,19},{17,20},{1... | collective-permute-start | bytes 393224 | tf_op jit(solution)/shard_map/ppermute | solution.py:46
  6.6 0.1 collective-permute-start.1
  6.7 0.8 dynamic_slice.14
  7.4 0.1 dynamic-slice_bitcast_fusion.1
  7.5 0.9 stage.1.own_ref
  8.4 0.8 dynamic-slice_bitcast_fusion.cot_ref
  9.2 6.2 %collective-permute-done.up3_ref = bf16[16,4096]{1,0:T(8,128)(2,1)S(1)} collective-permute-done((bf16[16,4096]{1,0:T(8,128)(2,1)}, bf16[16,4096]{1,0:T(8,128)(2,1)S(1)}, u32[]{:S(2)}, u32[]{:S(2)}) %collective-permute-start) | collective-permute-done | bytes 131104 | tf_op jit(solution)/shard_map/ppermute | solution.py:46
  15.4 3.2 %collective-permute-done.1.down3_ref = bf16[16,4096]{1,0:T(8,128)(2,1)S(1)} collective-permute-done((bf16[16,4096]{1,0:T(8,128)(2,1)}, bf16[16,4096]{1,0:T(8,128)(2,1)S(1)}, u32[]{:S(2)}, u32[]{:S(2)}) %collective-permute-start.1) | collective-permute-done | bytes 131104 | tf_op jit(solution)/shard_map/ppermute | solution.py:46
  18.6 0.1 pack.1
  18.7 0.1 collective-permute-start.2
  18.8 2.0 %collective-permute-start.3 = (bf16[16,10240]{1,0:T(8,128)(2,1)S(1)}, bf16[16,10240]{1,0:T(8,128)(2,1)S(1)}, u32[]{:S(2)}, u32[]{:S(2)}) collective-permute-start(bf16[16,10240]{1,0:T(8,128)(2,1)S(1)} %get-tuple-element.46), channel_id=1, source_target_pairs={{0,7},{1,0},{2,1},{3,2},{4,3},{5,4},{6,5},{7,6},{16,23},{17,16},{1... | collective-permute-start | bytes 983048 | tf_op jit(solution)/shard_map/ppermute | solution.py:46
  20.8 1.5 %collective-permute-start.5 = (bf16[16,8192]{1,0:T(8,128)(2,1)S(1)}, bf16[16,8192]{1,0:T(8,128)(2,1)S(1)}, u32[]{:S(2)}, u32[]{:S(2)}) collective-permute-start(bf16[16,8192]{1,0:T(8,128)(2,1)S(1)} %get-tuple-element.48.two), channel_id=1, source_target_pairs={{0,8},{1,9},{2,10},{3,11},{4,12},{5,13},{6,14},{7,15},{16,56},{17,... | collective-permute-start | bytes 786440 | tf_op jit(solution)/shard_map/ppermute | solution.py:46
  22.3 0.5 collective-permute-start.4
  23.5 5.1 %collective-permute-done.4.own_x = bf16[16,4224]{1,0:T(8,128)(2,1)S(1)} collective-permute-done((bf16[16,4224]{1,0:T(8,128)(2,1)S(1)}, bf16[16,4224]{1,0:T(8,128)(2,1)S(1)}, u32[]{:S(2)}, u32[]{:S(2)}) %collective-permute-start.4) | collective-permute-done | bytes 135200 | tf_op jit(solution)/shard_map/ppermute | solution.py:46
  28.6 0.0 collective-permute-done.5.two_x
  28.6 0.0 collective-permute-done.2.up
  28.6 0.2 collective-permute-done.3.down
  28.9 1.6 %collective-permute-start.6 = (bf16[16,10240]{1,0:T(8,128)(2,1)S(1)}, bf16[16,10240]{1,0:T(8,128)(2,1)S(1)}, u32[]{:S(2)}, u32[]{:S(2)}) collective-permute-start(bf16[16,10240]{1,0:T(8,128)(2,1)S(1)} %collective-permute-done.2.up), channel_id=1, source_target_pairs={{0,8},{1,9},{2,10},{3,11},{4,12},{5,13},{6,14},{7,15},{16,56},{17,... | collective-permute-start | bytes 983048 | tf_op jit(solution)/shard_map/ppermute | solution.py:46
  30.4 0.5 collective-permute-start.7
  31.0 0.1 copy.11
  31.1 7.4 %label_rows.1 = (bf16[2048,4096]{1,0:T(8,128)(2,1)S(1)}, bf16[128,4096]{1,0:T(8,128)(2,1)S(1)}, bf16[80,4096]{1,0:T(8,128)(2,1)S(1)}, bf16[48,4096]{1,0:T(8,128)(2,1)S(1)}) custom-call(s32[256,1]{1,0:T(8,128)S(1)} %broadcast_subtract_fusion.lab_ref, bf16[2048,4096]{1,0:T(8,128)(2,1)} %mem_ref.1), custom_call_target="tpu_custom_call" | custom-call | flops 1024 | bytes 1024 | tf_op jit(solution)/shard_map/label_rows/pallas_call | solution.py:262
  38.6 1.8 %collective-permute-start.9 = (bf16[80,4096]{1,0:T(8,128)(2,1)S(1)}, bf16[80,4096]{1,0:T(8,128)(2,1)S(1)}, u32[]{:S(2)}, u32[]{:S(2)}) collective-permute-start(bf16[80,4096]{1,0:T(8,128)(2,1)S(1)} %get-tuple-element.59), channel_id=1, source_target_pairs={{0,8},{1,9},{2,10},{3,11},{4,12},{5,13},{6,14},{7,15},{16,56},{17,... | collective-permute-start | bytes 1966088 | tf_op jit(solution)/shard_map/ppermute | solution.py:46
  40.3 5.5 %logits.1 = (bf16[256,2048]{1,0:T(8,128)(2,1)S(1)}, f32[8,128]{1,0:T(8,128)S(1)}) custom-call(f32[1]{0:T(128)} %exp.3.scale_ref, s32[1]{0:T(128)} %bitcast.6.shift_ref, bf16[16,4224]{1,0:T(8,128)(2,1)S(1)} %get-tuple-element.47.own, bf16[16,8192]{1,0:T(8,128)(2,1)S(1)} %get-tuple-element.48.two, bf16[16,10240]{1,0:T(8,128)(2,1)S(1)} %collective-permute-done.2.up, ...), custom_call_target="tpu_custom_call" | custom-call | flops 4294967296 | bytes 16777216 | tf_op jit(solution)/shard_map/logits/pallas_call | solution.py:178
  45.8 0.7 collective-permute-start.8
  46.5 4.5 %weighted.1 = (f32[128,4096]{1,0:T(8,128)S(1)}, bf16[80,4096]{1,0:T(8,128)(2,1)S(1)}, bf16[96,4096]{1,0:T(8,128)(2,1)S(1)}) custom-call(bf16[256,2048]{1,0:T(8,128)(2,1)S(1)} %get-tuple-element.55.e_ref, bf16[2048,4096]{1,0:T(8,128)(2,1)S(1)} %get-tuple-element.53.mem_ref, bf16[48,4096]{1,0:T(8,128)(2,1)S(1)} %get-tuple-element.56.g_ref), custom_call_target="tpu_custom_call" | custom-call | flops 4294967296 | bytes 16777216 | tf_op jit(solution)/shard_map/weighted/pallas_call | solution.py:220
  51.0 0.0 copy-start.1
  51.1 0.0 collective-permute-done.9.gr_ref
  51.1 1.8 %collective-permute-start.10 = (f32[2,8,128]{2,1,0:T(8,128)S(1)}, f32[2,8,128]{2,1,0:T(8,128)S(1)}, u32[]{:S(2)}, u32[]{:S(2)}) collective-permute-start(f32[2,8,128]{2,1,0:T(8,128)S(1)} %get-tuple-element.85), channel_id=1, source_target_pairs={{0,1},{1,2},{2,3},{3,4},{4,5},{5,6},{6,7},{7,0},{16,17},{17,18},{1... | collective-permute-start | bytes 24584 | tf_op jit(solution)/shard_map/ppermute | solution.py:46
  52.9 0.1 pad_add_fusion.2.place_ref
  53.0 0.3 collective-permute-start.11
  53.3 1.3 %collective-permute-start.14 = (bf16[80,4096]{1,0:T(8,128)(2,1)S(1)}, bf16[80,4096]{1,0:T(8,128)(2,1)S(1)}, u32[]{:S(2)}, u32[]{:S(2)}) collective-permute-start(bf16[80,4096]{1,0:T(8,128)(2,1)S(1)} %get-tuple-element.65), channel_id=1, source_target_pairs={{0,8},{1,9},{2,10},{3,11},{4,12},{5,13},{6,14},{7,15},{16,56},{17,... | collective-permute-start | bytes 1966088 | tf_op jit(solution)/shard_map/ppermute | solution.py:46
  54.6 0.2 collective-permute-done.10
  54.8 1.9 %collective-permute-start.13 = (f32[2,2,8,128]{3,2,1,0:T(8,128)S(1)}, f32[2,2,8,128]{3,2,1,0:T(8,128)S(1)}, u32[]{:S(2)}, u32[]{:S(2)}) collective-permute-start(f32[2,2,8,128]{3,2,1,0:T(8,128)S(1)} %pad_maximum_fusion.1), channel_id=1, source_target_pairs={{0,5},{1,6},{2,7},{3,0},{4,1},{5,2},{6,3},{7,4},{16,21},{17,22},{1... | collective-permute-start | bytes 49160 | tf_op jit(solution)/shard_map/ppermute | solution.py:46
  56.8 0.0 collective-permute-done.11
  56.8 3.1 %collective-permute-start.12 = (f32[3,2,8,128]{3,2,1,0:T(8,128)S(1)}, f32[3,2,8,128]{3,2,1,0:T(8,128)S(1)}, u32[]{:S(2)}, u32[]{:S(2)}) collective-permute-start(f32[3,2,8,128]{3,2,1,0:T(8,128)S(1)} %pad_maximum_fusion.mid_ref), channel_id=1, source_target_pairs={{0,3},{1,4},{2,5},{3,6},{4,7},{5,0},{6,1},{7,2},{16,19},{17,20},{1... | collective-permute-start | bytes 73736 | tf_op jit(solution)/shard_map/ppermute | solution.py:46
  59.9 1.3 %collective-permute-start.20 = (bf16[96,4096]{1,0:T(8,128)(2,1)S(1)}, bf16[96,4096]{1,0:T(8,128)(2,1)S(1)}, u32[]{:S(2)}, u32[]{:S(2)}) collective-permute-start(bf16[96,4096]{1,0:T(8,128)(2,1)S(1)} %get-tuple-element.71), channel_id=1, source_target_pairs={{0,8},{1,9},{2,10},{3,11},{4,12},{5,13},{6,14},{7,15},{16,56},{17,... | collective-permute-start | bytes 2359304 | tf_op jit(solution)/shard_map/ppermute | solution.py:46
  61.2 0.4 collective-permute-done.13.down_ref
  61.6 2.1 %collective-permute-done.12.up_ref = f32[3,2,8,128]{3,2,1,0:T(8,128)S(1)} collective-permute-done((f32[3,2,8,128]{3,2,1,0:T(8,128)S(1)}, f32[3,2,8,128]{3,2,1,0:T(8,128)S(1)}, u32[]{:S(2)}, u32[]{:S(2)}) %collective-permute-start.12) | collective-permute-done | bytes 24608 | tf_op jit(solution)/shard_map/ppermute | solution.py:46
  63.7 0.8 merge.1
  64.5 0.0 collective-permute-done.14.r_ref
  64.5 0.5 mix.1
  65.0 1.7 %collective-permute-start.15 = (bf16[16,10240]{1,0:T(8,128)(2,1)S(1)}, bf16[16,10240]{1,0:T(8,128)(2,1)S(1)}, u32[]{:S(2)}, u32[]{:S(2)}) collective-permute-start(bf16[16,10240]{1,0:T(8,128)(2,1)S(1)} %get-tuple-element.68), channel_id=1, source_target_pairs={{0,1},{1,2},{2,3},{3,4},{4,5},{5,6},{6,7},{7,0},{16,17},{17,18},{1... | collective-permute-start | bytes 983048 | tf_op jit(solution)/shard_map/ppermute | solution.py:46
  66.7 0.4 collective-permute-start.16
  67.1 3.2 %collective-permute-start.17 = (f32[8,128]{1,0:T(8,128)S(1)}, f32[8,128]{1,0:T(8,128)S(1)}, u32[]{:S(2)}, u32[]{:S(2)}) collective-permute-start(f32[8,128]{1,0:T(8,128)S(1)} %get-tuple-element.70), channel_id=1, source_target_pairs={{0,128},{1,129},{2,130},{3,131},{4,132},{5,133},{6,134},{7,135},{1... | collective-permute-start | bytes 12296 | tf_op jit(solution)/shard_map/ppermute | solution.py:46
  70.3 0.7 collective-permute-start.18
  71.0 1.2 %collective-permute-done.17 = f32[8,128]{1,0:T(8,128)S(1)} collective-permute-done((f32[8,128]{1,0:T(8,128)S(1)}, f32[8,128]{1,0:T(8,128)S(1)}, u32[]{:S(2)}, u32[]{:S(2)}) %collective-permute-start.17) | collective-permute-done | bytes 4128 | tf_op jit(solution)/shard_map/ppermute | solution.py:46
  72.2 3.0 %collective-permute-start.19 = (f32[8,128]{1,0:T(8,128)S(1)}, f32[8,128]{1,0:T(8,128)S(1)}, u32[]{:S(2)}, u32[]{:S(2)}) collective-permute-start(f32[8,128]{1,0:T(8,128)S(1)} %get-tuple-element.70), channel_id=1, source_target_pairs={{0,192},{1,193},{2,194},{3,195},{4,196},{5,197},{6,198},{7,199},{1... | collective-permute-start | bytes 12296 | tf_op jit(solution)/shard_map/ppermute | solution.py:46
  75.2 0.0 collective-permute-done.18
  75.2 1.8 %collective-permute-done.19 = f32[8,128]{1,0:T(8,128)S(1)} collective-permute-done((f32[8,128]{1,0:T(8,128)S(1)}, f32[8,128]{1,0:T(8,128)S(1)}, u32[]{:S(2)}, u32[]{:S(2)}) %collective-permute-start.19) | collective-permute-done | bytes 4128 | tf_op jit(solution)/shard_map/ppermute | solution.py:46
  77.0 0.3 rest.1
  77.4 0.0 collective-permute-done.15.au_ref
  77.4 0.0 collective-permute-done.16.ad_ref
  77.4 0.1 add_convert_fusion
  77.5 4.9 %collective-permute-start.21 = (bf16[16,4096]{1,0:T(8,128)(2,1)S(1)}, bf16[16,4096]{1,0:T(8,128)(2,1)S(1)}, u32[]{:S(2)}, u32[]{:S(2)}) collective-permute-start(bf16[16,4096]{1,0:T(8,128)(2,1)S(1)} %get-tuple-element.81), channel_id=1, source_target_pairs={{0,3},{1,4},{2,5},{3,6},{4,7},{5,0},{6,1},{7,2},{16,19},{17,20},{1... | collective-permute-start | bytes 393224 | tf_op jit(solution)/shard_map/ppermute | solution.py:46
  82.4 0.2 collective-permute-start.22
  82.6 2.6 %collective-permute-start.23 = (f32[8,128]{1,0:T(8,128)S(1)}, f32[8,128]{1,0:T(8,128)S(1)}, u32[]{:S(2)}, u32[]{:S(2)}) collective-permute-start(f32[8,128]{1,0:T(8,128)S(1)} %add_add_fusion), channel_id=1, source_target_pairs={{0,40},{1,41},{2,42},{3,43},{4,44},{5,45},{6,46},{7,47},{16,24},{1... | collective-permute-start | bytes 12296 | tf_op jit(solution)/shard_map/ppermute | solution.py:46
  85.2 2.2 %collective-permute-done.23 = f32[8,128]{1,0:T(8,128)S(1)} collective-permute-done((f32[8,128]{1,0:T(8,128)S(1)}, f32[8,128]{1,0:T(8,128)S(1)}, u32[]{:S(2)}, u32[]{:S(2)}) %collective-permute-start.23) | collective-permute-done | bytes 4128 | tf_op jit(solution)/shard_map/ppermute | solution.py:46
  87.4 0.0 collective-permute-start.24
  87.5 0.1 multiply_bitcast_fusion
  87.5 0.1 copy.12.factor_ref
  87.6 1.0 %collective-permute-done.24 = f32[8,128]{1,0:T(8,128)S(1)} collective-permute-done((f32[8,128]{1,0:T(8,128)S(1)}, f32[8,128]{1,0:T(8,128)S(1)}, u32[]{:S(2)}, u32[]{:S(2)}) %collective-permute-start.24) | collective-permute-done | bytes 4128 | tf_op jit(solution)/shard_map/ppermute | solution.py:46
  88.6 0.0 collective-permute-done.21.a3_ref
  88.6 4.8 %collective-permute-done.22.a5_ref = bf16[16,4096]{1,0:T(8,128)(2,1)S(1)} collective-permute-done((bf16[16,4096]{1,0:T(8,128)(2,1)S(1)}, bf16[16,4096]{1,0:T(8,128)(2,1)S(1)}, u32[]{:S(2)}, u32[]{:S(2)}) %collective-permute-start.22) | collective-permute-done | bytes 131104 | tf_op jit(solution)/shard_map/ppermute | solution.py:46
  93.5 0.8 final.1
  (21 shorter events, 0.1 us)
Async XLA Ops:
  0.6 39.7 %copy-start = (s32[2048]{0:T(1024)S(1)}, s32[2048]{0:T(1024)}, u32[]{:S(2)}) copy-start(s32[2048]{0:T(1024)} %param.10) | copy-start | bytes 24580
  0.6 14.8 %collective-permute-start = (bf16[16,4096]{1,0:T(8,128)(2,1)}, bf16[16,4096]{1,0:T(8,128)(2,1)S(1)}, u32[]{:S(2)}, u32[]{:S(2)}) collective-permute-start(bf16[16,4096]{1,0:T(8,128)(2,1)} %own_ref.1), channel_id=1, source_target_pairs={{0,3},{1,4},{2,5},{3,6},{4,7},{5,0},{6,1},{7,2},{16,19},{17,20},{1... | collective-permute-start | bytes 393224 | tf_op jit(solution)/shard_map/ppermute | solution.py:46
  6.6 12.1 %collective-permute-start.1 = (bf16[16,4096]{1,0:T(8,128)(2,1)}, bf16[16,4096]{1,0:T(8,128)(2,1)S(1)}, u32[]{:S(2)}, u32[]{:S(2)}) collective-permute-start(bf16[16,4096]{1,0:T(8,128)(2,1)} %own_ref.1), channel_id=1, source_target_pairs={{0,5},{1,6},{2,7},{3,0},{4,1},{5,2},{6,3},{7,4},{16,21},{17,22},{1... | collective-permute-start | bytes 393224 | tf_op jit(solution)/shard_map/ppermute | solution.py:46
  18.7 9.9 %collective-permute-start.2 = (bf16[16,10240]{1,0:T(8,128)(2,1)S(1)}, bf16[16,10240]{1,0:T(8,128)(2,1)S(1)}, u32[]{:S(2)}, u32[]{:S(2)}) collective-permute-start(bf16[16,10240]{1,0:T(8,128)(2,1)S(1)} %get-tuple-element.45), channel_id=1, source_target_pairs={{0,1},{1,2},{2,3},{3,4},{4,5},{5,6},{6,7},{7,0},{16,17},{17,18},{1... | collective-permute-start | bytes 983048 | tf_op jit(solution)/shard_map/ppermute | solution.py:46
  18.8 10.0 %collective-permute-start.3 = (bf16[16,10240]{1,0:T(8,128)(2,1)S(1)}, bf16[16,10240]{1,0:T(8,128)(2,1)S(1)}, u32[]{:S(2)}, u32[]{:S(2)}) collective-permute-start(bf16[16,10240]{1,0:T(8,128)(2,1)S(1)} %get-tuple-element.46), channel_id=1, source_target_pairs={{0,7},{1,0},{2,1},{3,2},{4,3},{5,4},{6,5},{7,6},{16,23},{17,16},{1... | collective-permute-start | bytes 983048 | tf_op jit(solution)/shard_map/ppermute | solution.py:46
  20.8 7.8 %collective-permute-start.5 = (bf16[16,8192]{1,0:T(8,128)(2,1)S(1)}, bf16[16,8192]{1,0:T(8,128)(2,1)S(1)}, u32[]{:S(2)}, u32[]{:S(2)}) collective-permute-start(bf16[16,8192]{1,0:T(8,128)(2,1)S(1)} %get-tuple-element.48.two), channel_id=1, source_target_pairs={{0,8},{1,9},{2,10},{3,11},{4,12},{5,13},{6,14},{7,15},{16,56},{17,... | collective-permute-start | bytes 786440 | tf_op jit(solution)/shard_map/ppermute | solution.py:46
  22.3 6.3 %collective-permute-start.4 = (bf16[16,4224]{1,0:T(8,128)(2,1)S(1)}, bf16[16,4224]{1,0:T(8,128)(2,1)S(1)}, u32[]{:S(2)}, u32[]{:S(2)}) collective-permute-start(bf16[16,4224]{1,0:T(8,128)(2,1)S(1)} %get-tuple-element.47.own), channel_id=1, source_target_pairs={{0,8},{1,9},{2,10},{3,11},{4,12},{5,13},{6,14},{7,15},{16,56},{17,... | collective-permute-start | bytes 405512 | tf_op jit(solution)/shard_map/ppermute | solution.py:46
  28.9 11.5 %collective-permute-start.6 = (bf16[16,10240]{1,0:T(8,128)(2,1)S(1)}, bf16[16,10240]{1,0:T(8,128)(2,1)S(1)}, u32[]{:S(2)}, u32[]{:S(2)}) collective-permute-start(bf16[16,10240]{1,0:T(8,128)(2,1)S(1)} %collective-permute-done.2.up), channel_id=1, source_target_pairs={{0,8},{1,9},{2,10},{3,11},{4,12},{5,13},{6,14},{7,15},{16,56},{17,... | collective-permute-start | bytes 983048 | tf_op jit(solution)/shard_map/ppermute | solution.py:46
  30.4 9.9 %collective-permute-start.7 = (bf16[16,10240]{1,0:T(8,128)(2,1)S(1)}, bf16[16,10240]{1,0:T(8,128)(2,1)S(1)}, u32[]{:S(2)}, u32[]{:S(2)}) collective-permute-start(bf16[16,10240]{1,0:T(8,128)(2,1)S(1)} %collective-permute-done.3.down), channel_id=1, source_target_pairs={{0,8},{1,9},{2,10},{3,11},{4,12},{5,13},{6,14},{7,15},{16,56},{17,... | collective-permute-start | bytes 983048 | tf_op jit(solution)/shard_map/ppermute | solution.py:46
  38.6 12.5 %collective-permute-start.9 = (bf16[80,4096]{1,0:T(8,128)(2,1)S(1)}, bf16[80,4096]{1,0:T(8,128)(2,1)S(1)}, u32[]{:S(2)}, u32[]{:S(2)}) collective-permute-start(bf16[80,4096]{1,0:T(8,128)(2,1)S(1)} %get-tuple-element.59), channel_id=1, source_target_pairs={{0,8},{1,9},{2,10},{3,11},{4,12},{5,13},{6,14},{7,15},{16,56},{17,... | collective-permute-start | bytes 1966088 | tf_op jit(solution)/shard_map/ppermute | solution.py:46
  45.8 5.2 %collective-permute-start.8 = (f32[8,128]{1,0:T(8,128)S(1)}, f32[8,128]{1,0:T(8,128)S(1)}, u32[]{:S(2)}, u32[]{:S(2)}) collective-permute-start(f32[8,128]{1,0:T(8,128)S(1)} %get-tuple-element.54), channel_id=1, source_target_pairs={{0,8},{1,9},{2,10},{3,11},{4,12},{5,13},{6,14},{7,15},{16,56},{17,... | collective-permute-start | bytes 12296 | tf_op jit(solution)/shard_map/ppermute | solution.py:46
  51.0 36.4 %copy-start.1 = (f32[256]{0:T(256)S(1)}, f32[256]{0:T(256)}, u32[]{:S(2)}) copy-start(f32[256]{0:T(256)} %param.11) | copy-start | bytes 3076
  51.1 3.7 %collective-permute-start.10 = (f32[2,8,128]{2,1,0:T(8,128)S(1)}, f32[2,8,128]{2,1,0:T(8,128)S(1)}, u32[]{:S(2)}, u32[]{:S(2)}) collective-permute-start(f32[2,8,128]{2,1,0:T(8,128)S(1)} %get-tuple-element.85), channel_id=1, source_target_pairs={{0,1},{1,2},{2,3},{3,4},{4,5},{5,6},{6,7},{7,0},{16,17},{17,18},{1... | collective-permute-start | bytes 24584 | tf_op jit(solution)/shard_map/ppermute | solution.py:46
  53.0 3.8 %collective-permute-start.11 = (f32[2,8,128]{2,1,0:T(8,128)S(1)}, f32[2,8,128]{2,1,0:T(8,128)S(1)}, u32[]{:S(2)}, u32[]{:S(2)}) collective-permute-start(f32[2,8,128]{2,1,0:T(8,128)S(1)} %get-tuple-element.85), channel_id=1, source_target_pairs={{0,7},{1,0},{2,1},{3,2},{4,3},{5,4},{6,5},{7,6},{16,23},{17,16},{1... | collective-permute-start | bytes 24584 | tf_op jit(solution)/shard_map/ppermute | solution.py:46
  53.3 11.2 %collective-permute-start.14 = (bf16[80,4096]{1,0:T(8,128)(2,1)S(1)}, bf16[80,4096]{1,0:T(8,128)(2,1)S(1)}, u32[]{:S(2)}, u32[]{:S(2)}) collective-permute-start(bf16[80,4096]{1,0:T(8,128)(2,1)S(1)} %get-tuple-element.65), channel_id=1, source_target_pairs={{0,8},{1,9},{2,10},{3,11},{4,12},{5,13},{6,14},{7,15},{16,56},{17,... | collective-permute-start | bytes 1966088 | tf_op jit(solution)/shard_map/ppermute | solution.py:46
  54.8 6.7 %collective-permute-start.13 = (f32[2,2,8,128]{3,2,1,0:T(8,128)S(1)}, f32[2,2,8,128]{3,2,1,0:T(8,128)S(1)}, u32[]{:S(2)}, u32[]{:S(2)}) collective-permute-start(f32[2,2,8,128]{3,2,1,0:T(8,128)S(1)} %pad_maximum_fusion.1), channel_id=1, source_target_pairs={{0,5},{1,6},{2,7},{3,0},{4,1},{5,2},{6,3},{7,4},{16,21},{17,22},{1... | collective-permute-start | bytes 49160 | tf_op jit(solution)/shard_map/ppermute | solution.py:46
  56.8 6.9 %collective-permute-start.12 = (f32[3,2,8,128]{3,2,1,0:T(8,128)S(1)}, f32[3,2,8,128]{3,2,1,0:T(8,128)S(1)}, u32[]{:S(2)}, u32[]{:S(2)}) collective-permute-start(f32[3,2,8,128]{3,2,1,0:T(8,128)S(1)} %pad_maximum_fusion.mid_ref), channel_id=1, source_target_pairs={{0,3},{1,4},{2,5},{3,6},{4,7},{5,0},{6,1},{7,2},{16,19},{17,20},{1... | collective-permute-start | bytes 73736 | tf_op jit(solution)/shard_map/ppermute | solution.py:46
  59.9 17.2 %collective-permute-start.20 = (bf16[96,4096]{1,0:T(8,128)(2,1)S(1)}, bf16[96,4096]{1,0:T(8,128)(2,1)S(1)}, u32[]{:S(2)}, u32[]{:S(2)}) collective-permute-start(bf16[96,4096]{1,0:T(8,128)(2,1)S(1)} %get-tuple-element.71), channel_id=1, source_target_pairs={{0,8},{1,9},{2,10},{3,11},{4,12},{5,13},{6,14},{7,15},{16,56},{17,... | collective-permute-start | bytes 2359304 | tf_op jit(solution)/shard_map/ppermute | solution.py:46
  65.0 12.4 %collective-permute-start.15 = (bf16[16,10240]{1,0:T(8,128)(2,1)S(1)}, bf16[16,10240]{1,0:T(8,128)(2,1)S(1)}, u32[]{:S(2)}, u32[]{:S(2)}) collective-permute-start(bf16[16,10240]{1,0:T(8,128)(2,1)S(1)} %get-tuple-element.68), channel_id=1, source_target_pairs={{0,1},{1,2},{2,3},{3,4},{4,5},{5,6},{6,7},{7,0},{16,17},{17,18},{1... | collective-permute-start | bytes 983048 | tf_op jit(solution)/shard_map/ppermute | solution.py:46
  66.7 10.7 %collective-permute-start.16 = (bf16[16,10240]{1,0:T(8,128)(2,1)S(1)}, bf16[16,10240]{1,0:T(8,128)(2,1)S(1)}, u32[]{:S(2)}, u32[]{:S(2)}) collective-permute-start(bf16[16,10240]{1,0:T(8,128)(2,1)S(1)} %get-tuple-element.69), channel_id=1, source_target_pairs={{0,7},{1,0},{2,1},{3,2},{4,3},{5,4},{6,5},{7,6},{16,23},{17,16},{1... | collective-permute-start | bytes 983048 | tf_op jit(solution)/shard_map/ppermute | solution.py:46
  67.1 5.1 %collective-permute-start.17 = (f32[8,128]{1,0:T(8,128)S(1)}, f32[8,128]{1,0:T(8,128)S(1)}, u32[]{:S(2)}, u32[]{:S(2)}) collective-permute-start(f32[8,128]{1,0:T(8,128)S(1)} %get-tuple-element.70), channel_id=1, source_target_pairs={{0,128},{1,129},{2,130},{3,131},{4,132},{5,133},{6,134},{7,135},{1... | collective-permute-start | bytes 12296 | tf_op jit(solution)/shard_map/ppermute | solution.py:46
  70.3 4.9 %collective-permute-start.18 = (f32[8,128]{1,0:T(8,128)S(1)}, f32[8,128]{1,0:T(8,128)S(1)}, u32[]{:S(2)}, u32[]{:S(2)}) collective-permute-start(f32[8,128]{1,0:T(8,128)S(1)} %get-tuple-element.70), channel_id=1, source_target_pairs={{0,64},{1,65},{2,66},{3,67},{4,68},{5,69},{6,70},{7,71},{16,80},{1... | collective-permute-start | bytes 12296 | tf_op jit(solution)/shard_map/ppermute | solution.py:46
  72.2 4.8 %collective-permute-start.19 = (f32[8,128]{1,0:T(8,128)S(1)}, f32[8,128]{1,0:T(8,128)S(1)}, u32[]{:S(2)}, u32[]{:S(2)}) collective-permute-start(f32[8,128]{1,0:T(8,128)S(1)} %get-tuple-element.70), channel_id=1, source_target_pairs={{0,192},{1,193},{2,194},{3,195},{4,196},{5,197},{6,198},{7,199},{1... | collective-permute-start | bytes 12296 | tf_op jit(solution)/shard_map/ppermute | solution.py:46
  77.5 11.1 %collective-permute-start.21 = (bf16[16,4096]{1,0:T(8,128)(2,1)S(1)}, bf16[16,4096]{1,0:T(8,128)(2,1)S(1)}, u32[]{:S(2)}, u32[]{:S(2)}) collective-permute-start(bf16[16,4096]{1,0:T(8,128)(2,1)S(1)} %get-tuple-element.81), channel_id=1, source_target_pairs={{0,3},{1,4},{2,5},{3,6},{4,7},{5,0},{6,1},{7,2},{16,19},{17,20},{1... | collective-permute-start | bytes 393224 | tf_op jit(solution)/shard_map/ppermute | solution.py:46
  82.4 11.0 %collective-permute-start.22 = (bf16[16,4096]{1,0:T(8,128)(2,1)S(1)}, bf16[16,4096]{1,0:T(8,128)(2,1)S(1)}, u32[]{:S(2)}, u32[]{:S(2)}) collective-permute-start(bf16[16,4096]{1,0:T(8,128)(2,1)S(1)} %get-tuple-element.82), channel_id=1, source_target_pairs={{0,5},{1,6},{2,7},{3,0},{4,1},{5,2},{6,3},{7,4},{16,21},{17,22},{1... | collective-permute-start | bytes 393224 | tf_op jit(solution)/shard_map/ppermute | solution.py:46
  82.6 4.8 %collective-permute-start.23 = (f32[8,128]{1,0:T(8,128)S(1)}, f32[8,128]{1,0:T(8,128)S(1)}, u32[]{:S(2)}, u32[]{:S(2)}) collective-permute-start(f32[8,128]{1,0:T(8,128)S(1)} %add_add_fusion), channel_id=1, source_target_pairs={{0,40},{1,41},{2,42},{3,43},{4,44},{5,45},{6,46},{7,47},{16,24},{1... | collective-permute-start | bytes 12296 | tf_op jit(solution)/shard_map/ppermute | solution.py:46
  87.4 1.2 %collective-permute-start.24 = (f32[8,128]{1,0:T(8,128)S(1)}, f32[8,128]{1,0:T(8,128)S(1)}, u32[]{:S(2)}, u32[]{:S(2)}) collective-permute-start(f32[8,128]{1,0:T(8,128)S(1)} %add.77), channel_id=1, source_target_pairs={{0,16},{1,17},{2,18},{3,19},{4,20},{5,21},{6,22},{7,23},{16,0},{17... | collective-permute-start | bytes 12296 | tf_op jit(solution)/shard_map/ppermute | solution.py:46

commit v8 on v7

--- a/solution.py
+++ b/solution.py
@@ -452,12 +452,12 @@
     au, ad = both(pu, pd, 1)
     p0, p3, p5 = rest_call(coef, o, r_second, g)
     part = (part + send(part, Y2)) + (send(part, Y1) + send(part, Y3))
-    au, ad, part, p0, p3, p5 = together(au, ad, part, p0, p3, p5)
+    au, ad, p0, p3, p5 = together(au, ad, p0, p3, p5)
     zero = jnp.zeros((16, half), f32)
     near, next_, last = slice(0, depth), slice(depth, 2 * depth), slice(2 * depth, 2 * depth + half)
     p3 = p3 + ad[:, next_].astype(f32) + jnp.concatenate([au[:, last].astype(f32), zero], axis=1)
     p5 = p5 + au[:, next_].astype(f32) + jnp.concatenate([zero, ad[:, last].astype(f32)], axis=1)
-    p3, p5, part = together(p3.astype(bf16), p5.astype(bf16), part)
+    p3, p5 = together(p3.astype(bf16), p5.astype(bf16))
     a3, a5 = both(p3, p5, 3)
     for pairs in (CROSS, CORE):
         part = part + send(part, pairs)

time: 94.6 us -> 94.7 us (level)
  no operation moved by 1% of the time
where the time goes in v8:
time: 94.7 us; the launch traced here: 94.5 us
  starting transfers between devices  41.3 us (44%)
  waiting for transfers between devices  28.6 us (30%)
  Pallas kernels  20.8 us (22%)
  local copies, waits for them, and re-layouts  1.83 us (2%)
  between operations  1.69 us (2%)
    ppermute x25, starting transfers between devices, send(): return lax.ppermute(x, AXES, pairs)  41.3 us
    ppermute x25, waiting for transfers between devices, send(): return lax.ppermute(x, AXES, pairs)  28.6 us
    pallas_call x1, Pallas kernels, labels_call(): pl.pallas_call(labels_kernel, in_specs=[vmem(), hbm()], out_specs=[vmem()...  7.41 us
    pallas_call x1, Pallas kernels, logits_call(): pl.pallas_call(logits_kernel, in_specs=[smem(), smem()] + [vmem()] * (len...  5.48 us
    pallas_call x1, Pallas kernels, weighted_call(): pl.pallas_call(weighted_kernel, in_specs=[vmem()] * 3, out_specs=[vmem()]...  4.52 us
  transfers between devices with their start and end apart: 25, of which 12 were waited for; matrix products, arithmetic and copies ran while one was open for 2% of the time, Pallas kernels for 21%

profile of v8, /device:TPU:32, one launch (start us, length us, event | category | flops | bytes accessed | tf_op | source)
XLA Modules:
  0.0 94.5 jit_solution(10854492343486654546)
XLA Ops:
  0.6 5.9 %collective-permute-start = (bf16[16,4096]{1,0:T(8,128)(2,1)}, bf16[16,4096]{1,0:T(8,128)(2,1)S(1)}, u32[]{:S(2)}, u32[]{:S(2)}) collective-permute-start(bf16[16,4096]{1,0:T(8,128)(2,1)} %own_ref.1), channel_id=1, source_target_pairs={{0,3},{1,4},{2,5},{3,6},{4,7},{5,0},{6,1},{7,2},{16,19},{17,20},{1... | collective-permute-start | bytes 393224 | tf_op jit(solution)/shard_map/ppermute | solution.py:46
  6.6 0.1 collective-permute-start.1
  6.7 0.8 dynamic_slice.14
  7.4 0.1 dynamic-slice_bitcast_fusion.1
  7.5 0.9 stage.1.own_ref
  8.4 0.8 dynamic-slice_bitcast_fusion.cot_ref
  9.2 6.2 %collective-permute-done.up3_ref = bf16[16,4096]{1,0:T(8,128)(2,1)S(1)} collective-permute-done((bf16[16,4096]{1,0:T(8,128)(2,1)}, bf16[16,4096]{1,0:T(8,128)(2,1)S(1)}, u32[]{:S(2)}, u32[]{:S(2)}) %collective-permute-start) | collective-permute-done | bytes 131104 | tf_op jit(solution)/shard_map/ppermute | solution.py:46
  15.4 3.2 %collective-permute-done.1.down3_ref = bf16[16,4096]{1,0:T(8,128)(2,1)S(1)} collective-permute-done((bf16[16,4096]{1,0:T(8,128)(2,1)}, bf16[16,4096]{1,0:T(8,128)(2,1)S(1)}, u32[]{:S(2)}, u32[]{:S(2)}) %collective-permute-start.1) | collective-permute-done | bytes 131104 | tf_op jit(solution)/shard_map/ppermute | solution.py:46
  18.6 0.1 pack.1
  18.7 0.1 collective-permute-start.2
  18.8 2.0 %collective-permute-start.3 = (bf16[16,10240]{1,0:T(8,128)(2,1)S(1)}, bf16[16,10240]{1,0:T(8,128)(2,1)S(1)}, u32[]{:S(2)}, u32[]{:S(2)}) collective-permute-start(bf16[16,10240]{1,0:T(8,128)(2,1)S(1)} %get-tuple-element.44), channel_id=1, source_target_pairs={{0,7},{1,0},{2,1},{3,2},{4,3},{5,4},{6,5},{7,6},{16,23},{17,16},{1... | collective-permute-start | bytes 983048 | tf_op jit(solution)/shard_map/ppermute | solution.py:46
  20.8 1.5 %collective-permute-start.5 = (bf16[16,8192]{1,0:T(8,128)(2,1)S(1)}, bf16[16,8192]{1,0:T(8,128)(2,1)S(1)}, u32[]{:S(2)}, u32[]{:S(2)}) collective-permute-start(bf16[16,8192]{1,0:T(8,128)(2,1)S(1)} %get-tuple-element.46.two), channel_id=1, source_target_pairs={{0,8},{1,9},{2,10},{3,11},{4,12},{5,13},{6,14},{7,15},{16,56},{17,... | collective-permute-start | bytes 786440 | tf_op jit(solution)/shard_map/ppermute | solution.py:46
  22.3 0.5 collective-permute-start.4
  23.5 5.1 %collective-permute-done.4.own_x = bf16[16,4224]{1,0:T(8,128)(2,1)S(1)} collective-permute-done((bf16[16,4224]{1,0:T(8,128)(2,1)S(1)}, bf16[16,4224]{1,0:T(8,128)(2,1)S(1)}, u32[]{:S(2)}, u32[]{:S(2)}) %collective-permute-start.4) | collective-permute-done | bytes 135200 | tf_op jit(solution)/shard_map/ppermute | solution.py:46
  28.6 0.0 collective-permute-done.5.two_x
  28.6 0.0 collective-permute-done.2.up
  28.6 0.2 collective-permute-done.3.down
  28.9 1.6 %collective-permute-start.6 = (bf16[16,10240]{1,0:T(8,128)(2,1)S(1)}, bf16[16,10240]{1,0:T(8,128)(2,1)S(1)}, u32[]{:S(2)}, u32[]{:S(2)}) collective-permute-start(bf16[16,10240]{1,0:T(8,128)(2,1)S(1)} %collective-permute-done.2.up), channel_id=1, source_target_pairs={{0,8},{1,9},{2,10},{3,11},{4,12},{5,13},{6,14},{7,15},{16,56},{17,... | collective-permute-start | bytes 983048 | tf_op jit(solution)/shard_map/ppermute | solution.py:46
  30.4 0.5 collective-permute-start.7
  31.0 0.1 copy.11
  31.1 7.4 %label_rows.1 = (bf16[2048,4096]{1,0:T(8,128)(2,1)S(1)}, bf16[128,4096]{1,0:T(8,128)(2,1)S(1)}, bf16[80,4096]{1,0:T(8,128)(2,1)S(1)}, bf16[48,4096]{1,0:T(8,128)(2,1)S(1)}) custom-call(s32[256,1]{1,0:T(8,128)S(1)} %broadcast_subtract_fusion.lab_ref, bf16[2048,4096]{1,0:T(8,128)(2,1)} %mem_ref.1), custom_call_target="tpu_custom_call" | custom-call | flops 1024 | bytes 1024 | tf_op jit(solution)/shard_map/label_rows/pallas_call | solution.py:262
  38.6 1.8 %collective-permute-start.9 = (bf16[80,4096]{1,0:T(8,128)(2,1)S(1)}, bf16[80,4096]{1,0:T(8,128)(2,1)S(1)}, u32[]{:S(2)}, u32[]{:S(2)}) collective-permute-start(bf16[80,4096]{1,0:T(8,128)(2,1)S(1)} %get-tuple-element.57), channel_id=1, source_target_pairs={{0,8},{1,9},{2,10},{3,11},{4,12},{5,13},{6,14},{7,15},{16,56},{17,... | collective-permute-start | bytes 1966088 | tf_op jit(solution)/shard_map/ppermute | solution.py:46
  40.3 0.0 collective-permute-done.6.up_x
  40.3 0.0 collective-permute-done.7.down_x
  40.3 5.5 %logits.1 = (bf16[256,2048]{1,0:T(8,128)(2,1)S(1)}, f32[8,128]{1,0:T(8,128)S(1)}) custom-call(f32[1]{0:T(128)} %exp.3.scale_ref, s32[1]{0:T(128)} %bitcast.6.shift_ref, bf16[16,4224]{1,0:T(8,128)(2,1)S(1)} %get-tuple-element.45.own, bf16[16,8192]{1,0:T(8,128)(2,1)S(1)} %get-tuple-element.46.two, bf16[16,10240]{1,0:T(8,128)(2,1)S(1)} %collective-permute-done.2.up, ...), custom_call_target="tpu_custom_call" | custom-call | flops 4294967296 | bytes 16777216 | tf_op jit(solution)/shard_map/logits/pallas_call | solution.py:178
  45.8 0.7 collective-permute-start.8
  46.5 4.5 %weighted.1 = (f32[128,4096]{1,0:T(8,128)S(1)}, bf16[80,4096]{1,0:T(8,128)(2,1)S(1)}, bf16[96,4096]{1,0:T(8,128)(2,1)S(1)}) custom-call(bf16[256,2048]{1,0:T(8,128)(2,1)S(1)} %get-tuple-element.53.e_ref, bf16[2048,4096]{1,0:T(8,128)(2,1)S(1)} %get-tuple-element.51.mem_ref, bf16[48,4096]{1,0:T(8,128)(2,1)S(1)} %get-tuple-element.54.g_ref), custom_call_target="tpu_custom_call" | custom-call | flops 4294967296 | bytes 16777216 | tf_op jit(solution)/shard_map/weighted/pallas_call | solution.py:220
  51.0 0.0 copy-start.1
  51.1 0.0 collective-permute-done.8
  51.1 1.8 %collective-permute-start.10 = (f32[2,8,128]{2,1,0:T(8,128)S(1)}, f32[2,8,128]{2,1,0:T(8,128)S(1)}, u32[]{:S(2)}, u32[]{:S(2)}) collective-permute-start(f32[2,8,128]{2,1,0:T(8,128)S(1)} %get-tuple-element.81), channel_id=1, source_target_pairs={{0,1},{1,2},{2,3},{3,4},{4,5},{5,6},{6,7},{7,0},{16,17},{17,18},{1... | collective-permute-start | bytes 24584 | tf_op jit(solution)/shard_map/ppermute | solution.py:46
  52.9 0.1 pad_add_fusion.2.place_ref
  53.0 0.3 collective-permute-start.11
  53.3 1.3 %collective-permute-start.14 = (bf16[80,4096]{1,0:T(8,128)(2,1)S(1)}, bf16[80,4096]{1,0:T(8,128)(2,1)S(1)}, u32[]{:S(2)}, u32[]{:S(2)}) collective-permute-start(bf16[80,4096]{1,0:T(8,128)(2,1)S(1)} %get-tuple-element.63), channel_id=1, source_target_pairs={{0,8},{1,9},{2,10},{3,11},{4,12},{5,13},{6,14},{7,15},{16,56},{17,... | collective-permute-start | bytes 1966088 | tf_op jit(solution)/shard_map/ppermute | solution.py:46
  54.6 0.2 collective-permute-done.10
  54.8 1.9 %collective-permute-start.13 = (f32[2,2,8,128]{3,2,1,0:T(8,128)S(1)}, f32[2,2,8,128]{3,2,1,0:T(8,128)S(1)}, u32[]{:S(2)}, u32[]{:S(2)}) collective-permute-start(f32[2,2,8,128]{3,2,1,0:T(8,128)S(1)} %pad_maximum_fusion.1), channel_id=1, source_target_pairs={{0,5},{1,6},{2,7},{3,0},{4,1},{5,2},{6,3},{7,4},{16,21},{17,22},{1... | collective-permute-start | bytes 49160 | tf_op jit(solution)/shard_map/ppermute | solution.py:46
  56.8 0.0 collective-permute-done.11
  56.8 3.1 %collective-permute-start.12 = (f32[3,2,8,128]{3,2,1,0:T(8,128)S(1)}, f32[3,2,8,128]{3,2,1,0:T(8,128)S(1)}, u32[]{:S(2)}, u32[]{:S(2)}) collective-permute-start(f32[3,2,8,128]{3,2,1,0:T(8,128)S(1)} %pad_maximum_fusion.mid_ref), channel_id=1, source_target_pairs={{0,3},{1,4},{2,5},{3,6},{4,7},{5,0},{6,1},{7,2},{16,19},{17,20},{1... | collective-permute-start | bytes 73736 | tf_op jit(solution)/shard_map/ppermute | solution.py:46
  59.9 1.3 %collective-permute-start.17 = (bf16[96,4096]{1,0:T(8,128)(2,1)S(1)}, bf16[96,4096]{1,0:T(8,128)(2,1)S(1)}, u32[]{:S(2)}, u32[]{:S(2)}) collective-permute-start(bf16[96,4096]{1,0:T(8,128)(2,1)S(1)} %get-tuple-element.68), channel_id=1, source_target_pairs={{0,8},{1,9},{2,10},{3,11},{4,12},{5,13},{6,14},{7,15},{16,56},{17,... | collective-permute-start | bytes 2359304 | tf_op jit(solution)/shard_map/ppermute | solution.py:46
  61.2 0.4 collective-permute-done.13.down_ref
  61.6 2.1 %collective-permute-done.12.up_ref = f32[3,2,8,128]{3,2,1,0:T(8,128)S(1)} collective-permute-done((f32[3,2,8,128]{3,2,1,0:T(8,128)S(1)}, f32[3,2,8,128]{3,2,1,0:T(8,128)S(1)}, u32[]{:S(2)}, u32[]{:S(2)}) %collective-permute-start.12) | collective-permute-done | bytes 24608 | tf_op jit(solution)/shard_map/ppermute | solution.py:46
  63.7 0.8 merge.1
  64.5 0.0 collective-permute-done.14.r_ref
  64.5 0.5 mix.1
  65.0 1.7 %collective-permute-start.15 = (bf16[16,10240]{1,0:T(8,128)(2,1)S(1)}, bf16[16,10240]{1,0:T(8,128)(2,1)S(1)}, u32[]{:S(2)}, u32[]{:S(2)}) collective-permute-start(bf16[16,10240]{1,0:T(8,128)(2,1)S(1)} %get-tuple-element.66), channel_id=1, source_target_pairs={{0,1},{1,2},{2,3},{3,4},{4,5},{5,6},{6,7},{7,0},{16,17},{17,18},{1... | collective-permute-start | bytes 983048 | tf_op jit(solution)/shard_map/ppermute | solution.py:46
  66.7 0.4 collective-permute-start.16
  67.1 3.2 %collective-permute-start.20 = (f32[8,128]{1,0:T(8,128)S(1)}, f32[8,128]{1,0:T(8,128)S(1)}, u32[]{:S(2)}, u32[]{:S(2)}) collective-permute-start(f32[8,128]{1,0:T(8,128)S(1)} %get-tuple-element.79), channel_id=1, source_target_pairs={{0,128},{1,129},{2,130},{3,131},{4,132},{5,133},{6,134},{7,135},{1... | collective-permute-start | bytes 12296 | tf_op jit(solution)/shard_map/ppermute | solution.py:46
  70.3 0.7 collective-permute-start.21
  71.0 1.3 %collective-permute-done.17.r_ref = bf16[96,4096]{1,0:T(8,128)(2,1)S(1)} collective-permute-done((bf16[96,4096]{1,0:T(8,128)(2,1)S(1)}, bf16[96,4096]{1,0:T(8,128)(2,1)S(1)}, u32[]{:S(2)}, u32[]{:S(2)}) %collective-permute-start.17) | collective-permute-done | bytes 786464 | tf_op jit(solution)/shard_map/ppermute | solution.py:46
  72.3 3.0 %collective-permute-start.22 = (f32[8,128]{1,0:T(8,128)S(1)}, f32[8,128]{1,0:T(8,128)S(1)}, u32[]{:S(2)}, u32[]{:S(2)}) collective-permute-start(f32[8,128]{1,0:T(8,128)S(1)} %get-tuple-element.79), channel_id=1, source_target_pairs={{0,192},{1,193},{2,194},{3,195},{4,196},{5,197},{6,198},{7,199},{1... | collective-permute-start | bytes 12296 | tf_op jit(solution)/shard_map/ppermute | solution.py:46
  75.3 0.3 rest.1
  75.6 0.0 collective-permute-done.15.au_ref
  75.7 0.1 add_convert_fusion
  75.8 4.3 %collective-permute-start.18 = (bf16[16,4096]{1,0:T(8,128)(2,1)S(1)}, bf16[16,4096]{1,0:T(8,128)(2,1)S(1)}, u32[]{:S(2)}, u32[]{:S(2)}) collective-permute-start(bf16[16,4096]{1,0:T(8,128)(2,1)S(1)} %get-tuple-element.77), channel_id=1, source_target_pairs={{0,3},{1,4},{2,5},{3,6},{4,7},{5,0},{6,1},{7,2},{16,19},{17,20},{1... | collective-permute-start | bytes 393224 | tf_op jit(solution)/shard_map/ppermute | solution.py:46
  80.1 0.8 collective-permute-start.19
  80.9 0.0 collective-permute-done.21
  80.9 0.0 collective-permute-done.22
  80.9 2.7 %collective-permute-start.23 = (f32[8,128]{1,0:T(8,128)S(1)}, f32[8,128]{1,0:T(8,128)S(1)}, u32[]{:S(2)}, u32[]{:S(2)}) collective-permute-start(f32[8,128]{1,0:T(8,128)S(1)} %add_add_fusion), channel_id=1, source_target_pairs={{0,40},{1,41},{2,42},{3,43},{4,44},{5,45},{6,46},{7,47},{16,24},{1... | collective-permute-start | bytes 12296 | tf_op jit(solution)/shard_map/ppermute | solution.py:46
  83.6 2.2 %collective-permute-done.23 = f32[8,128]{1,0:T(8,128)S(1)} collective-permute-done((f32[8,128]{1,0:T(8,128)S(1)}, f32[8,128]{1,0:T(8,128)S(1)}, u32[]{:S(2)}, u32[]{:S(2)}) %collective-permute-start.23) | collective-permute-done | bytes 4128 | tf_op jit(solution)/shard_map/ppermute | solution.py:46
  85.8 0.1 multiply_bitcast_fusion
  85.9 0.1 copy.12.factor_ref
  86.0 1.0 %collective-permute-done.24 = f32[8,128]{1,0:T(8,128)S(1)} collective-permute-done((f32[8,128]{1,0:T(8,128)S(1)}, f32[8,128]{1,0:T(8,128)S(1)}, u32[]{:S(2)}, u32[]{:S(2)}) %collective-permute-start.24) | collective-permute-done | bytes 4128 | tf_op jit(solution)/shard_map/ppermute | solution.py:46
  87.0 0.9 collective-permute-done.18.a3_ref
  87.9 5.7 %collective-permute-done.19.a5_ref = bf16[16,4096]{1,0:T(8,128)(2,1)S(1)} collective-permute-done((bf16[16,4096]{1,0:T(8,128)(2,1)S(1)}, bf16[16,4096]{1,0:T(8,128)(2,1)S(1)}, u32[]{:S(2)}, u32[]{:S(2)}) %collective-permute-start.19) | collective-permute-done | bytes 131104 | tf_op jit(solution)/shard_map/ppermute | solution.py:46
  93.6 0.8 final.1
  (21 shorter events, 0.1 us)
Async XLA Ops:
  0.6 39.7 %copy-start = (s32[2048]{0:T(1024)S(1)}, s32[2048]{0:T(1024)}, u32[]{:S(2)}) copy-start(s32[2048]{0:T(1024)} %param.10) | copy-start | bytes 24580
  0.6 14.8 %collective-permute-start = (bf16[16,4096]{1,0:T(8,128)(2,1)}, bf16[16,4096]{1,0:T(8,128)(2,1)S(1)}, u32[]{:S(2)}, u32[]{:S(2)}) collective-permute-start(bf16[16,4096]{1,0:T(8,128)(2,1)} %own_ref.1), channel_id=1, source_target_pairs={{0,3},{1,4},{2,5},{3,6},{4,7},{5,0},{6,1},{7,2},{16,19},{17,20},{1... | collective-permute-start | bytes 393224 | tf_op jit(solution)/shard_map/ppermute | solution.py:46
  6.6 12.1 %collective-permute-start.1 = (bf16[16,4096]{1,0:T(8,128)(2,1)}, bf16[16,4096]{1,0:T(8,128)(2,1)S(1)}, u32[]{:S(2)}, u32[]{:S(2)}) collective-permute-start(bf16[16,4096]{1,0:T(8,128)(2,1)} %own_ref.1), channel_id=1, source_target_pairs={{0,5},{1,6},{2,7},{3,0},{4,1},{5,2},{6,3},{7,4},{16,21},{17,22},{1... | collective-permute-start | bytes 393224 | tf_op jit(solution)/shard_map/ppermute | solution.py:46
  18.7 9.9 %collective-permute-start.2 = (bf16[16,10240]{1,0:T(8,128)(2,1)S(1)}, bf16[16,10240]{1,0:T(8,128)(2,1)S(1)}, u32[]{:S(2)}, u32[]{:S(2)}) collective-permute-start(bf16[16,10240]{1,0:T(8,128)(2,1)S(1)} %get-tuple-element.43), channel_id=1, source_target_pairs={{0,1},{1,2},{2,3},{3,4},{4,5},{5,6},{6,7},{7,0},{16,17},{17,18},{1... | collective-permute-start | bytes 983048 | tf_op jit(solution)/shard_map/ppermute | solution.py:46
  18.8 10.0 %collective-permute-start.3 = (bf16[16,10240]{1,0:T(8,128)(2,1)S(1)}, bf16[16,10240]{1,0:T(8,128)(2,1)S(1)}, u32[]{:S(2)}, u32[]{:S(2)}) collective-permute-start(bf16[16,10240]{1,0:T(8,128)(2,1)S(1)} %get-tuple-element.44), channel_id=1, source_target_pairs={{0,7},{1,0},{2,1},{3,2},{4,3},{5,4},{6,5},{7,6},{16,23},{17,16},{1... | collective-permute-start | bytes 983048 | tf_op jit(solution)/shard_map/ppermute | solution.py:46
  20.8 7.8 %collective-permute-start.5 = (bf16[16,8192]{1,0:T(8,128)(2,1)S(1)}, bf16[16,8192]{1,0:T(8,128)(2,1)S(1)}, u32[]{:S(2)}, u32[]{:S(2)}) collective-permute-start(bf16[16,8192]{1,0:T(8,128)(2,1)S(1)} %get-tuple-element.46.two), channel_id=1, source_target_pairs={{0,8},{1,9},{2,10},{3,11},{4,12},{5,13},{6,14},{7,15},{16,56},{17,... | collective-permute-start | bytes 786440 | tf_op jit(solution)/shard_map/ppermute | solution.py:46
  22.3 6.3 %collective-permute-start.4 = (bf16[16,4224]{1,0:T(8,128)(2,1)S(1)}, bf16[16,4224]{1,0:T(8,128)(2,1)S(1)}, u32[]{:S(2)}, u32[]{:S(2)}) collective-permute-start(bf16[16,4224]{1,0:T(8,128)(2,1)S(1)} %get-tuple-element.45.own), channel_id=1, source_target_pairs={{0,8},{1,9},{2,10},{3,11},{4,12},{5,13},{6,14},{7,15},{16,56},{17,... | collective-permute-start | bytes 405512 | tf_op jit(solution)/shard_map/ppermute | solution.py:46
  28.9 11.5 %collective-permute-start.6 = (bf16[16,10240]{1,0:T(8,128)(2,1)S(1)}, bf16[16,10240]{1,0:T(8,128)(2,1)S(1)}, u32[]{:S(2)}, u32[]{:S(2)}) collective-permute-start(bf16[16,10240]{1,0:T(8,128)(2,1)S(1)} %collective-permute-done.2.up), channel_id=1, source_target_pairs={{0,8},{1,9},{2,10},{3,11},{4,12},{5,13},{6,14},{7,15},{16,56},{17,... | collective-permute-start | bytes 983048 | tf_op jit(solution)/shard_map/ppermute | solution.py:46
  30.4 9.9 %collective-permute-start.7 = (bf16[16,10240]{1,0:T(8,128)(2,1)S(1)}, bf16[16,10240]{1,0:T(8,128)(2,1)S(1)}, u32[]{:S(2)}, u32[]{:S(2)}) collective-permute-start(bf16[16,10240]{1,0:T(8,128)(2,1)S(1)} %collective-permute-done.3.down), channel_id=1, source_target_pairs={{0,8},{1,9},{2,10},{3,11},{4,12},{5,13},{6,14},{7,15},{16,56},{17,... | collective-permute-start | bytes 983048 | tf_op jit(solution)/shard_map/ppermute | solution.py:46
  38.6 12.5 %collective-permute-start.9 = (bf16[80,4096]{1,0:T(8,128)(2,1)S(1)}, bf16[80,4096]{1,0:T(8,128)(2,1)S(1)}, u32[]{:S(2)}, u32[]{:S(2)}) collective-permute-start(bf16[80,4096]{1,0:T(8,128)(2,1)S(1)} %get-tuple-element.57), channel_id=1, source_target_pairs={{0,8},{1,9},{2,10},{3,11},{4,12},{5,13},{6,14},{7,15},{16,56},{17,... | collective-permute-start | bytes 1966088 | tf_op jit(solution)/shard_map/ppermute | solution.py:46
  45.8 5.2 %collective-permute-start.8 = (f32[8,128]{1,0:T(8,128)S(1)}, f32[8,128]{1,0:T(8,128)S(1)}, u32[]{:S(2)}, u32[]{:S(2)}) collective-permute-start(f32[8,128]{1,0:T(8,128)S(1)} %get-tuple-element.52), channel_id=1, source_target_pairs={{0,8},{1,9},{2,10},{3,11},{4,12},{5,13},{6,14},{7,15},{16,56},{17,... | collective-permute-start | bytes 12296 | tf_op jit(solution)/shard_map/ppermute | solution.py:46
  51.0 34.8 %copy-start.1 = (f32[256]{0:T(256)S(1)}, f32[256]{0:T(256)}, u32[]{:S(2)}) copy-start(f32[256]{0:T(256)} %param.11) | copy-start | bytes 3076
  51.1 3.7 %collective-permute-start.10 = (f32[2,8,128]{2,1,0:T(8,128)S(1)}, f32[2,8,128]{2,1,0:T(8,128)S(1)}, u32[]{:S(2)}, u32[]{:S(2)}) collective-permute-start(f32[2,8,128]{2,1,0:T(8,128)S(1)} %get-tuple-element.81), channel_id=1, source_target_pairs={{0,1},{1,2},{2,3},{3,4},{4,5},{5,6},{6,7},{7,0},{16,17},{17,18},{1... | collective-permute-start | bytes 24584 | tf_op jit(solution)/shard_map/ppermute | solution.py:46
  53.0 3.8 %collective-permute-start.11 = (f32[2,8,128]{2,1,0:T(8,128)S(1)}, f32[2,8,128]{2,1,0:T(8,128)S(1)}, u32[]{:S(2)}, u32[]{:S(2)}) collective-permute-start(f32[2,8,128]{2,1,0:T(8,128)S(1)} %get-tuple-element.81), channel_id=1, source_target_pairs={{0,7},{1,0},{2,1},{3,2},{4,3},{5,4},{6,5},{7,6},{16,23},{17,16},{1... | collective-permute-start | bytes 24584 | tf_op jit(solution)/shard_map/ppermute | solution.py:46
  53.3 11.2 %collective-permute-start.14 = (bf16[80,4096]{1,0:T(8,128)(2,1)S(1)}, bf16[80,4096]{1,0:T(8,128)(2,1)S(1)}, u32[]{:S(2)}, u32[]{:S(2)}) collective-permute-start(bf16[80,4096]{1,0:T(8,128)(2,1)S(1)} %get-tuple-element.63), channel_id=1, source_target_pairs={{0,8},{1,9},{2,10},{3,11},{4,12},{5,13},{6,14},{7,15},{16,56},{17,... | collective-permute-start | bytes 1966088 | tf_op jit(solution)/shard_map/ppermute | solution.py:46
  54.8 6.7 %collective-permute-start.13 = (f32[2,2,8,128]{3,2,1,0:T(8,128)S(1)}, f32[2,2,8,128]{3,2,1,0:T(8,128)S(1)}, u32[]{:S(2)}, u32[]{:S(2)}) collective-permute-start(f32[2,2,8,128]{3,2,1,0:T(8,128)S(1)} %pad_maximum_fusion.1), channel_id=1, source_target_pairs={{0,5},{1,6},{2,7},{3,0},{4,1},{5,2},{6,3},{7,4},{16,21},{17,22},{1... | collective-permute-start | bytes 49160 | tf_op jit(solution)/shard_map/ppermute | solution.py:46
  56.8 6.9 %collective-permute-start.12 = (f32[3,2,8,128]{3,2,1,0:T(8,128)S(1)}, f32[3,2,8,128]{3,2,1,0:T(8,128)S(1)}, u32[]{:S(2)}, u32[]{:S(2)}) collective-permute-start(f32[3,2,8,128]{3,2,1,0:T(8,128)S(1)} %pad_maximum_fusion.mid_ref), channel_id=1, source_target_pairs={{0,3},{1,4},{2,5},{3,6},{4,7},{5,0},{6,1},{7,2},{16,19},{17,20},{1... | collective-permute-start | bytes 73736 | tf_op jit(solution)/shard_map/ppermute | solution.py:46
  59.9 12.4 %collective-permute-start.17 = (bf16[96,4096]{1,0:T(8,128)(2,1)S(1)}, bf16[96,4096]{1,0:T(8,128)(2,1)S(1)}, u32[]{:S(2)}, u32[]{:S(2)}) collective-permute-start(bf16[96,4096]{1,0:T(8,128)(2,1)S(1)} %get-tuple-element.68), channel_id=1, source_target_pairs={{0,8},{1,9},{2,10},{3,11},{4,12},{5,13},{6,14},{7,15},{16,56},{17,... | collective-permute-start | bytes 2359304 | tf_op jit(solution)/shard_map/ppermute | solution.py:46
  65.0 10.6 %collective-permute-start.15 = (bf16[16,10240]{1,0:T(8,128)(2,1)S(1)}, bf16[16,10240]{1,0:T(8,128)(2,1)S(1)}, u32[]{:S(2)}, u32[]{:S(2)}) collective-permute-start(bf16[16,10240]{1,0:T(8,128)(2,1)S(1)} %get-tuple-element.66), channel_id=1, source_target_pairs={{0,1},{1,2},{2,3},{3,4},{4,5},{5,6},{6,7},{7,0},{16,17},{17,18},{1... | collective-permute-start | bytes 983048 | tf_op jit(solution)/shard_map/ppermute | solution.py:46
  66.7 8.9 %collective-permute-start.16 = (bf16[16,10240]{1,0:T(8,128)(2,1)S(1)}, bf16[16,10240]{1,0:T(8,128)(2,1)S(1)}, u32[]{:S(2)}, u32[]{:S(2)}) collective-permute-start(bf16[16,10240]{1,0:T(8,128)(2,1)S(1)} %get-tuple-element.67), channel_id=1, source_target_pairs={{0,7},{1,0},{2,1},{3,2},{4,3},{5,4},{6,5},{7,6},{16,23},{17,16},{1... | collective-permute-start | bytes 983048 | tf_op jit(solution)/shard_map/ppermute | solution.py:46
  67.1 13.8 %collective-permute-start.20 = (f32[8,128]{1,0:T(8,128)S(1)}, f32[8,128]{1,0:T(8,128)S(1)}, u32[]{:S(2)}, u32[]{:S(2)}) collective-permute-start(f32[8,128]{1,0:T(8,128)S(1)} %get-tuple-element.79), channel_id=1, source_target_pairs={{0,128},{1,129},{2,130},{3,131},{4,132},{5,133},{6,134},{7,135},{1... | collective-permute-start | bytes 12296 | tf_op jit(solution)/shard_map/ppermute | solution.py:46
  70.3 10.6 %collective-permute-start.21 = (f32[8,128]{1,0:T(8,128)S(1)}, f32[8,128]{1,0:T(8,128)S(1)}, u32[]{:S(2)}, u32[]{:S(2)}) collective-permute-start(f32[8,128]{1,0:T(8,128)S(1)} %get-tuple-element.79), channel_id=1, source_target_pairs={{0,64},{1,65},{2,66},{3,67},{4,68},{5,69},{6,70},{7,71},{16,80},{1... | collective-permute-start | bytes 12296 | tf_op jit(solution)/shard_map/ppermute | solution.py:46
  72.3 8.6 %collective-permute-start.22 = (f32[8,128]{1,0:T(8,128)S(1)}, f32[8,128]{1,0:T(8,128)S(1)}, u32[]{:S(2)}, u32[]{:S(2)}) collective-permute-start(f32[8,128]{1,0:T(8,128)S(1)} %get-tuple-element.79), channel_id=1, source_target_pairs={{0,192},{1,193},{2,194},{3,195},{4,196},{5,197},{6,198},{7,199},{1... | collective-permute-start | bytes 12296 | tf_op jit(solution)/shard_map/ppermute | solution.py:46
  75.8 12.1 %collective-permute-start.18 = (bf16[16,4096]{1,0:T(8,128)(2,1)S(1)}, bf16[16,4096]{1,0:T(8,128)(2,1)S(1)}, u32[]{:S(2)}, u32[]{:S(2)}) collective-permute-start(bf16[16,4096]{1,0:T(8,128)(2,1)S(1)} %get-tuple-element.77), channel_id=1, source_target_pairs={{0,3},{1,4},{2,5},{3,6},{4,7},{5,0},{6,1},{7,2},{16,19},{17,20},{1... | collective-permute-start | bytes 393224 | tf_op jit(solution)/shard_map/ppermute | solution.py:46
  80.1 13.5 %collective-permute-start.19 = (bf16[16,4096]{1,0:T(8,128)(2,1)S(1)}, bf16[16,4096]{1,0:T(8,128)(2,1)S(1)}, u32[]{:S(2)}, u32[]{:S(2)}) collective-permute-start(bf16[16,4096]{1,0:T(8,128)(2,1)S(1)} %get-tuple-element.78), channel_id=1, source_target_pairs={{0,5},{1,6},{2,7},{3,0},{4,1},{5,2},{6,3},{7,4},{16,21},{17,22},{1... | collective-permute-start | bytes 393224 | tf_op jit(solution)/shard_map/ppermute | solution.py:46
  80.9 4.9 %collective-permute-start.23 = (f32[8,128]{1,0:T(8,128)S(1)}, f32[8,128]{1,0:T(8,128)S(1)}, u32[]{:S(2)}, u32[]{:S(2)}) collective-permute-start(f32[8,128]{1,0:T(8,128)S(1)} %add_add_fusion), channel_id=1, source_target_pairs={{0,40},{1,41},{2,42},{3,43},{4,44},{5,45},{6,46},{7,47},{16,24},{1... | collective-permute-start | bytes 12296 | tf_op jit(solution)/shard_map/ppermute | solution.py:46
  85.8 1.2 %collective-permute-start.24 = (f32[8,128]{1,0:T(8,128)S(1)}, f32[8,128]{1,0:T(8,128)S(1)}, u32[]{:S(2)}, u32[]{:S(2)}) collective-permute-start(f32[8,128]{1,0:T(8,128)S(1)} %add.77), channel_id=1, source_target_pairs={{0,16},{1,17},{2,18},{3,19},{4,20},{5,21},{6,22},{7,23},{16,0},{17... | collective-permute-start | bytes 12296 | tf_op jit(solution)/shard_map/ppermute | solution.py:46
